TPU v7x, 32 devices: a whole 2x2x4 slice. The times are simulated.
32 devices in a mesh: fsdp: 4 (over y, x), ctx: 2 (over core), tp: 4 (over z).
Axes of the slice: x: 2, y: 2, z: 4, core: 2. Of those that a mesh axis runs over, the one named last changes fastest.
Arguments:
- inputs: bfloat16 [4, 1536, 768], P('fsdp', 'ctx'), may hold values from -6 to 6
- cotangent: bfloat16 [4, 1536, 768], P('fsdp', 'ctx'), may hold values from -6 to 6
- segments: int32 [4, 1536], P('fsdp', 'ctx'), may hold values from 0 to 15, never falling along the last dimension, each value on 1 to 768 neighbouring positions
- gains: float32 [3, 768], replicated, may hold values from 0.5 to 1.5
- last_gain: float32 [768], replicated, may hold values from 0.5 to 1.5
- in_weight: bfloat16 [2, 3, 768, 768], P(None, None, 'fsdp', 'tp'), may hold values from -0.21875 to 0.21875
- h3_out: bfloat16 [768, 768], P('tp', 'fsdp'), may hold values from -0.0546875 to 0.0546875
- attn_out: bfloat16 [768, 768], P('tp', 'fsdp'), may hold values from -0.875 to 0.875
- up_weight: bfloat16 [2, 768, 3072], P(None, 'fsdp', 'tp'), may hold values from -0.21875 to 0.21875
- down_weight: bfloat16 [2, 3072, 768], P(None, 'tp', 'fsdp'), may hold values from -0.109375 to 0.109375
- shift_taps: float32 [64, 768], P(None, 'tp'), may hold values from -1.5 to 1.5
- decay_rate: float32 [12, 64], P('tp'), may hold values from 3.2552085e-05 to 0.1
Outputs:
- output: bfloat16 [4, 1536, 768], P('fsdp', 'ctx')
- input_grad: float32 [4, 1536, 768], P('fsdp', 'ctx')
- gains_grad: float32 [3, 768], P(None, 'fsdp')
- last_gain_grad: float32 [768], P('fsdp')
- in_grad: float32 [2, 3, 768, 768], P(None, None, 'fsdp', 'tp')
- h3_out_grad: float32 [768, 768], P('tp', 'fsdp')
- attn_out_grad: float32 [768, 768], P('tp', 'fsdp')
- up_grad: float32 [2, 768, 3072], P(None, 'fsdp', 'tp')
- down_grad: float32 [2, 3072, 768], P(None, 'tp', 'fsdp')
- taps_grad: float32 [64, 768], P('fsdp', 'tp')
- rate_grad: float32 [12, 64], P('tp', 'fsdp')
Inputs may be any that keep to these rules, and one draw needn't show every extreme that they name: `segments`: within a sequence the ids never fall along the positions, start at 0 and take every value up to 15; no document has more than 768 positions, and one has exactly that many.
All inputs are finite; a program needn't handle non-finite values.
Results may differ from a plain program's by a relative error of at most 0.03.
Values may be sent and summed in bfloat16 or wider, within the bound.
No kernel may reach another device: no remote copies, remote signals or barrier semaphores. Data moves between devices by JAX's collectives and lax.ppermute only.
A program may use at most 192 MiB of HBM per device.

v0:
```python
import jax
import jax.numpy as jnp
from jax import lax
from jax.sharding import PartitionSpec as P

HEAD_DIM = 64


highest_score = lax.Precision.HIGHEST
epsilon = 1e-05
masked_low = -1e30


def passed_along(value, axis, steps):
    count = lax.axis_size(axis)
    first, last = (max(0, -steps), min(count, count - steps))
    return lax.ppermute(value, axis, [(source, source + steps) for source in range(first, last)])


def carried_in(shard, axis, join, neutral):
    place = lax.axis_index(axis)
    gathered = jax.tree.map(
        lambda a, kind: lax.all_gather(a.astype(kind), axis), shard, (jnp.bfloat16, jnp.bfloat16)
    )
    state = jax.tree.map(lambda a, e: jnp.zeros_like(a) + jnp.asarray(e, a.dtype), shard, neutral)

    def one(hop, state):
        return join(
            state,
            jax.tree.map(
                lambda a, own: lax.dynamic_index_in_dim(a, hop, 0, False).astype(own.dtype),
                gathered,
                shard,
            ),
        )

    return lax.fori_loop(0, place, one, state)


def entering(shard, axis, combine, identity):
    size, position = (lax.axis_size(axis), lax.axis_index(axis))
    everything = jax.tree.map(
        lambda part, kind: lax.all_gather(part.astype(kind), axis),
        shard,
        jax.tree.map(lambda a: jnp.bfloat16 if a.dtype == jnp.float32 else a.dtype, shard),
    )
    start = jax.tree.map(
        lambda part, zero: jnp.broadcast_to(jnp.asarray(zero, part.dtype), part.shape),
        shard,
        identity,
    )

    def hop(k, before):
        at = size - 1 - k
        reached = at > position
        new = combine(
            before, jax.tree.map(lambda part, own: part[at].astype(own.dtype), everything, shard)
        )
        return jax.tree.map(lambda a, b: jnp.where(reached, a, b), new, before)

    return lax.fori_loop(0, size, hop, start)


def layer_norm(residual, gain_row):
    center = jnp.mean(residual, axis=-1, keepdims=True)
    shifted = residual - center
    spread = jnp.mean(shifted * shifted, axis=-1, keepdims=True)
    return shifted * lax.rsqrt(spread + epsilon) * gain_row


def gelu_tanh(values):
    return jax.nn.gelu(values, approximate=True)


def shift_mix(key_ext, seg_ext, tap_weights):
    tap_count = tap_weights.shape[0]
    row_count = key_ext.shape[0] - tap_count + 1
    seg_now = seg_ext[tap_count - 1 :]
    running = jnp.zeros((row_count, key_ext.shape[1]), jnp.float32)
    for tap_index in range(tap_count):
        begin = tap_count - 1 - tap_index
        moved_rows = key_ext[begin : begin + row_count]
        same_doc = (seg_ext[begin : begin + row_count] == seg_now).astype(jnp.float32)
        running = running + moved_rows * same_doc[:, None] * tap_weights[tap_index][None, :]
    return running


def shift_back(key_ext, seg_ext, tap_weights, dshift):
    tap_count = tap_weights.shape[0]
    row_count = key_ext.shape[0] - tap_count + 1
    seg_now = seg_ext[tap_count - 1 :]
    dkey_ext = jnp.zeros(key_ext.shape, jnp.float32)
    tap_rows = []
    for tap_index in range(tap_count):
        begin = tap_count - 1 - tap_index
        same_doc = (seg_ext[begin : begin + row_count] == seg_now).astype(jnp.float32)
        masked_grad = dshift * same_doc[:, None]
        dkey_ext = dkey_ext + jnp.pad(
            masked_grad * tap_weights[tap_index][None, :], ((begin, tap_count - 1 - begin), (0, 0))
        )
        tap_rows.append(jnp.sum(masked_grad * key_ext[begin : begin + row_count], axis=0))
    return (dkey_ext, jnp.stack(tap_rows))


def decay_blocks(queries, shifted, values, decay_rate, seg_here, entry_seg):
    row_count, head_count, key_width = queries.shape
    block_rows = min(128, row_count)
    block_count = row_count // block_rows
    positions = jnp.arange(block_rows, dtype=jnp.float32)
    middle = 0.5 * block_rows
    log_keep = -decay_rate
    rise_amount = jnp.exp(log_keep[None] * (positions[:, None, None] + 1.0))
    query_fac = jnp.exp(log_keep[None] * (positions[:, None, None] - middle))
    key_fac = jnp.exp(log_keep[None] * (middle - positions[:, None, None]))
    tail_factor = jnp.exp(log_keep[None] * (block_rows - 1.0 - positions[:, None, None]))
    whole_fac = jnp.exp(log_keep * block_rows)
    causal = positions[:, None] >= positions[None, :]

    def one_block(carry, block_in):
        current_state, factor_now, seg_before = carry
        query_block_rows, key_block_rows, value_block_rows, seg_b = block_in
        carried_state = (seg_b == seg_before).astype(jnp.float32)
        block_result = jnp.einsum(
            "qlm,lmp->qlp",
            query_block_rows * rise_amount * carried_state[:, None, None],
            current_state,
            precision=highest_score,
        )
        scores = jnp.einsum(
            "thk,shk->hts",
            query_block_rows * query_fac,
            key_block_rows * key_fac,
            precision=highest_score,
        )
        allowed = causal & (seg_b[:, None] == seg_b[None, :])
        scores = jnp.where(allowed[None], scores, 0.0)
        block_result = block_result + jnp.einsum(
            "hts,shv->thv", scores, value_block_rows, precision=highest_score
        )
        seg_last = seg_b[block_rows - 1]
        keep_on = (seg_last == seg_before).astype(jnp.float32)
        input_final = (seg_b == seg_last).astype(jnp.float32)
        added_term = jnp.einsum(
            "zct,zcy->cty",
            key_block_rows * tail_factor * input_final[:, None, None],
            value_block_rows,
            precision=highest_score,
        )
        current_state = (whole_fac * keep_on)[:, :, None] * current_state + added_term
        factor_now = factor_now * whole_fac * keep_on
        return ((current_state, factor_now, seg_last), block_result)

    start_carry = (
        jnp.zeros((head_count, key_width, values.shape[2]), jnp.float32),
        jnp.ones((head_count, key_width), jnp.float32),
        entry_seg,
    )
    blocks_in = (
        queries.reshape(block_count, block_rows, head_count, key_width),
        shifted.reshape(block_count, block_rows, head_count, key_width),
        values.reshape(block_count, block_rows, head_count, -1),
        seg_here.reshape(block_count, block_rows),
    )
    (state_end, factor_end, seg_final), outs = lax.scan(
        jax.checkpoint(one_block), start_carry, blocks_in
    )
    return (outs.reshape(row_count, head_count, -1), factor_end, state_end)


def state_local(queries, shifted, values, decay_rate, seg_here, entry_seg):
    row_count = queries.shape[0]
    head_count = decay_rate.shape[0]
    scaled_values = queries * HEAD_DIM ** (-0.5)
    return decay_blocks(
        scaled_values.reshape(row_count, head_count, -1),
        shifted.reshape(row_count, head_count, -1),
        values.reshape(row_count, head_count, -1),
        decay_rate,
        seg_here,
        entry_seg,
    )


def entry_term(queries, decay_rate, seg_here, entry_seg, incoming_state):
    row_count = queries.shape[0]
    head_count = decay_rate.shape[0]
    scaled_values = (queries * HEAD_DIM ** (-0.5)).reshape(row_count, head_count, -1)
    positions = jnp.arange(row_count, dtype=jnp.float32)
    rise_amount = jnp.exp(-decay_rate[None] * (positions[:, None, None] + 1.0))
    carried_state = (seg_here == entry_seg).astype(jnp.float32)
    return jnp.einsum(
        "qlm,lmp->qlp",
        scaled_values * rise_amount * carried_state[:, None, None],
        incoming_state,
        precision=highest_score,
    )


def chain_join(earlier, later):
    return (later[0] * earlier[0], later[1] + later[0][..., None] * earlier[1])


def tensor_sum(partial_value):
    return lax.psum(partial_value.astype(jnp.bfloat16), "tp").astype(jnp.float32)


def gather_layer(proj_in, proj_out, proj_up, proj_down):
    return (
        lax.all_gather(proj_in, "fsdp", axis=1, tiled=True),
        lax.all_gather(proj_out, "fsdp", axis=1, tiled=True),
        lax.all_gather(proj_up, "fsdp", axis=0, tiled=True),
        lax.all_gather(proj_down, "fsdp", axis=1, tiled=True),
    )


def project_in(residual, gain_row, proj_in):
    normed = layer_norm(residual, gain_row).astype(jnp.bfloat16)
    triple = jnp.einsum("td,jdc->jtc", normed, proj_in, preferred_element_type=jnp.float32).astype(
        jnp.bfloat16
    )
    return triple


def feed_forward(residual, gain_row, proj_up, proj_down):
    normed = layer_norm(residual, gain_row).astype(jnp.bfloat16)
    up_values = jnp.dot(normed, proj_up, preferred_element_type=jnp.float32)
    hidden = gelu_tanh(up_values).astype(jnp.bfloat16)
    return residual + tensor_sum(jnp.dot(hidden, proj_down, preferred_element_type=jnp.float32))


def feed_back(residual, gain_row, proj_up, proj_down, grad_out):
    normed, norm_back = jax.vjp(layer_norm, residual, gain_row)
    normed_bf = normed.astype(jnp.bfloat16)
    up_values = jnp.dot(normed_bf, proj_up, preferred_element_type=jnp.float32)
    hidden, gelu_back = jax.vjp(gelu_tanh, up_values)
    hidden_bf = hidden.astype(jnp.bfloat16)
    grad_bf = grad_out.astype(jnp.bfloat16)
    down_grad = jnp.einsum("tf,td->fd", hidden_bf, grad_bf, preferred_element_type=jnp.float32)
    dhidden = jnp.einsum("td,fd->tf", grad_bf, proj_down, preferred_element_type=jnp.float32)
    dup_values = gelu_back(dhidden)[0].astype(jnp.bfloat16)
    up_grad = jnp.einsum("td,tf->df", normed_bf, dup_values, preferred_element_type=jnp.float32)
    dnormed = tensor_sum(
        jnp.einsum("tf,df->td", dup_values, proj_up, preferred_element_type=jnp.float32)
    )
    dresidual, dgain = norm_back(dnormed)
    return (grad_out + dresidual, dgain, up_grad, down_grad)


def project_back(normed_bf, norm_back, dtriple, proj_in):
    in_grad = jnp.einsum("td,jtc->jdc", normed_bf, dtriple, preferred_element_type=jnp.float32)
    dnormed = tensor_sum(
        jnp.einsum("jtc,jdc->td", dtriple, proj_in, preferred_element_type=jnp.float32)
    )
    dresidual, dgain = norm_back(dnormed)
    return (in_grad, dresidual, dgain)


def h3_forward(triple, seg_here, tap_weights, decay_rate):
    tap_count = tap_weights.shape[0]
    row_count = triple.shape[1]
    halo_keys, halo_segs = passed_along(
        (
            triple[1][row_count - tap_count + 1 :],
            seg_here[row_count - tap_count + 1 :].astype(jnp.bfloat16),
        ),
        "ctx",
        1,
    )
    entry_seg = halo_segs[tap_count - 2].astype(jnp.int32)
    seg_ext = jnp.concatenate([halo_segs.astype(jnp.int32), seg_here])
    key_ext = jnp.concatenate([halo_keys, triple[1]]).astype(jnp.float32)
    queries = triple[0].astype(jnp.float32)
    values = triple[2].astype(jnp.float32)
    shifted = shift_mix(key_ext, seg_ext, tap_weights)
    local_out, factor_end, state_end = state_local(
        queries, shifted, values, decay_rate, seg_here, entry_seg
    )
    identity = (jnp.ones_like(factor_end), jnp.zeros_like(state_end))
    incoming_state = carried_in((factor_end, state_end), "ctx", chain_join, identity)[1]
    mixer_out = local_out + entry_term(queries, decay_rate, seg_here, entry_seg, incoming_state)
    return (
        mixer_out.reshape(row_count, -1).astype(jnp.bfloat16),
        (halo_keys, halo_segs, incoming_state),
    )


def h3_back(
    residual, gain_row, proj_in, proj_out, kept_h3, tap_weights, decay_rate, seg_here, grad_out
):
    halo_keys, halo_segs, incoming_state = kept_h3
    normed, norm_back = jax.vjp(layer_norm, residual, gain_row)
    normed_bf = normed.astype(jnp.bfloat16)
    triple = jnp.einsum(
        "td,jdc->jtc", normed_bf, proj_in, preferred_element_type=jnp.float32
    ).astype(jnp.bfloat16)
    tap_count = tap_weights.shape[0]
    row_count, channels = (triple.shape[1], triple.shape[2])
    entry_seg = halo_segs[tap_count - 2].astype(jnp.int32)
    seg_ext = jnp.concatenate([halo_segs.astype(jnp.int32), seg_here])
    key_ext = jnp.concatenate([halo_keys, triple[1]]).astype(jnp.float32)
    queries = triple[0].astype(jnp.float32)
    values = triple[2].astype(jnp.float32)
    shifted = shift_mix(key_ext, seg_ext, tap_weights)

    def main_part(query_in, shift_in, value_in, rate_in):
        return state_local(query_in, shift_in, value_in, rate_in, seg_here, entry_seg)

    def entry_part(query_in, rate_in, state_part):
        return entry_term(query_in, rate_in, seg_here, entry_seg, state_part)

    (local_out, factor_end, state_end), main_back = jax.vjp(
        main_part, queries, shifted, values, decay_rate
    )
    entry_out, entry_back = jax.vjp(entry_part, queries, decay_rate, incoming_state)
    mixer_out = (local_out + entry_out).reshape(row_count, channels).astype(jnp.bfloat16)
    grad_bf = grad_out.astype(jnp.bfloat16)
    out_grad = jnp.einsum("tc,td->cd", mixer_out, grad_bf, preferred_element_type=jnp.float32)
    dmixed = jnp.einsum("td,cd->tc", grad_bf, proj_out, preferred_element_type=jnp.float32).reshape(
        local_out.shape
    )
    dquery_entry, drate_entry, dstate_in = entry_back(dmixed)
    identity = (jnp.ones_like(factor_end), jnp.zeros_like(dstate_in))
    dstate_end = entering((factor_end, dstate_in), "ctx", chain_join, identity)[1]
    dfactor = jnp.sum(dstate_end * incoming_state, axis=-1)
    dquery_main, dshift, dvalues, drate_main = main_back((dmixed, dfactor, dstate_end))
    dkey_ext, dtaps = shift_back(key_ext, seg_ext, tap_weights, dshift)
    halo_grad = passed_along(dkey_ext[: tap_count - 1].astype(jnp.bfloat16), "ctx", -1).astype(
        jnp.float32
    )
    dkeys = dkey_ext[tap_count - 1 :] + jnp.concatenate(
        [jnp.zeros((row_count - tap_count + 1, channels), jnp.float32), halo_grad]
    )
    dtriple = jnp.stack([dquery_main + dquery_entry, dkeys, dvalues]).astype(jnp.bfloat16)
    in_grad, dresidual, dgain = project_back(normed_bf, norm_back, dtriple, proj_in)
    return (grad_out + dresidual, dgain, in_grad, out_grad, dtaps, drate_main + drate_entry)


def attend_forward(triple, seg_here):
    row_count, channels = (triple.shape[1], triple.shape[2])
    head_count = channels // HEAD_DIM
    query_rows = triple[0].reshape(row_count, head_count, HEAD_DIM)
    query_pos = lax.axis_index("ctx") * row_count + jnp.arange(row_count, dtype=jnp.int32)
    key_pair = jnp.concatenate([triple[1], triple[2]], axis=1)
    score_scale = HEAD_DIM ** (-0.5)
    start_carry = (
        jnp.full((head_count, row_count), masked_low, jnp.float32),
        jnp.zeros((head_count, row_count), jnp.float32),
        jnp.zeros((row_count, head_count, HEAD_DIM), jnp.float32),
    )
    pair_rows = lax.all_gather(key_pair, "ctx", axis=0, tiled=True)
    seg_rows = lax.all_gather(seg_here.astype(jnp.bfloat16), "ctx", axis=0, tiled=True)
    block_rows = min(row_count, pair_rows.shape[0])
    block_count = pair_rows.shape[0] // block_rows
    pair_blocks = pair_rows.reshape(block_count, block_rows, 2, head_count, HEAD_DIM)
    seg_blocks = seg_rows.astype(jnp.int32).reshape(block_count, block_rows)
    offsets = jnp.arange(block_count, dtype=jnp.int32) * block_rows

    def key_block(running, block_in):
        pair_b, seg_b, offset = block_in

        def compute(state):
            row_top, row_total, accum = state
            key_pos = offset + jnp.arange(block_rows, dtype=jnp.int32)
            scores = (
                jnp.einsum(
                    "thd,shd->hts", query_rows, pair_b[:, 0], preferred_element_type=jnp.float32
                )
                * score_scale
            )
            allowed = (
                (key_pos[None, :] <= query_pos[:, None]) & (seg_b[None, :] == seg_here[:, None])
            )[None]
            masked = jnp.where(allowed, scores, masked_low)
            new_top = jnp.maximum(row_top, jnp.max(masked, axis=-1))
            shrink = jnp.exp(row_top - new_top)
            expo = jnp.where(allowed, jnp.exp(masked - new_top[:, :, None]), 0.0)
            row_total = row_total * shrink + jnp.sum(expo, axis=-1)
            accum = accum * shrink.T[:, :, None] + jnp.einsum(
                "hts,shd->thd",
                expo.astype(jnp.bfloat16),
                pair_b[:, 1],
                preferred_element_type=jnp.float32,
            )
            return (new_top, row_total, accum)

        skip_block = (
            (offset > query_pos[row_count - 1])
            | (seg_b[block_rows - 1] < seg_here[0])
            | (seg_b[0] > seg_here[row_count - 1])
        )
        return (lax.cond(skip_block, lambda state: state, compute, running), None)

    result, unused = lax.scan(key_block, start_carry, (pair_blocks, seg_blocks, offsets))
    row_top, row_total, accum = result
    mixer_raw = accum / row_total.T[:, :, None]
    return (mixer_raw.reshape(row_count, channels), row_top, row_total)


def block_grads(
    query_rows,
    grad_rows,
    row_top,
    row_total,
    inner,
    query_segs,
    query_pos,
    key_rows,
    value_rows,
    key_segs,
    key_pos,
):
    score_scale = HEAD_DIM ** (-0.5)
    scores = (
        jnp.einsum("thd,shd->hts", query_rows, key_rows, preferred_element_type=jnp.float32)
        * score_scale
    )
    allowed = (
        (key_pos[None, :] <= query_pos[:, None]) & (key_segs[None, :] == query_segs[:, None])
    )[None]
    expo = jnp.where(
        allowed, jnp.exp(jnp.where(allowed, scores, masked_low) - row_top[:, :, None]), 0.0
    )
    weighted = (grad_rows.astype(jnp.float32) / row_total.T[:, :, None]).astype(jnp.bfloat16)
    dprob = jnp.einsum("thd,shd->hts", weighted, value_rows, preferred_element_type=jnp.float32)
    dscore = (expo * (dprob - (inner / row_total)[:, :, None])).astype(jnp.bfloat16)
    dquery = (
        jnp.einsum("hts,shd->thd", dscore, key_rows, preferred_element_type=jnp.float32)
        * score_scale
    )
    dkey = (
        jnp.einsum("hts,thd->shd", dscore, query_rows, preferred_element_type=jnp.float32)
        * score_scale
    )
    dvalue = jnp.einsum(
        "hts,thd->shd", expo.astype(jnp.bfloat16), weighted, preferred_element_type=jnp.float32
    )
    return (dquery, dkey, dvalue)


def attend_back(
    residual, gain_row, proj_in, proj_out, mixer_raw, row_top, row_total, seg_here, grad_out
):
    normed, norm_back = jax.vjp(layer_norm, residual, gain_row)
    normed_bf = normed.astype(jnp.bfloat16)
    triple = jnp.einsum(
        "td,jdc->jtc", normed_bf, proj_in, preferred_element_type=jnp.float32
    ).astype(jnp.bfloat16)
    row_count, channels = (triple.shape[1], triple.shape[2])
    head_count = channels // HEAD_DIM
    grad_bf = grad_out.astype(jnp.bfloat16)
    out_grad = jnp.einsum(
        "tc,td->cd", mixer_raw.astype(jnp.bfloat16), grad_bf, preferred_element_type=jnp.float32
    )
    dmixed = jnp.einsum("td,cd->tc", grad_bf, proj_out, preferred_element_type=jnp.float32).astype(
        jnp.bfloat16
    )
    inner = jnp.sum(
        (dmixed.astype(jnp.float32) * mixer_raw).reshape(row_count, head_count, HEAD_DIM), axis=-1
    ).T
    query_rows = triple[0].reshape(row_count, head_count, HEAD_DIM)
    grad_rows = dmixed.reshape(row_count, head_count, HEAD_DIM)
    own_pos = lax.axis_index("ctx") * row_count + jnp.arange(row_count, dtype=jnp.int32)
    seg_bf = seg_here.astype(jnp.bfloat16)
    zero_rows = jnp.zeros((row_count, head_count, HEAD_DIM), jnp.float32)
    key_pair = jnp.concatenate([triple[1], triple[2]], axis=1)
    whole_pair, whole_segs = (
        lax.all_gather(key_pair, "ctx", axis=0, tiled=True),
        lax.all_gather(seg_bf, "ctx", axis=0, tiled=True),
    )
    block_count = whole_pair.shape[0] // row_count
    pair_blocks = whole_pair.reshape(block_count, row_count, 2, head_count, HEAD_DIM)
    seg_blocks = whole_segs.astype(jnp.int32).reshape(block_count, row_count)
    offsets = jnp.arange(block_count, dtype=jnp.int32) * row_count

    def key_step(dquery_total, block_in):
        pair_b, seg_b, offset = block_in

        def compute(unused):
            dquery, dkey, dvalue = block_grads(
                query_rows,
                grad_rows,
                row_top,
                row_total,
                inner,
                seg_here,
                own_pos,
                pair_b[:, 0],
                pair_b[:, 1],
                seg_b,
                offset + jnp.arange(row_count, dtype=jnp.int32),
            )
            return (
                dquery,
                jnp.concatenate(
                    [dkey.reshape(row_count, channels), dvalue.reshape(row_count, channels)], axis=1
                ),
            )

        def skipped(unused):
            return (zero_rows, jnp.zeros((row_count, 2 * channels), jnp.float32))

        skip_block = (
            (offset > own_pos[row_count - 1])
            | (seg_b[row_count - 1] < seg_here[0])
            | (seg_b[0] > seg_here[row_count - 1])
        )
        dquery, term = lax.cond(skip_block, skipped, compute, 0)
        return (dquery_total + dquery, term)

    dquery_total, terms = lax.scan(key_step, zero_rows, (pair_blocks, seg_blocks, offsets))
    mine = lax.psum_scatter(
        terms.reshape(block_count * row_count, 2 * channels).astype(jnp.bfloat16),
        "ctx",
        scatter_dimension=0,
        tiled=True,
    ).astype(jnp.float32)
    dquery_all = dquery_total.reshape(row_count, channels)
    dkey_all = mine[:, :channels]
    dvalue_all = mine[:, channels:]
    dtriple = jnp.stack([dquery_all, dkey_all, dvalue_all]).astype(jnp.bfloat16)
    in_grad, dresidual, dgain = project_back(normed_bf, norm_back, dtriple, proj_in)
    return (grad_out + dresidual, dgain, in_grad, out_grad)


def shards(
    inputs,
    cotangent,
    segments,
    gains,
    last_gain,
    in_weight,
    h3_out,
    attn_out,
    up_weight,
    down_weight,
    shift_taps,
    decay_rate,
):
    seg_here = segments[0] + 1
    start_rows = inputs[0].astype(jnp.float32)
    lower_layer = gather_layer(in_weight[0], h3_out, up_weight[0], down_weight[0])
    upper_layer = gather_layer(in_weight[1], attn_out, up_weight[1], down_weight[1])
    triple = project_in(start_rows, gains[0], lower_layer[0])
    mixer_out, kept_h3 = h3_forward(triple, seg_here, shift_taps, decay_rate)
    after_h3 = start_rows + tensor_sum(
        jnp.dot(mixer_out, lower_layer[1], preferred_element_type=jnp.float32)
    )
    after_ff1 = feed_forward(after_h3, gains[1], lower_layer[2], lower_layer[3])
    triple = project_in(after_ff1, gains[2], upper_layer[0])
    mixer_raw, row_top, row_total = attend_forward(triple, seg_here)
    after_attn = after_ff1 + tensor_sum(
        jnp.dot(mixer_raw.astype(jnp.bfloat16), upper_layer[1], preferred_element_type=jnp.float32)
    )
    final_rows = feed_forward(after_attn, last_gain, upper_layer[2], upper_layer[3])
    lower_layer = gather_layer(in_weight[0], h3_out, up_weight[0], down_weight[0])
    upper_layer = gather_layer(in_weight[1], attn_out, up_weight[1], down_weight[1])
    grad_rows = cotangent[0].astype(jnp.float32)
    grad_rows, gain_ff1, up_upper, down_upper = feed_back(
        after_attn, last_gain, upper_layer[2], upper_layer[3], grad_rows
    )
    grad_rows, gain_attn, in_upper, out_upper = attend_back(
        after_ff1,
        gains[2],
        upper_layer[0],
        upper_layer[1],
        mixer_raw,
        row_top,
        row_total,
        seg_here,
        grad_rows,
    )
    grad_rows, gain_ff0, up_lower, down_lower = feed_back(
        after_h3, gains[1], lower_layer[2], lower_layer[3], grad_rows
    )
    grad_rows, gain_h3, in_lower, out_lower, taps_back, rate_back = h3_back(
        start_rows,
        gains[0],
        lower_layer[0],
        lower_layer[1],
        kept_h3,
        shift_taps,
        decay_rate,
        seg_here,
        grad_rows,
    )
    weight_grads = (
        jnp.stack([in_lower, in_upper]),
        out_lower,
        out_upper,
        jnp.stack([up_lower, up_upper]),
        jnp.stack([down_lower, down_upper]),
        jnp.stack([gain_h3, gain_ff0, gain_attn]),
        gain_ff1,
        taps_back,
        rate_back,
    )
    weight_grads = (
        lax.psum_scatter(
            weight_grads[0].astype(jnp.bfloat16), "fsdp", scatter_dimension=2, tiled=True
        ).astype(jnp.float32),
        lax.psum_scatter(
            weight_grads[1].astype(jnp.bfloat16), "fsdp", scatter_dimension=1, tiled=True
        ).astype(jnp.float32),
        lax.psum_scatter(
            weight_grads[2].astype(jnp.bfloat16), "fsdp", scatter_dimension=1, tiled=True
        ).astype(jnp.float32),
        lax.psum_scatter(
            weight_grads[3].astype(jnp.bfloat16), "fsdp", scatter_dimension=1, tiled=True
        ).astype(jnp.float32),
        lax.psum_scatter(
            weight_grads[4].astype(jnp.bfloat16), "fsdp", scatter_dimension=2, tiled=True
        ).astype(jnp.float32),
        lax.psum_scatter(
            weight_grads[5].astype(jnp.bfloat16), "fsdp", scatter_dimension=1, tiled=True
        ).astype(jnp.float32),
        lax.psum_scatter(
            weight_grads[6].astype(jnp.bfloat16), "fsdp", scatter_dimension=0, tiled=True
        ).astype(jnp.float32),
        lax.psum_scatter(
            weight_grads[7].astype(jnp.bfloat16), "fsdp", scatter_dimension=0, tiled=True
        ).astype(jnp.float32),
        lax.psum_scatter(
            weight_grads[8].astype(jnp.bfloat16), "fsdp", scatter_dimension=1, tiled=True
        ).astype(jnp.float32),
    )
    weight_grads = (
        lax.psum(weight_grads[0].astype(jnp.bfloat16), "ctx").astype(jnp.float32),
        lax.psum(weight_grads[1].astype(jnp.bfloat16), "ctx").astype(jnp.float32),
        lax.psum(weight_grads[2].astype(jnp.bfloat16), "ctx").astype(jnp.float32),
        lax.psum(weight_grads[3].astype(jnp.bfloat16), "ctx").astype(jnp.float32),
        lax.psum(weight_grads[4].astype(jnp.bfloat16), "ctx").astype(jnp.float32),
        lax.psum(weight_grads[5].astype(jnp.bfloat16), "ctx").astype(jnp.float32),
        lax.psum(weight_grads[6].astype(jnp.bfloat16), "ctx").astype(jnp.float32),
        lax.psum(weight_grads[7].astype(jnp.bfloat16), "ctx").astype(jnp.float32),
        lax.psum(weight_grads[8].astype(jnp.bfloat16), "ctx").astype(jnp.float32),
    )
    return (
        final_rows.astype(jnp.bfloat16)[None],
        grad_rows[None],
        weight_grads[5],
        weight_grads[6],
        weight_grads[0],
        weight_grads[1],
        weight_grads[2],
        weight_grads[3],
        weight_grads[4],
        weight_grads[7],
        weight_grads[8],
    )


def solution(mesh):
    placed = (
        P("fsdp", "ctx", None),
        P("fsdp", "ctx", None),
        P("fsdp", "ctx"),
        P(),
        P(),
        P(None, None, "fsdp", "tp"),
        P("tp", "fsdp"),
        P("tp", "fsdp"),
        P(None, "fsdp", "tp"),
        P(None, "tp", "fsdp"),
        P(None, "tp"),
        P("tp", None),
    )
    return jax.shard_map(
        shards,
        mesh=mesh,
        in_specs=placed,
        out_specs=(
            P("fsdp", "ctx", None),
            P("fsdp", "ctx", None),
            P(None, "fsdp"),
            P("fsdp"),
            P(None, None, "fsdp", "tp"),
            P("tp", "fsdp"),
            P("tp", "fsdp"),
            P(None, "fsdp", "tp"),
            P(None, "tp", "fsdp"),
            P("fsdp", "tp"),
            P("tp", "fsdp"),
        ),
        check_vma=False,
    )
```

profile of v0, /device:TPU:1, one launch (start us, length us, event | category | flops | bytes accessed | tf_op | source)
XLA Modules:
  0.0 1160.2 jit_solution(3864178973581250741)
XLA Ops:
  16.2 16.5 %all-gather = bf16[1,3,768,192]{3,1,0,2:T(4,128)(2,1)S(1)} all-gather(bf16[1,3,192,192]{3,1,0,2:T(4,128)(2,1)S(1)} %copy.150), channel_id=2, replica_groups=mesh['fsdp'=4,'ctx'=2,'tp'=4] {'fsdp'}, dimensions={2}, use_global_device_ids=true | all-gather | bytes 1105920 | tf_op jit(solution)/shard_map/all_gather | solution.py:209
  47.0 7.7 all_gather.69
  66.7 15.5 %multiply_add_fusion.3 = f32[768,192]{0,1:T(8,128)S(1)} fusion(f32[831,192]{0,1:T(8,128)S(1)} %maximum_convert_fusion, f32[192]{0:T(256)} %bitcast.1061, f32[768]{0:T(1024)} %get-tuple-element.2578, f32[192]{0:T(256)} %bitcast.1063, f32[768]{0:T(1024)} %get-tuple-element.2579, f32[192]{0:T(256)} %bitcast.1083, f32[768]{0:T(1024)} %get-tuple-element.2580, ...), kind=kLoop, calls=%fused_computation.506 | loop fusion | flops 28016640 | bytes 38581248 | tf_op jit(solution)/shard_map/add | solution.py:84
  85.7 58.2 %while.140 = (s32[]{:T(128)}, f32[3,64,64]{2,1,0:T(8,128)S(1)}, f32[3,64]{1,0:T(4,128)S(1)}, s32[]{:T(128)}, f32[6,128,3,64]{1,0,3,2:T(8,128)}, /*index=5*/f32[6...) while((s32[]{:T(128)}, f32[3,64,64]{2,1,0:T(8,128)S(1)}, ...), condition=%wide.region_38.39_spmd.clone.clone.clone, body=%wide.region_37.38_spmd.clone.clone.clone.sunk | while | flops 113677760 | bytes 1925656 | solution.py:164
  90.9 3.8 dynamic_update_slice.100
  100.6 3.8 dynamic_update_slice.100
  110.3 3.8 dynamic_update_slice.100
  120.0 3.8 dynamic_update_slice.100
  129.7 3.8 dynamic_update_slice.100
  139.4 3.8 dynamic_update_slice.100
  144.9 50.3 %while.139 = (s32[]{:T(128)}, f32[3,64,64]{2,1,0:T(8,128)S(1)}, f32[3,64]{1,0:T(4,128)S(1)}, s32[]{:T(128)}, f32[6,128,3,64]{1,0,3,2:T(8,128)}, /*index=5*/s32[6...) while((s32[]{:T(128)}, f32[3,64,64]{2,1,0:T(8,128)S(1)}, ...), condition=%wide.region_3.4_spmd.clone.clone.clone, body=%wide.region_2.3_spmd.clone.clone.clone.sunk | while | flops 113665280 | bytes 1775338 | solution.py:164
  148.8 3.8 dynamic_update_slice.97
  165.6 3.8 dynamic_update_slice.97
  173.9 3.8 dynamic_update_slice.97
  190.7 3.8 dynamic_update_slice.97
  198.0 6.7 all-gather.10
  217.9 52.7 %all-reduce.82.cloned.1.call-done = bf16[768,768]{1,0:T(8,128)(2,1)} async-done(((bf16[768,768]{1,0:T(8,128)(2,1)}), bf16[768,768]{1,0:T(8,128)(2,1)}) %all-reduce.82.cloned.1.call-update) | async-done | bytes 1179664 | tf_op jit(solution)/shard_map/psum | solution.py:204
  273.0 4.0 fusion.227
  277.0 4.6 convolution_convert_fusion.8
  281.9 17.0 %all-gather.5 = bf16[1,3,768,192]{3,1,0,2:T(4,128)(2,1)S(1)} all-gather(bf16[1,3,192,192]{3,1,0,2:T(4,128)(2,1)S(1)} %copy.151), channel_id=7, replica_groups=mesh['fsdp'=4,'ctx'=2,'tp'=4] {'fsdp'}, dimensions={2}, use_global_device_ids=true | all-gather | bytes 1105920 | tf_op jit(solution)/shard_map/all_gather | solution.py:209
  301.0 36.2 %all-reduce.84.cloned.1.call-done = bf16[768,768]{1,0:T(8,128)(2,1)} async-done(((bf16[768,768]{1,0:T(8,128)(2,1)}), bf16[768,768]{1,0:T(8,128)(2,1)}) %all-reduce.84.cloned.1.call-update) | async-done | bytes 1179664 | tf_op jit(solution)/shard_map/psum | solution.py:204
  346.7 9.2 all_gather.75
  362.6 29.6 %while.136 = (s32[]{:T(128)}, f32[3,768]{1,0:T(4,128)S(1)}, f32[3,768]{1,0:T(4,128)}, f32[768,3,64]{0,2,1:T(8,128)}, s32[2]{0:T(128)}, /*index=5*/s32[768]{0:T(1...) while((s32[]{:T(128)}, f32[3,768]{1,0:T(4,128)S(1)}, ...), condition=%wide.region_17.18_spmd, body=%wide.region_12.17_spmd.sunk | while | flops 478060032 | bytes 31737276 | solution.py:393
  381.1 11.1 conditional.5
  397.0 64.0 %all-reduce.86.cloned.1.call-done = bf16[768,768]{1,0:T(8,128)(2,1)} async-done(((bf16[768,768]{1,0:T(8,128)(2,1)}), bf16[768,768]{1,0:T(8,128)(2,1)}) %all-reduce.86.cloned.1.call-update) | async-done | bytes 1179664 | tf_op jit(solution)/shard_map/psum | solution.py:204
  464.5 4.5 fusion.219
  469.0 4.6 fusion.196
  477.1 55.4 %all-reduce.88.cloned.1.call-done = bf16[768,768]{1,0:T(8,128)(2,1)} async-done(((bf16[768,768]{1,0:T(8,128)(2,1)}), bf16[768,768]{1,0:T(8,128)(2,1)}) %all-reduce.88.cloned.1.call-update) | async-done | bytes 1179664 | tf_op jit(solution)/shard_map/psum | solution.py:204
  541.9 38.6 %while.137 = (s32[]{:T(128)}, f32[768,3,64]{0,2,1:T(8,128)}, bf16[2,768,384]{1,2,0:T(8,128)(2,1)}, s32[2]{0:T(128)}, s32[768]{0:T(1024)}, /*index=5*/s32[2,768]{...) while((s32[]{:T(128)}, f32[768,3,64]{0,2,1:T(8,128)}, ...), condition=%wide.region_29.30_spmd.clone, body=%wide.region_26.29_spmd.clone.sunk | while | flops 1158269952 | bytes 43460520 | solution.py:510
  561.9 15.8 %conditional.6 = (f32[768,3,64]{0,2,1:T(8,128)S(1)}, bf16[1,768,384]{1,2,0:T(8,128)(2,1)S(1)}) conditional(s32[]{:T(128)} %convert_element_type.1337, (s32[]{:T(128)}, s32[768]{0:T(1024)}, s32[1,768]{1,0:T(1,128)S(1)}, s32[768]{0:T(1024)S(1)}, bf16[2,768,2,3,64]{1,4,3,2,0:T(8,128)(2,1)}, /*index=5*/s32[]{:T(128)}, bf16[768,3,64]{0,2,1:T(8,128)(2,1)}, ...), branch_computations={%region_27.27_spmd, %region_28.28_spmd} | conditional | flops 1157975040 | bytes 40504376 | solution.py:507
  583.1 23.8 %reduce-scatter.17.cloned.1.call-done = bf16[768,384]{0,1:T(8,128)(2,1)} async-done(((bf16[1536,384]{0,1:T(8,128)(2,1)}), bf16[768,384]{0,1:T(8,128)(2,1)}) %reduce-scatter.17.cloned.1.call-update) | async-done | bytes 589840 | tf_op jit(solution)/shard_map/reduce_scatter | solution.py:511
  612.3 56.8 %all-reduce.90.cloned.1.call-done = bf16[768,768]{1,0:T(8,128)(2,1)} async-done(((bf16[768,768]{1,0:T(8,128)(2,1)}), bf16[768,768]{1,0:T(8,128)(2,1)}) %all-reduce.90.cloned.1.call-update) | async-done | bytes 1179664 | tf_op jit(solution)/shard_map/psum | solution.py:204
  682.7 4.3 convolution_convert_fusion.6
  688.5 47.6 %all-reduce.92.cloned.1.call-done = bf16[768,768]{1,0:T(8,128)(2,1)} async-done(((bf16[768,768]{1,0:T(8,128)(2,1)}), bf16[768,768]{1,0:T(8,128)(2,1)}) %all-reduce.92.cloned.1.call-update) | async-done | bytes 1179664 | tf_op jit(solution)/shard_map/psum | solution.py:204
  754.1 122.1 %while.141 = (s32[]{:T(128)}, f32[128,3,64]{0,2,1:T(8,128)S(1)}, f32[128,3,64]{0,2,1:T(8,128)S(1)}, f32[128,3,64]{0,2,1:T(8,128)S(1)}, f32[128,3,64]{0,2,1:T(8,1...) while((s32[]{:T(128)}, f32[128,3,64]{0,2,1:T(8,128)S(1)}, ...), condition=%wide.region_44.45_spmd.clone.clone.clone, body=%wide.region_42.44_spmd.clone.clone.clone.sunk | while | flops 265250624 | bytes 7128167 | solution.py:164
  766.8 3.8 dynamic_update_slice.104
  827.8 3.8 dynamic_update_slice.104
  907.8 18.2 %pad_add_fusion = f32[831,192]{0,1:T(8,128)S(1)} fusion(f32[768,192]{0,1:T(8,128)} %fusion.303, f32[768,192]{0,1:T(8,128)} %get-tuple-element.2504, f32[768,192]{0,1:T(8,128)} %get-tuple-element.2503, f32[768,192]{0,1:T(8,128)} %get-tuple-element.2502, f32[768,192]{0,1:T(8,128)} %get-tuple-element.2501, f32[768,192]{0,1:T(8,128)} %get-tuple-element.2500, ...), kind=kLoop, calls=%fused_computation.356 | loop fusion | flops 10051776 | bytes 38386944 | tf_op jit(solution)/shard_map/add | solution.py:98
  936.3 4.5 fusion.204
  942.2 3.9 fusion.203
  947.7 6.9 copy.118
  960.9 5.9 copy.132
  966.8 6.9 reshape.699
  995.0 36.4 %all-reduce.96.cloned.1.call-done = (bf16[768,768]{1,0:T(8,128)(2,1)}, bf16[768,768]{1,0:T(8,128)(2,1)}) async-done(((bf16[768,768]{1,0:T(8,128)(2,1)}, bf16[768,768]{1,0:T(8,128)(2,1)}), (bf16[768,768]{1,0:T(8,128)(2,1)}, bf16[768,768]{1,0:T(8,128)(2,1)})) %all-reduce.96.cloned.1.call-update) | async-done | bytes 2359312 | tf_op jit(solution)/shard_map/psum | solution.py:204
  1039.7 4.9 stack.406
  1046.3 65.9 %all-reduce.94.cloned.1.call-done = bf16[2,768,768]{1,0,2:T(2,128)(2,1)} async-done(((bf16[2,768,768]{1,0,2:T(2,128)(2,1)}), bf16[2,768,768]{1,0,2:T(2,128)(2,1)}) %all-reduce.94.cloned.1.call-update) | async-done | bytes 2359312
  1122.6 6.9 all-reduce.69
  1136.1 6.6 all-reduce.70
  (1339 shorter events, 453.1 us)
Async XLA Ops:
  8.0 262.5 %all-reduce.82.cloned.1.call-start = ((), (), s32[]{:S(2)}) async-start(), calls=%async_computation.7 | async-start | bytes 2359296 | tf_op jit(solution)/shard_map/psum | solution.py:204
  9.4 49.7 %collective-permute-start = (bf16[63]{0:T(256)(128)(2,1)}, bf16[63]{0:T(256)(128)(2,1)}, u32[]{:S(2)}, u32[]{:S(2)}) collective-permute-start(bf16[63]{0:T(256)(128)(2,1)} %fusion.386), channel_id=1, source_target_pairs={{0,4},{1,5},{2,6},{3,7},{8,12},{9,13},{10,14},{11,15},{16,20},{17,... | collective-permute-start | bytes 386 | tf_op jit(solution)/shard_map/ppermute | solution.py:17
  38.8 26.1 %collective-permute-start.1 = (bf16[63,192]{0,1:T(8,128)(2,1)}, bf16[63,192]{0,1:T(8,128)(2,1)}, u32[]{:S(2)}, u32[]{:S(2)}) collective-permute-start(bf16[63,192]{0,1:T(8,128)(2,1)} %slice_bitcast_fusion.14), channel_id=1, source_target_pairs={{0,4},{1,5},{2,6},{3,7},{8,12},{9,13},{10,14},{11,15},{16,20},{17,... | collective-permute-start | bytes 72584 | tf_op jit(solution)/shard_map/ppermute | solution.py:17
  85.7 59.2 %copy-start.101 = (f32[3,64]{1,0:T(4,128)S(1)}, f32[3,64]{1,0:T(4,128)}, u32[]{:S(2)}) copy-start(f32[3,64]{1,0:T(4,128)} %custom-call.1) | copy-start | bytes 2308
  214.5 58.4 %all-gather.21.cloned.1.call-start = ((), (), s32[]{:S(2)}) async-start(), calls=%async_computation.17 | async-start | bytes 1474560 | tf_op jit(solution)/shard_map/all_gather | solution.py:211
  216.5 60.5 %all-gather.23.cloned.1.call-start = ((), (), s32[]{:S(2)}) async-start(), calls=%async_computation.18 | async-start | bytes 1474560 | tf_op jit(solution)/shard_map/all_gather | solution.py:212
  217.8 55.1 %copy-start.111 = (f32[768]{0:T(1024)S(1)}, f32[768]{0:T(1024)}, u32[]{:S(2)}) copy-start(f32[768]{0:T(1024)} %get-tuple-element.2188) | copy-start | bytes 9220
  217.8 119.4 %all-reduce.84.cloned.1.call-start = ((), (), s32[]{:S(2)}) async-start(), calls=%async_computation.8 | async-start | bytes 2359296 | tf_op jit(solution)/shard_map/psum | solution.py:204
  281.6 75.4 %all-gather.19.cloned.1.call-start = ((), (), s32[]{:S(2)}) async-start(), calls=%async_computation.9 | async-start | bytes 1769472 | tf_op jit(solution)/shard_map/all_gather | solution.py:350
  339.4 333.6 %copy-start.4 = (f32[768,768]{1,0:T(8,128)}, f32[768,768]{1,0:T(8,128)S(1)}, u32[]{:S(2)}) copy-start(f32[768,768]{1,0:T(8,128)S(1)} %get-tuple-element.2400) | copy-start | bytes 7077892
  344.0 117.0 %all-reduce.86.cloned.1.call-start = ((), (), s32[]{:S(2)}) async-start(), calls=%async_computation.10 | async-start | bytes 2359296 | tf_op jit(solution)/shard_map/psum | solution.py:204
  395.6 68.9 %all-gather.25.cloned.1.call-start = ((), (), s32[]{:S(2)}) async-start(), calls=%async_computation.19 | async-start | bytes 1474560 | tf_op jit(solution)/shard_map/all_gather | solution.py:211
  396.2 72.8 %all-gather.27.cloned.1.call-start = ((), (), s32[]{:S(2)}) async-start(), calls=%async_computation.20 | async-start | bytes 1474560 | tf_op jit(solution)/shard_map/all_gather | solution.py:212
  396.9 135.5 %all-reduce.88.cloned.1.call-start = ((), (), s32[]{:S(2)}) async-start(), calls=%async_computation.11 | async-start | bytes 2359296 | tf_op jit(solution)/shard_map/psum | solution.py:204
  462.6 73.6 %copy-start.106 = (f32[768]{0:T(1024)}, f32[768]{0:T(1024)S(1)}, u32[]{:S(2)}) copy-start(f32[768]{0:T(1024)S(1)} %broadcast_multiply_fusion.3) | copy-start | bytes 9220
  464.5 71.7 %copy-start.264 = (f32[768]{0:T(1024)}, f32[768]{0:T(1024)S(1)}, u32[]{:S(2)}) copy-start(f32[768]{0:T(1024)S(1)} %fusion.377) | copy-start | bytes 9220
  476.9 130.0 %reduce-scatter.17.cloned.1.call-start = ((), (), s32[]{:S(2)}) async-start(), calls=%async_computation.12 | async-start | bytes 1769472 | tf_op jit(solution)/shard_map/reduce_scatter | solution.py:511
  583.0 86.2 %all-reduce.90.cloned.1.call-start = ((), (), s32[]{:S(2)}) async-start(), calls=%async_computation.13 | async-start | bytes 2359296 | tf_op jit(solution)/shard_map/psum | solution.py:204
  608.7 60.5 %copy-start.95 = (f32[768]{0:T(1024)S(1)}, f32[768]{0:T(1024)}, u32[]{:S(2)}) copy-start(f32[768]{0:T(1024)} %copy-done.94) | copy-start | bytes 9220
  608.7 60.5 %copy-start.254 = (f32[768]{0:T(1024)S(1)}, f32[768]{0:T(1024)}, u32[]{:S(2)}) copy-start(f32[768]{0:T(1024)} %get-tuple-element.2186) | copy-start | bytes 9220
  612.0 59.1 %copy-start.271 = (f32[768]{0:T(1024)S(1)}, f32[768]{0:T(1024)}, u32[]{:S(2)}) copy-start(f32[768]{0:T(1024)} %copy-done.270) | copy-start | bytes 9220
  612.0 59.1 %copy-start.273 = (f32[768]{0:T(1024)S(1)}, f32[768]{0:T(1024)}, u32[]{:S(2)}) copy-start(f32[768]{0:T(1024)} %copy-done.272) | copy-start | bytes 9220
  612.1 124.1 %all-reduce.92.cloned.1.call-start = ((), (), s32[]{:S(2)}) async-start(), calls=%async_computation.14 | async-start | bytes 2359296 | tf_op jit(solution)/shard_map/psum | solution.py:204
  680.5 302.0 %reduce-scatter.29.cloned.1.call-start = ((), (), s32[]{:S(2)}) async-start(), calls=%async_computation.24 | async-start | bytes 491520
  687.1 49.1 %copy-start.3 = (bf16[1,768,768]{2,1,0:T(8,128)(2,1)S(1)}, bf16[1,768,768]{2,1,0:T(8,128)(2,1)}, u32[]{:S(2)}) copy-start(bf16[1,768,768]{2,1,0:T(8,128)(2,1)} %param.30) | copy-start | bytes 3538948
  687.1 49.1 %copy-start.9 = (bf16[768,768]{1,0:T(8,128)(2,1)S(1)}, bf16[768,768]{1,0:T(8,128)(2,1)}, u32[]{:S(2)}) copy-start(bf16[768,768]{1,0:T(8,128)(2,1)} %all-reduce.82.cloned.1.call-done) | copy-start | bytes 3538948
  687.1 49.1 %copy-start.92 = (f32[768]{0:T(1024)S(1)}, f32[768]{0:T(1024)}, u32[]{:S(2)}) copy-start(f32[768]{0:T(1024)} %copy-done.91) | copy-start | bytes 9220
  687.5 50.8 %copy-start.269 = (f32[768]{0:T(1024)S(1)}, f32[768]{0:T(1024)}, u32[]{:S(2)}) copy-start(f32[768]{0:T(1024)} %copy-done.268) | copy-start | bytes 9220
  687.5 50.8 %copy-start.257 = (f32[768]{0:T(1024)S(1)}, f32[768]{0:T(1024)}, u32[]{:S(2)}) copy-start(f32[768]{0:T(1024)} %copy-done.256) | copy-start | bytes 9220
  688.5 343.0 %all-reduce.96.cloned.1.call-start = ((), (), s32[]{:S(2)}) async-start(), calls=%async_computation.26 | async-start | bytes 4718592 | tf_op jit(solution)/shard_map/psum | solution.py:204
  754.0 122.2 %copy-start.1 = (f32[831,192]{0,1:T(8,128)S(1)}, f32[831,192]{0,1:T(8,128)}, u32[]{:S(2)}) copy-start(f32[831,192]{0,1:T(8,128)} %copy-done) | copy-start | bytes 1914628
  754.0 122.2 %copy-start.244 = (f32[768]{0:T(1024)S(1)}, f32[768]{0:T(1024)}, u32[]{:S(2)}) copy-start(f32[768]{0:T(1024)} %get-tuple-element.2578) | copy-start | bytes 9220
  754.0 122.2 %copy-start.245 = (f32[768]{0:T(1024)S(1)}, f32[768]{0:T(1024)}, u32[]{:S(2)}) copy-start(f32[768]{0:T(1024)} %get-tuple-element.2579) | copy-start | bytes 9220
  754.0 122.2 %copy-start.246 = (f32[768]{0:T(1024)S(1)}, f32[768]{0:T(1024)}, u32[]{:S(2)}) copy-start(f32[768]{0:T(1024)} %get-tuple-element.2580) | copy-start | bytes 9220
  754.0 122.2 %copy-start.247 = (f32[768]{0:T(1024)S(1)}, f32[768]{0:T(1024)}, u32[]{:S(2)}) copy-start(f32[768]{0:T(1024)} %get-tuple-element.2581) | copy-start | bytes 9220
  754.0 122.2 %copy-start.248 = (f32[768]{0:T(1024)S(1)}, f32[768]{0:T(1024)}, u32[]{:S(2)}) copy-start(f32[768]{0:T(1024)} %get-tuple-element.2582) | copy-start | bytes 9220
  754.0 122.2 %copy-start.249 = (f32[768]{0:T(1024)S(1)}, f32[768]{0:T(1024)}, u32[]{:S(2)}) copy-start(f32[768]{0:T(1024)} %get-tuple-element.2583) | copy-start | bytes 9220
  754.0 122.2 %copy-start.250 = (f32[768]{0:T(1024)S(1)}, f32[768]{0:T(1024)}, u32[]{:S(2)}) copy-start(f32[768]{0:T(1024)} %get-tuple-element.2584) | copy-start | bytes 9220
  754.0 122.2 %copy-start.251 = (f32[768]{0:T(1024)S(1)}, f32[768]{0:T(1024)}, u32[]{:S(2)}) copy-start(f32[768]{0:T(1024)} %get-tuple-element.2585) | copy-start | bytes 9220
  754.0 122.2 %copy-start.252 = (f32[768]{0:T(1024)S(1)}, f32[768]{0:T(1024)}, u32[]{:S(2)}) copy-start(f32[768]{0:T(1024)} %get-tuple-element.2586) | copy-start | bytes 9220
  926.7 5.0 collective-permute-start.2
  936.3 108.4 %reduce-scatter.27.cloned.1.call-start = ((), (), s32[]{:S(2)}) async-start(), calls=%async_computation.23 | async-start | bytes 491520
  942.2 170.0 %all-reduce.94.cloned.1.call-start = ((), (), s32[]{:S(2)}) async-start(), calls=%async_computation.25 | async-start | bytes 4718592
  954.7 159.9 %reduce-scatter.25.cloned.1.call-start = ((), (), s32[]{:S(2)}) async-start(), calls=%async_computation.22 | async-start | bytes 2211840
  973.8 146.0 %reduce-scatter.19.cloned.1.call-start = ((), (), s32[]{:S(2)}) async-start(), calls=%async_computation.15 | async-start | bytes 2949120 | tf_op jit(solution)/shard_map/reduce_scatter | solution.py:607
  980.6 154.7 %reduce-scatter.23.cloned.1.call-start = ((), (), s32[]{:S(2)}) async-start(), calls=%async_computation.21 | async-start | bytes 245760
  1036.7 99.4 %reduce-scatter.21.cloned.1.call-start = ((), (), s32[]{:S(2)}) async-start(), calls=%async_computation.16 | async-start | bytes 40960 | tf_op jit(solution)/shard_map/reduce_scatter | solution.py:619
  1044.6 100.5 %all-reduce.98.cloned.1.call-start = ((), (), s32[]{:S(2)}) async-start(), calls=%async_computation.27 | async-start | bytes 3932160 | tf_op jit(solution)/shard_map/psum | solution.py:627
  (317 other events, 1924.2 us)
Sparse Core Ops, SparseCore 0:
  214.6 55.8 all-reduce.81
  281.7 55.4 all-reduce.83
  344.1 8.9 all-gather.18
  395.7 65.2 all-reduce.85
  477.0 55.4 all-reduce.87
  583.1 23.7 reduce-scatter.16
  612.2 56.9 all-reduce.89
  680.7 55.4 all-reduce.91
  936.4 95.0 all-reduce.95
  1034.4 77.7 all-reduce.93
  1120.0 21.7 all-reduce.97
Sparse Core Ops, SparseCore 1:
  217.4 27.2 all-gather.20
  246.9 27.5 all-gather.22
  398.5 36.5 all-gather.24
  437.5 27.5 all-gather.26
  688.5 23.1 reduce-scatter.28
  942.3 23.2 reduce-scatter.26
  973.8 31.4 reduce-scatter.24
  1009.1 37.2 reduce-scatter.18
  1049.8 25.1 reduce-scatter.22
  1078.0 35.7 reduce-scatter.20
where the time goes:
time: 1170 us; the launch traced here: 1160 us
  waiting for transfers between devices  441 us (38%)
  local copies, waits for them, and re-layouts  262 us (22%)
  other arithmetic  178 us (15%)
  matrix products  130 us (11%)
  blocking collectives  78.9 us (7%)
  loops' own time  40.8 us (3%)
  between operations  22.8 us (2%)
    psum x7, waiting for transfers between devices, tensor_sum(): lax.psum(partial_value.astype(jnp.bfloat16), 'tp').astype(jnp.float32)  349 us
    dynamic_update_slice x30, local copies, waits for them, and re-layouts, decay_blocks(): lax.scan(jax.checkpoint(one_block), start_carry, blocks_in)  92.5 us
    unnamed x26, waiting for transfers between devices  67.5 us
    unnamed x701, local copies, waits for them, and re-layouts  51.1 us
    all_gather x2, blocking collectives, gather_layer(): lax.all_gather(proj_in, 'fsdp', axis=1, tiled=True)  33.5 us
    another operation x3, loops' own time, decay_blocks(): lax.scan(jax.checkpoint(one_block), start_carry, blocks_in)  24.7 us
    reduce_scatter x1, waiting for transfers between devices, attend_back(): lax.psum_scatter(terms.reshape(block_count * row_count, 2 * channels).ast...  23.8 us
  transfers between devices with their start and end apart: 24, of which 9 were waited for; matrix products, arithmetic and copies ran while one was open for 28% of the time, Pallas kernels for 0%

commit v1 on v0

v1 whole, which is shorter than its diff:
```python
import functools

import jax
import jax.numpy as jnp
from jax import lax
from jax.experimental import pallas as pl
from jax.experimental.pallas import tpu as pltpu
from jax.sharding import PartitionSpec as P

HEAD_DIM = 64
epsilon = 1e-05
masked_low = -1e30
bf16 = jnp.bfloat16
f32 = jnp.float32
scale = HEAD_DIM ** (-0.5)
CHUNK = 256
LIMIT = 56 * 1024 * 1024


def nn(a, b):
    return lax.dot_general(a, b, (((1,), (0,)), ((), ())), preferred_element_type=f32)


def nt(a, b):
    return lax.dot_general(a, b, (((1,), (1,)), ((), ())), preferred_element_type=f32)


def tn(a, b):
    return lax.dot_general(a, b, (((0,), (0,)), ((), ())), preferred_element_type=f32)


def head_masks(rows, channels):
    lane = lax.broadcasted_iota(jnp.int32, (rows, channels), 1)
    return [(lane >= HEAD_DIM * h) & (lane < HEAD_DIM * (h + 1)) for h in range(channels // HEAD_DIM)]


def same_head(channels):
    row = lax.broadcasted_iota(jnp.int32, (channels, channels), 0) // HEAD_DIM
    lane = lax.broadcasted_iota(jnp.int32, (channels, channels), 1) // HEAD_DIM
    return row == lane


def call(kernel, outs, scratch=(), smem=0, n_in=0, flops=0, nbytes=0):
    vm = pl.BlockSpec(memory_space=pltpu.VMEM)
    sm = pl.BlockSpec(memory_space=pltpu.SMEM)
    return pl.pallas_call(
        kernel,
        out_shape=[jax.ShapeDtypeStruct(s, d) for s, d in outs],
        in_specs=[sm] * smem + [vm] * n_in,
        out_specs=[vm] * len(outs),
        scratch_shapes=list(scratch),
        compiler_params=pltpu.CompilerParams(vmem_limit_bytes=LIMIT),
        cost_estimate=pl.CostEstimate(flops=int(flops), bytes_accessed=int(nbytes), transcendentals=0),
    )


def rolled_down(ext_ref, copies, rows):
    for r in range(8):
        copies[r, 8:rows, :] = ext_ref[8 - r : rows - r, :]


def shift_kernel(taps_n, key_ref, halo_ref, taps_ref, age_ref, tail_ref, value_ref, ks_ref, st_ref, ext, copies):
    rows, channels = key_ref.shape
    ext[0:taps_n, :] = halo_ref[...].astype(f32)
    ext[taps_n : taps_n + rows, :] = key_ref[...].astype(f32)
    rolled_down(ext, copies, rows + taps_n)

    def block(b, carry):
        start = pl.multiple_of(b * 64, 64)
        age = age_ref[pl.ds(start, 64), :]
        acc = jnp.zeros((64, channels), f32)
        for m in range(taps_n // 8):
            for r in range(8):
                j = 8 * m + r
                moved = copies[r, pl.ds(start + taps_n - 8 * m, 64), :]
                acc = acc + jnp.where(age >= j, moved, 0.0) * taps_ref[j : j + 1, :]
        ks_ref[pl.ds(start, 64), :] = acc
        return carry

    lax.fori_loop(0, rows // 64, block, 0)
    kt = (ks_ref[...] * tail_ref[...]).astype(bf16)
    st_ref[...] = jnp.where(same_head(channels), tn(value_ref[...], kt), 0.0)


def shift_forward(key, halo, taps, age, tail, value):
    rows, channels = key.shape
    taps_n = taps.shape[0]
    return call(
        functools.partial(shift_kernel, taps_n),
        [((rows, channels), f32), ((channels, channels), f32)],
        [pltpu.VMEM((rows + taps_n, channels), f32), pltpu.VMEM((8, rows + taps_n, channels), f32)],
        n_in=6,
        flops=4 * rows * channels * taps_n * 20,
        nbytes=4e6,
    )(key, halo, taps, age, tail, value)


def decay_factors(rate_row, rows):
    pos = lax.broadcasted_iota(jnp.int32, (rows, rate_row.shape[1]), 0).astype(f32)
    mid = 0.5 * rows
    q_fac = jnp.exp(-rate_row * (pos - mid))
    k_fac = jnp.exp(rate_row * (pos - mid))
    rise = jnp.exp(-rate_row * (pos + 1.0))
    tail = jnp.exp(-rate_row * (rows - 1.0 - pos))
    whole = jnp.exp(-rate_row * rows)
    return pos, mid, q_fac, k_fac, rise, tail, whole


def h3_kernel(q_ref, ks_ref, v_ref, sin_ref, rate_ref, segc_ref, segr_ref, entry_ref, y_ref, save_ref):
    rows, channels = q_ref.shape
    blocks = rows // CHUNK
    _, _, q_fac, k_fac, rise, tail, whole = decay_factors(rate_ref[...], CHUNK)
    heads = head_masks(CHUNK, channels)
    block_diag = same_head(channels)
    causal = lax.broadcasted_iota(jnp.int32, (CHUNK, CHUNK), 0) >= lax.broadcasted_iota(
        jnp.int32, (CHUNK, CHUNK), 1
    )
    state = sin_ref[...]
    for b in range(blocks):
        sl = slice(b * CHUNK, (b + 1) * CHUNK)
        seg_c = segc_ref[sl, :]
        seg_r = segr_ref[:, sl]
        before = entry_ref[...] if b == 0 else segc_ref[b * CHUNK - 1 : b * CHUNK, :]
        last = segc_ref[(b + 1) * CHUNK - 1 : (b + 1) * CHUNK, :]
        carried = (seg_c == before).astype(f32)
        final = (seg_c == last).astype(f32)
        keep = (last == before).astype(f32)
        q = q_ref[sl, :].astype(f32) * scale
        k = ks_ref[sl, :]
        v = v_ref[sl, :]
        qf = (q * q_fac).astype(bf16)
        kf = (k * k_fac).astype(bf16)
        qr = (q * (rise * carried)).astype(bf16)
        kt = (k * (tail * final)).astype(bf16)
        allowed = causal & (seg_c == seg_r)
        save_ref[b, :, :] = state
        y = nt(qr, state.astype(bf16))
        for hm in heads:
            scores = nt(jnp.where(hm, qf, jnp.zeros_like(qf)), kf)
            scores = jnp.where(allowed, scores, 0.0).astype(bf16)
            y = y + jnp.where(hm, nn(scores, v), 0.0)
        y_ref[sl, :] = y.astype(bf16)
        state = state * (whole * keep) + jnp.where(block_diag, tn(v, kt), 0.0)


def h3_forward_call(q, ks, v, state_in, rate_row, seg_col, seg_row, entry):
    rows, channels = q.shape
    return call(
        h3_kernel,
        [((rows, channels), bf16), ((rows // CHUNK, channels, channels), f32)],
        n_in=8,
        flops=3e9,
        nbytes=3e6,
    )(q, ks, v, state_in, rate_row, seg_col, seg_row, entry)


def h3_back_kernel(
    taps_n,
    q_ref,
    ks_ref,
    v_ref,
    dy_ref,
    save_ref,
    dst_ref,
    rate_ref,
    segc_ref,
    segr_ref,
    entry_ref,
    key_ref,
    halo_ref,
    taps_ref,
    age_ref,
    rem_ref,
    dq_ref,
    dk_ref,
    dv_ref,
    dtaps_ref,
    drate_ref,
    ext,
    copies,
    dext,
    dcopies,
    tap_acc,
):
    rows, channels = q_ref.shape
    blocks = rows // CHUNK
    pos, mid, q_fac, k_fac, rise, tail, whole = decay_factors(rate_ref[...], CHUNK)
    heads = head_masks(CHUNK, channels)
    block_diag = same_head(channels)
    row = lax.broadcasted_iota(jnp.int32, (CHUNK, CHUNK), 0)
    lane = lax.broadcasted_iota(jnp.int32, (CHUNK, CHUNK), 1)
    dstate = dst_ref[...]
    drate = jnp.zeros((1, channels), f32)
    dext[0:taps_n, :] = jnp.zeros((taps_n, channels), f32)
    dext[rows + taps_n : rows + 2 * taps_n, :] = jnp.zeros((taps_n, channels), f32)
    for b in reversed(range(blocks)):
        sl = slice(b * CHUNK, (b + 1) * CHUNK)
        seg_c = segc_ref[sl, :]
        seg_r = segr_ref[:, sl]
        before = entry_ref[...] if b == 0 else segc_ref[b * CHUNK - 1 : b * CHUNK, :]
        last = segc_ref[(b + 1) * CHUNK - 1 : (b + 1) * CHUNK, :]
        carried = (seg_c == before).astype(f32)
        final = (seg_c == last).astype(f32)
        keep = (last == before).astype(f32)
        q = q_ref[sl, :].astype(f32) * scale
        k = ks_ref[sl, :]
        v = v_ref[sl, :]
        dy = dy_ref[sl, :].astype(bf16)
        qf = (q * q_fac).astype(bf16)
        kf = (k * k_fac).astype(bf16)
        rise_c = rise * carried
        tail_c = tail * final
        qr = (q * rise_c).astype(bf16)
        kt = (k * tail_c).astype(bf16)
        same = seg_c == seg_r
        low_mask = (row >= lane) & same
        up_mask = (row <= lane) & same
        state = save_ref[b, :, :]
        dstate_b = dstate.astype(bf16)
        dqf = jnp.zeros((CHUNK, channels), f32)
        dkf = jnp.zeros((CHUNK, channels), f32)
        dv = nt(kt, dstate_b)
        zero = jnp.zeros_like(qf)
        for hm in heads:
            kh = jnp.where(hm, kf, zero)
            vh = jnp.where(hm, v, zero)
            scores_t = jnp.where(up_mask, nt(kh, qf), 0.0).astype(bf16)
            dv = dv + jnp.where(hm, nn(scores_t, dy), 0.0)
            dsc = jnp.where(low_mask, nt(dy, vh), 0.0).astype(bf16)
            dsc_t = jnp.where(up_mask, nt(vh, dy), 0.0).astype(bf16)
            dqf = dqf + nn(dsc, kh)
            dkf = dkf + jnp.where(hm, nn(dsc_t, qf), 0.0)
        dqr = nn(dy, state.astype(bf16))
        dkt = nn(v, dstate_b)
        dq_ref[sl, :] = ((dqf * q_fac + dqr * rise_c) * scale).astype(bf16)
        dv_ref[sl, :] = dv.astype(bf16)
        dext[taps_n + b * CHUNK : taps_n + (b + 1) * CHUNK, :] = dkf * k_fac + dkt * tail_c
        part = (pos - mid) * (qf.astype(f32) * dqf - kf.astype(f32) * dkf)
        part = part + (pos + 1.0) * (qr.astype(f32) * dqr)
        part = part + (CHUNK - 1.0 - pos) * (kt.astype(f32) * dkt)
        drate = drate + jnp.sum(part, axis=0, keepdims=True)
        held = dstate * (whole * keep)
        drate = drate + CHUNK * jnp.sum(state * held, axis=0, keepdims=True)
        dstate = held + jnp.where(block_diag, tn(dy, qr), 0.0)
    drate_ref[...] = -drate

    total = rows + taps_n
    ext[0:taps_n, :] = halo_ref[...].astype(f32)
    ext[taps_n:total, :] = key_ref[...].astype(f32)
    rolled_down(ext, copies, total)
    for r in range(8):
        dcopies[r, 0 : total + taps_n - 8, :] = dext[r : total + taps_n - 8 + r, :]
    tap_acc[...] = jnp.zeros(tap_acc.shape, f32)

    def block(b, carry):
        start = pl.multiple_of(b * 64, 64)
        rem = rem_ref[pl.ds(start, 64), :]
        acc = jnp.zeros((64, channels), f32)
        for m in range(taps_n // 8):
            for r in range(8):
                j = 8 * m + r
                moved = dcopies[r, pl.ds(start + 8 * m, 64), :]
                acc = acc + jnp.where(rem >= j, moved, 0.0) * taps_ref[j : j + 1, :]
        dk_ref[pl.ds(start, 64), :] = acc
        return carry

    lax.fori_loop(0, total // 64, block, 0)

    def tap_block(b, carry):
        start = pl.multiple_of(b * 64, 64)
        age = age_ref[pl.ds(start, 64), :]
        grad = dext[pl.ds(start + taps_n, 64), :]
        for m in range(taps_n // 8):
            for r in range(8):
                j = 8 * m + r
                moved = copies[r, pl.ds(start + taps_n - 8 * m, 64), :]
                term = jnp.where(age >= j, moved, 0.0) * grad
                tap_acc[j, :, :] += jnp.sum(term.reshape(8, 8, channels), axis=0)
        return carry

    lax.fori_loop(0, rows // 64, tap_block, 0)
    dtaps_ref[...] = jnp.sum(tap_acc[...], axis=1)


def h3_back_call(q, ks, v, dy, save, dstate, rate_row, seg_col, seg_row, entry, key, halo, taps, age, rem):
    rows, channels = q.shape
    taps_n = taps.shape[0]
    total = rows + taps_n
    return call(
        functools.partial(h3_back_kernel, taps_n),
        [
            ((rows, channels), bf16),
            ((total, channels), f32),
            ((rows, channels), bf16),
            ((taps_n, channels), f32),
            ((1, channels), f32),
        ],
        [
            pltpu.VMEM((total, channels), f32),
            pltpu.VMEM((8, total, channels), f32),
            pltpu.VMEM((total + taps_n, channels), f32),
            pltpu.VMEM((8, total + taps_n, channels), f32),
            pltpu.VMEM((taps_n, 8, channels), f32),
        ],
        n_in=15,
        flops=20e9,
        nbytes=6e6,
    )(q, ks, v, dy, save, dstate, rate_row, seg_col, seg_row, entry, key, halo, taps, age, rem)


def attend_kernel(lim_ref, q_ref, k_ref, v_ref, segc_ref, segr_ref, o_ref, stat_ref):
    rows, channels = q_ref.shape
    n_heads = channels // HEAD_DIM
    heads = head_masks(CHUNK, channels)
    row = lax.broadcasted_iota(jnp.int32, (CHUNK, CHUNK), 0)
    lane = lax.broadcasted_iota(jnp.int32, (CHUNK, CHUNK), 1)
    stat_lane = lax.broadcasted_iota(jnp.int32, (CHUNK, 128), 1)
    for b in range(rows // CHUNK):
        sl = slice(b * CHUNK, (b + 1) * CHUNK)
        low, high = lim_ref[0, b], lim_ref[1, b]
        q = q_ref[sl, :]
        seg_c = segc_ref[sl, :]
        qh = [jnp.where(hm, q, jnp.zeros_like(q)) for hm in heads]

        def step(t, carry):
            at = pl.multiple_of(t * CHUNK, CHUNK)
            keys = k_ref[pl.ds(at, CHUNK), :]
            values = v_ref[pl.ds(at, CHUNK), :]
            seg_r = segr_ref[t]
            allowed = (row >= lane + (t - high) * CHUNK) & (seg_c == seg_r)
            new = []
            for h in range(n_heads):
                top, total, acc = carry[h]
                z = jnp.where(allowed, nt(qh[h], keys) * scale, masked_low)
                new_top = jnp.maximum(top, jnp.max(z, axis=1, keepdims=True))
                shrink = jnp.exp(top - new_top)
                e = jnp.where(allowed, jnp.exp(z - new_top), 0.0)
                total = total * shrink + jnp.sum(e, axis=1, keepdims=True)
                acc = acc * shrink + nn(e.astype(bf16), values)
                new.append((new_top, total, acc))
            return tuple(new)

        start = tuple(
            (
                jnp.full((CHUNK, 1), masked_low, f32),
                jnp.zeros((CHUNK, 1), f32),
                jnp.zeros((CHUNK, channels), f32),
            )
            for _ in range(n_heads)
        )
        state = lax.fori_loop(low, high + 1, step, start)
        out = jnp.zeros((CHUNK, channels), f32)
        stats = jnp.zeros((CHUNK, 128), f32)
        for h in range(n_heads):
            top, total, acc = state[h]
            out = out + jnp.where(heads[h], acc / total, 0.0)
            stats = jnp.where(stat_lane == h, top, stats)
            stats = jnp.where(stat_lane == 8 + h, total, stats)
        o_ref[sl, :] = out
        stat_ref[b, :, :] = stats.T[0:16, :]


def attend_call(lim, q, k, v, seg_col, seg_tiles):
    rows, channels = q.shape
    return call(
        attend_kernel,
        [((rows, channels), f32), ((rows // CHUNK, 16, CHUNK), f32)],
        smem=1,
        n_in=5,
        flops=10e9,
        nbytes=4e6,
    )(lim, q, k, v, seg_col, seg_tiles)


def attend_back_kernel(
    lim_ref, q_ref, k_ref, v_ref, do_ref, o_ref, stat_ref, segc_ref, segr_ref, dq_ref, dkv_ref
):
    rows, channels = q_ref.shape
    n_heads = channels // HEAD_DIM
    heads = head_masks(CHUNK, channels)
    row = lax.broadcasted_iota(jnp.int32, (CHUNK, CHUNK), 0)
    lane = lax.broadcasted_iota(jnp.int32, (CHUNK, CHUNK), 1)
    stat_lane = lax.broadcasted_iota(jnp.int32, (CHUNK, 128), 1)
    dkv_ref[...] = jnp.zeros(dkv_ref.shape, f32)
    for b in range(rows // CHUNK):
        sl = slice(b * CHUNK, (b + 1) * CHUNK)
        low, high = lim_ref[0, b], lim_ref[1, b]
        q = q_ref[sl, :]
        do = do_ref[sl, :].astype(f32)
        o = o_ref[sl, :]
        seg_q = segr_ref[high]
        zero = jnp.zeros_like(q)
        qh = [jnp.where(hm, q, zero) for hm in heads]
        cols = jnp.zeros((CHUNK, 128), f32)
        for h in range(n_heads):
            inner = jnp.sum(jnp.where(heads[h], do * o, 0.0), axis=1, keepdims=True)
            cols = jnp.where(stat_lane == h, inner, cols)
        inner_rows = cols.T
        totals = stat_ref[b, 8:16, :]
        inv_cols = jnp.concatenate([1.0 / jnp.maximum(totals, 1e-30), jnp.zeros((120, CHUNK), f32)]).T
        wh = []
        for h in range(n_heads):
            inv = inv_cols[:, h : h + 1]
            wh.append(jnp.where(heads[h], do * inv, 0.0).astype(bf16))

        def step(t, dq):
            at = pl.multiple_of(t * CHUNK, CHUNK)
            keys = k_ref[pl.ds(at, CHUNK), :]
            values = v_ref[pl.ds(at, CHUNK), :]
            seg_k = segc_ref[pl.ds(at, CHUNK), :]
            allowed = (lane >= row + (t - high) * CHUNK) & (seg_k == seg_q)
            dk = jnp.zeros((CHUNK, channels), f32)
            dv = jnp.zeros((CHUNK, channels), f32)
            for h in range(n_heads):
                top = stat_ref[b, h : h + 1, :]
                total = stat_ref[b, 8 + h : 9 + h, :]
                z = jnp.where(allowed, nt(keys, qh[h]) * scale, masked_low)
                e = jnp.where(allowed, jnp.exp(z - top), 0.0)
                dp = nt(values, wh[h])
                dz = (e * (dp - inner_rows[h : h + 1, :] / total)).astype(bf16)
                dk = dk + nn(dz, qh[h])
                dv = dv + nn(e.astype(bf16), wh[h])
                dq = dq + jnp.where(heads[h], tn(dz, keys), 0.0)
            dkv_ref[pl.ds(at, CHUNK), 0:channels] += dk * scale
            dkv_ref[pl.ds(at, CHUNK), channels : 2 * channels] += dv
            return dq

        dq = lax.fori_loop(low, high + 1, step, jnp.zeros((CHUNK, channels), f32))
        dq_ref[sl, :] = (dq * scale).astype(bf16)


def attend_back_call(lim, q, k, v, do, o, stats, seg_keys_col, seg_tiles):
    rows, channels = q.shape
    return call(
        attend_back_kernel,
        [((rows, channels), bf16), ((k.shape[0], 2 * channels), f32)],
        smem=1,
        n_in=8,
        flops=20e9,
        nbytes=8e6,
    )(lim, q, k, v, do, o, stats, seg_keys_col, seg_tiles)


def at_rows(value, start, count):
    return lax.dynamic_slice_in_dim(value, start, count, 0)


def chain_join(earlier, later):
    return (later[0] * earlier[0], later[1] + later[0] * earlier[1])


class Rows:
    def __init__(self):
        self.blocks = lax.axis_size("ctx")
        self.place = lax.axis_index("ctx")

    def enter(self, rows):
        return rows

    def enter_ids(self, ids):
        return ids

    def leave(self, rows):
        return rows

    def leave_grad(self, rows):
        return rows

    def spread(self, rows, ordered):
        return rows

    def total(self, partial, ordered):
        return lax.psum(partial.astype(bf16), "tp").astype(f32)

    def local(self, value):
        return value

    def weights(self, proj_in, proj_out, proj_up, proj_down):
        return (
            lax.all_gather(proj_in, "fsdp", axis=1, tiled=True),
            lax.all_gather(proj_out, "fsdp", axis=1, tiled=True),
            lax.all_gather(proj_up, "fsdp", axis=0, tiled=True),
            lax.all_gather(proj_down, "fsdp", axis=1, tiled=True),
        )

    def from_previous(self, value):
        n = self.blocks
        return lax.ppermute(value, "ctx", [(i, i + 1) for i in range(n - 1)])

    def to_previous(self, value):
        n = self.blocks
        return lax.ppermute(value, "ctx", [(i + 1, i) for i in range(n - 1)])

    def state_before(self, factor, state):
        if self.blocks == 2:
            return self.from_previous(state.astype(bf16)).astype(f32)
        factors = lax.all_gather(factor.astype(bf16), "ctx").astype(f32)
        states = lax.all_gather(state.astype(bf16), "ctx")

        def one(hop, held):
            return states[hop].astype(f32) + factors[hop] * held

        return lax.fori_loop(0, self.place, one, jnp.zeros_like(state))

    def grad_after(self, factor, dstate):
        if self.blocks == 2:
            return self.to_previous(dstate.astype(bf16)).astype(f32)
        factors = lax.all_gather(factor.astype(bf16), "ctx").astype(f32)
        states = lax.all_gather(dstate.astype(bf16), "ctx")

        def one(hop, held):
            at = self.blocks - 1 - hop
            return states[at].astype(f32) + factors[at] * held

        return lax.fori_loop(0, self.blocks - 1 - self.place, one, jnp.zeros_like(dstate))

    def keys(self, key, value, ids):
        if self.blocks == 2:
            before = self.from_previous(jnp.concatenate([key, value], axis=1))
            ids_before = self.from_previous(ids.astype(bf16)).astype(jnp.int32)
            channels = key.shape[1]
            return (
                jnp.concatenate([before[:, :channels], key]),
                jnp.concatenate([before[:, channels:], value]),
                jnp.concatenate([ids_before, ids]),
                jnp.int32(key.shape[0]),
            )
        return (
            lax.all_gather(key, "ctx", axis=0, tiled=True),
            lax.all_gather(value, "ctx", axis=0, tiled=True),
            lax.all_gather(ids.astype(bf16), "ctx", axis=0, tiled=True).astype(jnp.int32),
            self.place * key.shape[0],
        )

    def key_grads(self, grads):
        if self.blocks == 2:
            rows = grads.shape[0] // 2
            return grads[rows:] + self.to_previous(grads[:rows].astype(bf16)).astype(f32)
        return lax.psum_scatter(
            grads.astype(bf16), "ctx", scatter_dimension=0, tiled=True
        ).astype(f32)

    def reduce(self, value, dim):
        value = lax.psum_scatter(value.astype(bf16), "fsdp", scatter_dimension=dim, tiled=True)
        return lax.psum(value, "ctx").astype(f32)

    def weight_grads(self, proj_in, proj_out, proj_up, proj_down):
        return (
            self.reduce(proj_in, 1),
            self.reduce(proj_out, 1),
            self.reduce(proj_up, 0),
            self.reduce(proj_down, 1),
        )

    def mixer_grads(self, taps, rate):
        return self.reduce(taps, 0), self.reduce(rate, 1)

    def gain_grads(self, rows):
        return self.reduce(rows, 1)


def norm_parts(rows):
    center = jnp.mean(rows, axis=-1, keepdims=True)
    shifted = rows - center
    spread = jnp.mean(shifted * shifted, axis=-1, keepdims=True)
    return center, lax.rsqrt(spread + epsilon)


def norm(rows, gain):
    center, inv = norm_parts(rows)
    return ((rows - center) * inv * gain).astype(bf16), (center, inv)


def norm_back(rows, kept, gain, grad):
    center, inv = kept
    unit = (rows - center) * inv
    dunit = grad * gain
    mean_d = jnp.mean(dunit, axis=-1, keepdims=True)
    mean_du = jnp.mean(dunit * unit, axis=-1, keepdims=True)
    return inv * (dunit - mean_d - unit * mean_du), jnp.sum(grad * unit, axis=0)


def gelu_tanh(values):
    return jax.nn.gelu(values, approximate=True)


def dot_nn(a, b):
    return jnp.dot(a, b, preferred_element_type=f32)


def dot_nt(a, b):
    return jnp.einsum("tf,df->td", a, b, preferred_element_type=f32)


def dot_tn(a, b):
    return jnp.einsum("tf,td->fd", a, b, preferred_element_type=f32)


def feed_forward(normed, proj_up, proj_down):
    up = dot_nn(normed, proj_up)
    hidden = gelu_tanh(up).astype(bf16)
    return dot_nn(hidden, proj_down), up, hidden


def feed_back(normed, up, hidden, grad_bf, proj_up, proj_down):
    down_grad = dot_tn(hidden, grad_bf)
    dhidden = dot_nt(grad_bf, proj_down)
    dup = jax.vjp(gelu_tanh, up)[1](dhidden)[0].astype(bf16)
    return dot_nt(dup, proj_up), dot_tn(normed, dup), down_grad


def project(normed, proj_in):
    return [dot_nn(normed, proj_in[j]).astype(bf16) for j in range(3)]


def project_back(normed, grads, proj_in):
    dnormed = sum(dot_nt(grads[j], proj_in[j]) for j in range(3))
    return dnormed, jnp.stack([dot_tn(normed, grads[j]) for j in range(3)])


def expand_state(small):
    channels = small.shape[1]
    return jnp.where(same_head(channels), jnp.tile(small, (channels // HEAD_DIM, 1)), 0.0)


def compact_state(state):
    channels = state.shape[1]
    return jnp.sum(state.reshape(channels // HEAD_DIM, HEAD_DIM, channels), axis=0)


def mixer_setup(ids, halo_ids, taps_n, rate_row):
    rows, channels = ids.shape[0], rate_row.shape[1]
    ext = jnp.concatenate([halo_ids, ids])
    at = jnp.arange(rows + taps_n, dtype=jnp.int32)
    same = ext[:, None] == ext[None, :]
    age = jnp.sum((same & (at[None, :] < at[:, None])).astype(jnp.int32), axis=1)[taps_n:]
    rem = jnp.sum((same & (at[None, :] > at[:, None])).astype(jnp.int32), axis=1)
    entry, last = halo_ids[taps_n - 1], ids[rows - 1]
    pos = jnp.arange(rows, dtype=f32)[:, None]
    tail = jnp.exp(-rate_row * (rows - 1.0 - pos)) * (ids == last).astype(f32)[:, None]
    rise = jnp.exp(-rate_row * (pos + 1.0)) * (ids == entry).astype(f32)[:, None]
    factor = jnp.exp(-rate_row * rows) * (entry == last).astype(f32)
    return (
        jnp.broadcast_to(age[:, None], (rows, channels)),
        jnp.broadcast_to(rem[:, None], (rows + taps_n, channels)),
        tail,
        rise,
        factor,
        entry.reshape(1, 1),
    )


def run(plan, inputs, cotangent, segments, gains, last_gain, in_weight, h3_out, attn_out, up_weight, down_weight, shift_taps, decay_rate):
    x0 = plan.enter(inputs[0]).astype(f32)
    grad = plan.enter(cotangent[0]).astype(f32)
    ids = plan.enter_ids(segments[0] + 1)
    taps, rate = plan.local(shift_taps), plan.local(decay_rate)
    in0, out0, up0, down0 = plan.weights(in_weight[0], h3_out, up_weight[0], down_weight[0])
    in1, out1, up1, down1 = plan.weights(in_weight[1], attn_out, up_weight[1], down_weight[1])
    taps_n = taps.shape[0]
    rows = ids.shape[0]
    rate_row = rate.reshape(1, -1)
    halo_ids = plan.from_previous(ids[rows - taps_n :].astype(bf16)).astype(jnp.int32)
    age, rem, tail, rise, factor, entry = mixer_setup(ids, halo_ids, taps_n, rate_row)
    seg_col, seg_row = ids[:, None], ids[None, :]

    n0, kept0 = norm(x0, gains[0])
    n0 = plan.spread(n0, True)
    q0, k0, v0 = project(n0, in0)
    halo = plan.from_previous(k0[rows - taps_n :])
    ks, state_end = shift_forward(k0, halo, taps, age, tail, v0)
    state_in = expand_state(plan.state_before(factor, compact_state(state_end)))
    y0, saved = h3_forward_call(q0, ks, v0, state_in, rate_row, seg_col, seg_row, entry)
    x1 = x0 + plan.total(dot_nn(y0, out0), True)
    m0, kept1 = norm(x1, gains[1])
    m0 = plan.spread(m0, False)
    part, u0, r0 = feed_forward(m0, up0, down0)
    x2 = x1 + plan.total(part, False)

    n2, kept2 = norm(x2, gains[2])
    n2 = plan.spread(n2, True)
    q2, k2, v2 = project(n2, in1)
    keys, values, key_ids, offset = plan.keys(k2, v2, ids)
    tiles = jnp.arange(rows // CHUNK, dtype=jnp.int32)
    firsts = ids[:: CHUNK]
    limits = jnp.stack(
        [
            jnp.sum((key_ids[None, :] < firsts[:, None]).astype(jnp.int32), axis=1) // CHUNK,
            offset // CHUNK + tiles,
        ]
    )
    seg_tiles = key_ids.reshape(-1, 1, CHUNK)
    mixed, stats = attend_call(limits, q2, keys, values, seg_col, seg_tiles)
    mixed_bf = mixed.astype(bf16)
    x3 = x2 + plan.total(dot_nn(mixed_bf, out1), True)
    m1, kept3 = norm(x3, last_gain)
    m1 = plan.spread(m1, False)
    part, u1, r1 = feed_forward(m1, up1, down1)
    x4 = x3 + plan.total(part, False)
    output = plan.leave(x4.astype(bf16))

    grad_bf = plan.spread(grad.astype(bf16), False)
    part, up1_grad, down1_grad = feed_back(m1, u1, r1, grad_bf, up1, down1)
    dres, gain3 = norm_back(x3, kept3, last_gain, plan.total(part, False))
    grad = grad + dres
    grad_bf = plan.spread(grad.astype(bf16), True)
    out1_grad = dot_tn(mixed_bf, grad_bf)
    dmixed = dot_nt(grad_bf, out1).astype(bf16)
    dq, dkv = attend_back_call(
        limits, q2, keys, values, dmixed, mixed, stats, key_ids[:, None], seg_tiles
    )
    dkv = plan.key_grads(dkv).astype(bf16)
    channels = dq.shape[1]
    part, in1_grad = project_back(n2, (dq, dkv[:, :channels], dkv[:, channels:]), in1)
    dres, gain2 = norm_back(x2, kept2, gains[2], plan.total(part, True))
    grad = grad + dres
    second = plan.weight_grads(in1_grad, out1_grad, up1_grad, down1_grad)

    grad_bf = plan.spread(grad.astype(bf16), False)
    part, up0_grad, down0_grad = feed_back(m0, u0, r0, grad_bf, up0, down0)
    dres, gain1 = norm_back(x1, kept1, gains[1], plan.total(part, False))
    grad = grad + dres
    grad_bf = plan.spread(grad.astype(bf16), True)
    out0_grad = dot_tn(y0, grad_bf)
    dy = dot_nt(grad_bf, out0)
    dstate_in = compact_state(
        jnp.where(
            same_head(channels),
            dot_tn(dy.astype(bf16), (q0.astype(f32) * (rise * scale)).astype(bf16)),
            0.0,
        )
    )
    dstate_end = expand_state(plan.grad_after(factor, dstate_in))
    dq, dk, dv, dtaps, drate = h3_back_call(
        q0, ks, v0, dy, saved, dstate_end, rate_row, seg_col, seg_row, entry, k0, halo, taps, age, rem
    )
    halo_grad = plan.to_previous(dk[:taps_n].astype(bf16)).astype(f32)
    dk = jnp.concatenate([dk[taps_n:rows], dk[rows:] + halo_grad]).astype(bf16)
    part, in0_grad = project_back(n0, (dq, dk, dv), in0)
    dres, gain0 = norm_back(x0, kept0, gains[0], plan.total(part, True))
    input_grad = plan.leave_grad(grad + dres)
    first = plan.weight_grads(in0_grad, out0_grad, up0_grad, down0_grad)
    dtaps, drate = plan.mixer_grads(dtaps, drate.reshape(rate.shape))
    gain_rows = plan.gain_grads(jnp.stack([gain0, gain1, gain2, gain3]))
    return (
        output[None],
        input_grad[None],
        gain_rows[:3],
        gain_rows[3],
        jnp.stack([first[0], second[0]]),
        first[1],
        second[1],
        jnp.stack([first[2], second[2]]),
        jnp.stack([first[3], second[3]]),
        dtaps,
        drate,
    )


def shards(*arguments):
    return run(Rows(), *arguments)


def solution(mesh):
    placed = (
        P("fsdp", "ctx", None),
        P("fsdp", "ctx", None),
        P("fsdp", "ctx"),
        P(),
        P(),
        P(None, None, "fsdp", "tp"),
        P("tp", "fsdp"),
        P("tp", "fsdp"),
        P(None, "fsdp", "tp"),
        P(None, "tp", "fsdp"),
        P(None, "tp"),
        P("tp", None),
    )
    return jax.shard_map(
        shards,
        mesh=mesh,
        in_specs=placed,
        out_specs=(
            P("fsdp", "ctx", None),
            P("fsdp", "ctx", None),
            P(None, "fsdp"),
            P("fsdp"),
            P(None, None, "fsdp", "tp"),
            P("tp", "fsdp"),
            P("tp", "fsdp"),
            P(None, "fsdp", "tp"),
            P(None, "tp", "fsdp"),
            P("fsdp", "tp"),
            P("tp", "fsdp"),
        ),
        check_vma=False,
    )
```

time: 1170 us -> 910 us (0.78)
  local copies, waits for them, and re-layouts: 262 us -> 55.9 us
  other arithmetic: 178 us -> 59 us
  waiting for transfers between devices: 441 us -> 554 us
  Pallas kernels: 0 us -> 70.8 us
  matrix products: 130 us -> 75.4 us
  loops' own time: 40.8 us -> 0 us
  blocking collectives: 78.9 us -> 55.4 us
    reduce_scatter x3 -> x5, waiting for transfers between devices: 23.8 us -> 151 us  [reduce(): lax.psum_scatter(value.astype(bf16), 'fsdp', scatter_dimension=dim, tiled...]
    dynamic_update_slice x32 -> x0, local copies, waits for them, and re-layouts: 94.2 us -> none  [the longest x30 92.5 us: decay_blocks(): lax.scan(jax.checkpoint(one_block), start_carry, blocks_in)]
    pallas_call x0 -> x5, Pallas kernels: none -> 70.8 us  [the longest x1 26.5 us: h3_back_call(): call(functools.partial(h3_back_kernel, taps_n), [((rows, channels), bf16)...]
    dot_general x134 -> x37, matrix products: 127 us -> 75.4 us  [the longest x12 29.4 us: dot_nn(): return jnp.dot(a, b, preferred_element_type=f32)]
    unnamed x26 -> x27, waiting for transfers between devices: 67.5 us -> 20.2 us
    another operation x11 -> x0, loops' own time: 40.8 us -> none  [the longest x3 24.7 us: decay_blocks(): lax.scan(jax.checkpoint(one_block), start_carry, blocks_in)]
    add x14 -> x6, other arithmetic: 44.2 us -> 5.68 us  [the longest x3 4.4 us: run(): grad = grad + dres]
    psum x8, waiting for transfers between devices: 349 us -> 382 us  [the longest x7 382 us: total(): return lax.psum(partial.astype(bf16), 'tp').astype(f32)]
  transfers between devices with their start and end apart: 24 -> 30, of which waited for: 9 -> 14; matrix products, arithmetic and copies ran while one was open for 28% -> 12% of each run, Pallas kernels for 0% -> 0%
where the time goes in v1:
time: 910 us; the launch traced here: 903 us
  waiting for transfers between devices  554 us (61%)
  matrix products  75.4 us (8%)
  Pallas kernels  70.8 us (8%)
  other arithmetic  59 us (6%)
  local copies, waits for them, and re-layouts  55.9 us (6%)
  blocking collectives  55.4 us (6%)
  between operations  18.6 us (2%)
  starting transfers between devices  14.2 us (2%)
    psum x7, waiting for transfers between devices, total(): return lax.psum(partial.astype(bf16), 'tp').astype(f32)  382 us
    reduce_scatter x5, waiting for transfers between devices, reduce(): lax.psum_scatter(value.astype(bf16), 'fsdp', scatter_dimension=dim, tiled...  151 us
    unnamed x229, local copies, waits for them, and re-layouts  38.7 us
    dot_general x12, matrix products, dot_nn(): return jnp.dot(a, b, preferred_element_type=f32)  29.4 us
    all_gather x2, blocking collectives, weights(): lax.all_gather(proj_in, 'fsdp', axis=1, tiled=True)  26.8 us
    pallas_call x1, Pallas kernels, h3_back_call(): call(functools.partial(h3_back_kernel, taps_n), [((rows, channels), bf16)...  26.5 us
    dot_general x13, matrix products, dot_tn(): return jnp.einsum('tf,td->fd', a, b, preferred_element_type=f32)  25.9 us
    unnamed x27, waiting for transfers between devices  20.2 us
  transfers between devices with their start and end apart: 30, of which 14 were waited for; matrix products, arithmetic and copies ran while one was open for 12% of the time, Pallas kernels for 0%

profile of v1, /device:TPU:1, one launch (start us, length us, event | category | flops | bytes accessed | tf_op | source)
XLA Modules:
  0.0 902.8 jit_solution(2996990395818206652)
XLA Ops:
  14.3 13.2 %all-gather = bf16[1,3,768,192]{3,2,1,0:T(8,128)(2,1)S(1)} all-gather(bf16[1,3,192,192]{3,2,1,0:T(8,128)(2,1)S(1)} %get-tuple-element.135), channel_id=2, replica_groups=mesh['fsdp'=4,'ctx'=2,'tp'=4] {'fsdp'}, dimensions={2}, use_global_device_ids=true | all-gather | bytes 1105920 | tf_op jit(solution)/shard_map/all_gather | solution.py:480
  39.4 10.7 %shard_map.203 = (f32[768,192]{1,0:T(8,128)}, f32[192,192]{1,0:T(8,128)}) custom-call(bf16[768,192]{1,0:T(8,128)(2,1)} %copy-done.93, bf16[64,192]{1,0:T(8,128)(2,1)} %copy-done.98, f32[64,192]{1,0:T(8,128)} %taps_ref.3, s32[768,192]{1,0:T(8,128)} %broadcast_in_dim.15.age_ref, f32[768,192]{1,0:T(8,128)} %exponential_multiply_fusion.tail_ref, ...), custom_call_target="tpu_custom_call" | custom-call | flops 754974720 | bytes 4000000 | tf_op jit(solution)/shard_map/pallas_call | solution.py:88
  52.4 8.0 all_gather.25
  62.9 4.7 shard_map.204
  67.5 2.6 convolution_convert_fusion.9
  72.3 57.7 %all-reduce.13.cloned.1.call-done = bf16[768,768]{1,0:T(8,128)(2,1)} async-done(((bf16[768,768]{1,0:T(8,128)(2,1)}), bf16[768,768]{1,0:T(8,128)(2,1)}) %all-reduce.13.cloned.1.call-update) | async-done | bytes 1179664 | tf_op jit(solution)/shard_map/psum | solution.py:473
  132.9 4.0 fusion.77
  136.9 4.6 convolution_convert_fusion.8
  143.5 13.7 %all-gather.3 = bf16[1,3,768,192]{3,2,1,0:T(8,128)(2,1)} all-gather(bf16[1,3,192,192]{3,2,1,0:T(8,128)(2,1)S(1)} %get-tuple-element.134), channel_id=5, replica_groups=mesh['fsdp'=4,'ctx'=2,'tp'=4] {'fsdp'}, dimensions={2}, use_global_device_ids=true | all-gather | bytes 1105920 | tf_op jit(solution)/shard_map/all_gather | solution.py:480
  157.2 8.6 all_gather.29
  166.6 30.6 %all-reduce.15.cloned.1.call-done = bf16[768,768]{1,0:T(8,128)(2,1)} async-done(((bf16[768,768]{1,0:T(8,128)(2,1)}), bf16[768,768]{1,0:T(8,128)(2,1)}) %all-reduce.15.cloned.1.call-update) | async-done | bytes 1179664 | tf_op jit(solution)/shard_map/psum | solution.py:473
  208.8 2.6 convolution_convert_fusion.12.q_ref
  214.8 12.8 %shard_map.205 = (f32[768,192]{1,0:T(8,128)}, f32[3,16,256]{2,1,0:T(8,128)}) custom-call(s32[2,3]{1,0:T(2,128)} %pad_add_fusion.3.lim_ref, bf16[768,192]{1,0:T(8,128)(2,1)} %convolution_convert_fusion.12.q_ref, bf16[1536,192]{1,0:T(8,128)(2,1)} %pad_maximum_fusion.2.k_ref, bf16[1536,192]{1,0:T(8,128)(2,1)} %pad_maximum_fusion.3.v_ref, ...), custom_call_target="tpu_custom_call" | custom-call | flops 10000000000 | bytes 4000000 | tf_op jit(solution)/shard_map/pallas_call | solution.py:365
  227.6 2.7 convolution_convert_fusion.7
  232.0 53.5 %all-reduce.17.cloned.1.call-done = bf16[768,768]{1,0:T(8,128)(2,1)} async-done(((bf16[768,768]{1,0:T(8,128)(2,1)}), bf16[768,768]{1,0:T(8,128)(2,1)}) %all-reduce.17.cloned.1.call-update) | async-done | bytes 1179664 | tf_op jit(solution)/shard_map/psum | solution.py:473
  289.5 4.6 fusion.69
  294.1 4.6 fusion.54
  303.1 54.4 %all-reduce.19.cloned.1.call-done = bf16[768,768]{1,0:T(8,128)(2,1)} async-done(((bf16[768,768]{1,0:T(8,128)(2,1)}), bf16[768,768]{1,0:T(8,128)(2,1)}) %all-reduce.19.cloned.1.call-update) | async-done | bytes 1179664 | tf_op jit(solution)/shard_map/psum | solution.py:473
  357.5 3.8 fusion.28
  361.4 2.2 fusion.26
  368.1 16.2 %shard_map.206 = (bf16[768,192]{1,0:T(8,128)(2,1)}, f32[1536,384]{1,0:T(8,128)}) custom-call(s32[2,3]{1,0:T(2,128)} %pad_add_fusion.3.lim_ref, bf16[768,192]{1,0:T(8,128)(2,1)} %convolution_convert_fusion.12.q_ref, bf16[1536,192]{1,0:T(8,128)(2,1)} %pad_maximum_fusion.2.k_ref, bf16[1536,192]{1,0:T(8,128)(2,1)} %pad_maximum_fusion.3.v_ref, ...), custom_call_target="tpu_custom_call" | custom-call | flops 20000000000 | bytes 8000000 | tf_op jit(solution)/shard_map/pallas_call | solution.py:434
  391.4 55.3 %all-reduce.21.cloned.1.call-done = bf16[768,768]{1,0:T(8,128)(2,1)} async-done(((bf16[768,768]{1,0:T(8,128)(2,1)}), bf16[768,768]{1,0:T(8,128)(2,1)}) %all-reduce.21.cloned.1.call-update) | async-done | bytes 1179664 | tf_op jit(solution)/shard_map/psum | solution.py:473
  446.7 3.1 fusion.33
  451.9 2.2 fusion.47
  457.4 55.5 %all-reduce.23.cloned.1.call-done = bf16[768,768]{1,0:T(8,128)(2,1)} async-done(((bf16[768,768]{1,0:T(8,128)(2,1)}), bf16[768,768]{1,0:T(8,128)(2,1)}) %all-reduce.23.cloned.1.call-update) | async-done | bytes 1179664 | tf_op jit(solution)/shard_map/psum | solution.py:473
  512.9 3.3 fusion.38
  519.4 2.6 collective-permute-start.6
  521.9 4.5 convolution_convert_fusion.6
  529.5 26.5 %shard_map.207 = (bf16[768,192]{1,0:T(8,128)(2,1)}, f32[832,192]{1,0:T(8,128)}, bf16[768,192]{1,0:T(8,128)(2,1)}, f32[64,192]{1,0:T(8,128)}, f32[1,192]{1,0:T(1,128)}) custom-call(bf16[768,192]{1,0:T(8,128)(2,1)} %convolution_convert_fusion.15.q_ref, f32[768,192]{1,0:T(8,128)} %get-tuple-element.24.ks_ref, ...), custom_call_target="tpu_custom_call" | custom-call | flops 20000000000 | bytes 6000000 | tf_op jit(solution)/shard_map/pallas_call | solution.py:289
  565.0 2.3 convolution_convert_fusion.16
  572.6 2.2 copy.105
  574.8 4.3 reshape.334
  583.3 75.2 %all-reduce.25.cloned.1.call-done = (bf16[768,768]{1,0:T(8,128)(2,1)}, bf16[768,768]{1,0:T(8,128)(2,1)}) async-done(((bf16[768,768]{1,0:T(8,128)(2,1)}, bf16[768,768]{1,0:T(8,128)(2,1)}), (bf16[768,768]{1,0:T(8,128)(2,1)}, bf16[768,768]{1,0:T(8,128)(2,1)})) %all-reduce.25.cloned.1.call-update) | async-done | bytes 2359312 | tf_op jit(solution)/shard_map/psum | solution.py:473
  658.5 3.2 fusion.40
  665.4 2.2 copy.103
  667.6 4.3 reshape.332
  672.0 3.6 convolution_convert_fusion.2
  675.7 4.4 convolution_convert_fusion
  680.2 4.1 convolution_convert_fusion.3
  684.7 4.7 convolution_convert_fusion.1
  700.3 29.8 %reduce-scatter.24.cloned.1.call-done = bf16[192,768]{1,0:T(8,128)(2,1)} async-done(((bf16[768,768]{1,0:T(8,128)(2,1)}), bf16[192,768]{1,0:T(8,128)(2,1)}) %reduce-scatter.24.cloned.1.call-update) | async-done | bytes 294928 | tf_op jit(solution)/shard_map/reduce_scatter | solution.py:544
  730.1 32.0 %reduce-scatter.28.cloned.1.call-done = bf16[768,192]{0,1:T(8,128)(2,1)} async-done(((bf16[768,768]{0,1:T(8,128)(2,1)}), bf16[768,192]{0,1:T(8,128)(2,1)}) %reduce-scatter.28.cloned.1.call-update) | async-done | bytes 294928 | tf_op jit(solution)/shard_map/reduce_scatter | solution.py:544
  762.1 31.9 %reduce-scatter.22.cloned.1.call-done = bf16[192,768]{1,0:T(8,128)(2,1)} async-done(((bf16[768,768]{1,0:T(8,128)(2,1)}), bf16[192,768]{1,0:T(8,128)(2,1)}) %reduce-scatter.22.cloned.1.call-update) | async-done | bytes 294928 | tf_op jit(solution)/shard_map/reduce_scatter | solution.py:544
  794.0 32.0 %reduce-scatter.26.cloned.1.call-done = bf16[768,192]{0,1:T(8,128)(2,1)} async-done(((bf16[768,768]{0,1:T(8,128)(2,1)}), bf16[768,192]{0,1:T(8,128)(2,1)}) %reduce-scatter.26.cloned.1.call-update) | async-done | bytes 294928 | tf_op jit(solution)/shard_map/reduce_scatter | solution.py:544
  827.4 6.9 all-reduce
  835.6 17.2 %reduce-scatter.32.cloned.1.call-done = bf16[192,4]{1,0:T(8,128)(2,1)} async-done(((bf16[768,4]{1,0:T(8,128)(2,1)}), bf16[192,4]{1,0:T(8,128)(2,1)}) %reduce-scatter.32.cloned.1.call-update) | async-done | bytes 1552
  853.7 25.5 %reduce-scatter.30.cloned.1.call-done = bf16[16,192]{1,0:T(8,128)(2,1)} async-done(((bf16[64,192]{1,0:T(8,128)(2,1)}), bf16[16,192]{1,0:T(8,128)(2,1)}) %reduce-scatter.30.cloned.1.call-update) | async-done | bytes 6160 | tf_op jit(solution)/shard_map/reduce_scatter | solution.py:544
  879.2 5.0 all-reduce.2
  (419 shorter events, 125.1 us)
Async XLA Ops:
  8.0 122.0 %all-reduce.13.cloned.1.call-start = ((), (), s32[]{:S(2)}) async-start(), calls=%async_computation.10 | async-start | bytes 2359296 | tf_op jit(solution)/shard_map/psum | solution.py:473
  8.9 24.3 %collective-permute-start.1 = (bf16[64]{0:T(256)(128)(2,1)S(1)}, bf16[64]{0:T(256)(128)(2,1)S(1)}, u32[]{:S(2)}, u32[]{:S(2)}) collective-permute-start(bf16[64]{0:T(256)(128)(2,1)S(1)} %fusion.108), channel_id=1, source_target_pairs={{0,4},{1,5},{2,6},{3,7},{8,12},{9,13},{10,14},{11,15},{16,20},{17,... | collective-permute-start | bytes 392 | tf_op jit(solution)/shard_map/ppermute | solution.py:488
  14.3 118.1 %copy-start.68 = (f32[768]{0:T(1024)}, f32[768]{0:T(1024)S(1)}, u32[]{:S(2)}) copy-start(f32[768]{0:T(1024)S(1)} %get-tuple-element.106) | copy-start | bytes 9220
  28.5 9.8 %collective-permute-start = (bf16[64,192]{1,0:T(8,128)(2,1)S(1)}, bf16[64,192]{1,0:T(8,128)(2,1)S(1)}, u32[]{:S(2)}, u32[]{:S(2)}) collective-permute-start(bf16[64,192]{1,0:T(8,128)(2,1)S(1)} %slice.151), channel_id=1, source_target_pairs={{0,4},{1,5},{2,6},{3,7},{8,12},{9,13},{10,14},{11,15},{16,20},{17,... | collective-permute-start | bytes 73736 | tf_op jit(solution)/shard_map/ppermute | solution.py:488
  29.9 32.1 %copy-start.81 = (pred[192]{0:T(512)(128)(4,1)}, pred[192]{0:T(512)(128)(4,1)S(1)}, u32[]{:S(2)}) copy-start(pred[192]{0:T(512)(128)(4,1)S(1)} %compare_and_fusion.2) | copy-start | bytes 580
  29.9 32.1 %copy-start.74 = (s32[192]{0:T(256)}, s32[192]{0:T(256)S(1)}, u32[]{:S(2)}) copy-start(s32[192]{0:T(256)S(1)} %get-tuple-element.141) | copy-start | bytes 2308
  30.0 32.1 %copy-start.76 = (s32[192]{0:T(256)}, s32[192]{0:T(256)S(1)}, u32[]{:S(2)}) copy-start(s32[192]{0:T(256)S(1)} %get-tuple-element.142) | copy-start | bytes 2308
  51.1 10.9 %collective-permute-start.2 = (bf16[64,192]{1,0:T(8,128)(2,1)S(1)}, bf16[64,192]{1,0:T(8,128)(2,1)S(1)}, u32[]{:S(2)}, u32[]{:S(2)}) collective-permute-start(bf16[64,192]{1,0:T(8,128)(2,1)S(1)} %reduce_sum.230), channel_id=1, source_target_pairs={{0,4},{1,5},{2,6},{3,7},{8,12},{9,13},{10,14},{11,15},{16,20},{17,... | collective-permute-start | bytes 73736 | tf_op jit(solution)/shard_map/ppermute | solution.py:488
  70.2 62.2 %all-gather.11.cloned.1.call-start = ((), (), s32[]{:S(2)}) async-start(), calls=%async_computation.21 | async-start | bytes 1474560 | tf_op jit(solution)/shard_map/all_gather | solution.py:482
  71.1 65.8 %all-gather.13.cloned.1.call-start = ((), (), s32[]{:S(2)}) async-start(), calls=%async_computation.22 | async-start | bytes 1474560 | tf_op jit(solution)/shard_map/all_gather | solution.py:483
  72.1 125.1 %all-reduce.15.cloned.1.call-start = ((), (), s32[]{:S(2)}) async-start(), calls=%async_computation.11 | async-start | bytes 2359296 | tf_op jit(solution)/shard_map/psum | solution.py:473
  141.5 144.0 %all-reduce.17.cloned.1.call-start = ((), (), s32[]{:S(2)}) async-start(), calls=%async_computation.12 | async-start | bytes 2359296 | tf_op jit(solution)/shard_map/psum | solution.py:473
  141.6 24.3 %collective-permute-start.3 = (bf16[768]{0:T(1024)(128)(2,1)S(1)}, bf16[768]{0:T(1024)(128)(2,1)S(1)}, u32[]{:S(2)}, u32[]{:S(2)}) collective-permute-start(bf16[768]{0:T(1024)(128)(2,1)S(1)} %convert_element_type.267), channel_id=1, source_target_pairs={{0,4},{1,5},{2,6},{3,7},{8,12},{9,13},{10,14},{11,15},{16,20},{17,... | collective-permute-start | bytes 4616 | tf_op jit(solution)/shard_map/ppermute | solution.py:488
  165.9 33.4 %copy-start.71 = (s32[768]{0:T(1024)}, s32[768]{0:T(1024)S(1)}, u32[]{:S(2)}) copy-start(s32[768]{0:T(1024)S(1)} %convert_element_type.268) | copy-start | bytes 9220
  203.1 8.4 collective-permute-start.4
  230.2 59.2 %all-gather.15.cloned.1.call-start = ((), (), s32[]{:S(2)}) async-start(), calls=%async_computation.23 | async-start | bytes 1474560 | tf_op jit(solution)/shard_map/all_gather | solution.py:482
  230.8 63.2 %all-gather.17.cloned.1.call-start = ((), (), s32[]{:S(2)}) async-start(), calls=%async_computation.24 | async-start | bytes 1474560 | tf_op jit(solution)/shard_map/all_gather | solution.py:483
  232.0 125.5 %all-reduce.19.cloned.1.call-start = ((), (), s32[]{:S(2)}) async-start(), calls=%async_computation.13 | async-start | bytes 2359296 | tf_op jit(solution)/shard_map/psum | solution.py:473
  301.9 144.8 %all-reduce.21.cloned.1.call-start = ((), (), s32[]{:S(2)}) async-start(), calls=%async_computation.14 | async-start | bytes 2359296 | tf_op jit(solution)/shard_map/psum | solution.py:473
  303.1 58.3 %copy-start.63 = (f32[768]{0:T(1024)S(1)}, f32[768]{0:T(1024)}, u32[]{:S(2)}) copy-start(f32[768]{0:T(1024)} %copy-done.62) | copy-start | bytes 9220
  303.1 58.3 %copy-start.72 = (f32[768]{0:T(1024)S(1)}, f32[768]{0:T(1024)}, u32[]{:S(2)}) copy-start(f32[768]{0:T(1024)} %add_rsqrt_fusion) | copy-start | bytes 9220
  385.8 3.0 collective-permute-start.5
  389.8 56.9 %copy-start.58 = (f32[768]{0:T(1024)S(1)}, f32[768]{0:T(1024)}, u32[]{:S(2)}) copy-start(f32[768]{0:T(1024)} %copy-done.57) | copy-start | bytes 9220
  389.8 56.9 %copy-start.60 = (f32[768]{0:T(1024)S(1)}, f32[768]{0:T(1024)}, u32[]{:S(2)}) copy-start(f32[768]{0:T(1024)} %get-tuple-element.104) | copy-start | bytes 9220
  391.4 121.5 %all-reduce.23.cloned.1.call-start = ((), (), s32[]{:S(2)}) async-start(), calls=%async_computation.15 | async-start | bytes 2359296 | tf_op jit(solution)/shard_map/psum | solution.py:473
  455.1 57.8 %copy-start.10 = (bf16[768,768]{1,0:T(8,128)(2,1)S(1)}, bf16[768,768]{1,0:T(8,128)(2,1)}, u32[]{:S(2)}) copy-start(bf16[768,768]{1,0:T(8,128)(2,1)} %all-reduce.13.cloned.1.call-done) | copy-start | bytes 3538948
  455.1 57.8 %copy-start.56 = (f32[768]{0:T(1024)S(1)}, f32[768]{0:T(1024)}, u32[]{:S(2)}) copy-start(f32[768]{0:T(1024)} %copy-done.55) | copy-start | bytes 9220
  455.1 57.8 %copy-start.66 = (f32[768]{0:T(1024)S(1)}, f32[768]{0:T(1024)}, u32[]{:S(2)}) copy-start(f32[768]{0:T(1024)} %copy-done.65) | copy-start | bytes 9220
  455.1 57.8 %copy-start.69 = (f32[768]{0:T(1024)S(1)}, f32[768]{0:T(1024)}, u32[]{:S(2)}) copy-start(f32[768]{0:T(1024)} %copy-done.68) | copy-start | bytes 9220
  457.3 201.2 %all-reduce.25.cloned.1.call-start = ((), (), s32[]{:S(2)}) async-start(), calls=%async_computation.30 | async-start | bytes 4718592 | tf_op jit(solution)/shard_map/psum | solution.py:473
  519.4 8.3 collective-permute-start.6
  557.2 2.9 collective-permute-start.7
  563.4 127.9 %reduce-scatter.40.cloned.1.call-start = ((), (), s32[]{:S(2)}) async-start(), calls=%async_computation.29 | async-start | bytes 491520
  569.3 123.6 %reduce-scatter.36.cloned.1.call-start = ((), (), s32[]{:S(2)}) async-start(), calls=%async_computation.27 | async-start | bytes 1228800
  579.1 79.4 %copy-start.52 = (f32[768]{0:T(1024)S(1)}, f32[768]{0:T(1024)}, u32[]{:S(2)}) copy-start(f32[768]{0:T(1024)} %copy-done.51) | copy-start | bytes 9220
  579.1 79.4 %copy-start.54 = (f32[768]{0:T(1024)S(1)}, f32[768]{0:T(1024)}, u32[]{:S(2)}) copy-start(f32[768]{0:T(1024)} %copy-done.53) | copy-start | bytes 9220
  579.1 116.0 %reduce-scatter.38.cloned.1.call-start = ((), (), s32[]{:S(2)}) async-start(), calls=%async_computation.28 | async-start | bytes 491520
  583.2 114.9 %reduce-scatter.34.cloned.1.call-start = ((), (), s32[]{:S(2)}) async-start(), calls=%async_computation.26 | async-start | bytes 1228800
  671.9 58.2 %reduce-scatter.24.cloned.1.call-start = ((), (), s32[]{:S(2)}) async-start(), calls=%async_computation.17 | async-start | bytes 1474560 | tf_op jit(solution)/shard_map/reduce_scatter | solution.py:544
  675.6 86.5 %reduce-scatter.28.cloned.1.call-start = ((), (), s32[]{:S(2)}) async-start(), calls=%async_computation.19 | async-start | bytes 1474560 | tf_op jit(solution)/shard_map/reduce_scatter | solution.py:544
  680.1 113.9 %reduce-scatter.22.cloned.1.call-start = ((), (), s32[]{:S(2)}) async-start(), calls=%async_computation.16 | async-start | bytes 1474560 | tf_op jit(solution)/shard_map/reduce_scatter | solution.py:544
  684.3 141.7 %reduce-scatter.26.cloned.1.call-start = ((), (), s32[]{:S(2)}) async-start(), calls=%async_computation.18 | async-start | bytes 1474560 | tf_op jit(solution)/shard_map/reduce_scatter | solution.py:544
  689.4 163.4 %reduce-scatter.32.cloned.1.call-start = ((), (), s32[]{:S(2)}) async-start(), calls=%async_computation.25 | async-start | bytes 245760
  690.5 188.7 %reduce-scatter.30.cloned.1.call-start = ((), (), s32[]{:S(2)}) async-start(), calls=%async_computation.20 | async-start | bytes 40960 | tf_op jit(solution)/shard_map/reduce_scatter | solution.py:544
  691.2 195.4 %all-reduce.27.cloned.1.call-start = ((), (), s32[]{:S(2)}) async-start(), calls=%async_computation.31 | async-start | bytes 3932160 | tf_op jit(solution)/shard_map/psum | solution.py:545
  692.9 133.1 %copy-start.100 = (u32[32]{0:T(128)S(1)}, u32[32]{0:T(128)}, u32[]{:S(2)}) copy-start(u32[32]{0:T(128)} %constant.121) | copy-start | bytes 388
  692.9 134.4 %copy-start.99 = (f32[1,192]{1,0:T(1,128)S(1)}, f32[1,192]{1,0:T(1,128)}, u32[]{:S(2)}) copy-start(f32[1,192]{1,0:T(1,128)} %get-tuple-element.36) | copy-start | bytes 2308
  700.3 134.1 %copy-start.39 = (bf16[768,768]{1,0:T(8,128)(2,1)S(1)}, bf16[768,768]{1,0:T(8,128)(2,1)}, u32[]{:S(2)}) copy-start(bf16[768,768]{1,0:T(8,128)(2,1)} %get-tuple-element.110) | copy-start | bytes 3538948
  (87 other events, 396.7 us)
Sparse Core Ops, SparseCore 0:
  70.3 59.6 all-reduce.12
  141.6 55.4 all-reduce.14
  230.4 55.0 all-reduce.16
  302.0 55.4 all-reduce.18
  391.5 55.1 all-reduce.20
  457.4 55.4 all-reduce.22
  563.5 94.9 all-reduce.24
  826.2 21.8 all-reduce.26
Sparse Core Ops, SparseCore 1:
  73.1 31.0 all-gather.10
  106.4 27.5 all-gather.12
  232.6 26.3 all-gather.14
  260.8 27.5 all-gather.16
  569.4 23.1 reduce-scatter.39
  595.6 27.4 reduce-scatter.35
  625.6 24.3 reduce-scatter.37
  672.0 26.1 reduce-scatter.33
  701.5 28.5 reduce-scatter.23
  733.6 28.5 reduce-scatter.27
  765.5 28.4 reduce-scatter.21
  797.5 28.5 reduce-scatter.25
  829.2 23.5 reduce-scatter.31
  855.5 23.6 reduce-scatter.29

commit v2 on v1

v2 whole, which is shorter than its diff:
```python
import functools

import jax
import jax.numpy as jnp
from jax import lax
from jax.experimental import pallas as pl
from jax.experimental.pallas import tpu as pltpu
from jax.sharding import PartitionSpec as P

HEAD_DIM = 64
epsilon = 1e-05
masked_low = -1e30
bf16 = jnp.bfloat16
f32 = jnp.float32
scale = HEAD_DIM ** (-0.5)
CHUNK = 256


def nn(a, b):
    return lax.dot_general(a, b, (((1,), (0,)), ((), ())), preferred_element_type=f32)


def nt(a, b):
    return lax.dot_general(a, b, (((1,), (1,)), ((), ())), preferred_element_type=f32)


def tn(a, b):
    return lax.dot_general(a, b, (((0,), (0,)), ((), ())), preferred_element_type=f32)


def head_masks(rows, channels):
    lane = lax.broadcasted_iota(jnp.int32, (rows, channels), 1)
    return [(lane >= HEAD_DIM * h) & (lane < HEAD_DIM * (h + 1)) for h in range(channels // HEAD_DIM)]


def same_head(channels):
    row = lax.broadcasted_iota(jnp.int32, (channels, channels), 0) // HEAD_DIM
    lane = lax.broadcasted_iota(jnp.int32, (channels, channels), 1) // HEAD_DIM
    return row == lane


def compact(state):
    channels = state.shape[1]
    state = jnp.where(same_head(channels), state, 0.0)
    parts = [state[HEAD_DIM * h : HEAD_DIM * (h + 1), :] for h in range(channels // HEAD_DIM)]
    return sum(parts[1:], parts[0]).astype(bf16)


def expand(small):
    channels = small.shape[1]
    tall = jnp.concatenate([small.astype(f32)] * (channels // HEAD_DIM), axis=0)
    return jnp.where(same_head(channels), tall, 0.0)


def params(mib):
    return pltpu.CompilerParams(vmem_limit_bytes=mib * 1024 * 1024)


def kernel_call(kernel, outs, arrays, scalars=(), scratch=(), mib=32, us=2.0):
    vm = pl.BlockSpec(memory_space=pltpu.VMEM)
    sm = pl.BlockSpec(memory_space=pltpu.SMEM)
    return pl.pallas_call(
        kernel,
        out_shape=[jax.ShapeDtypeStruct(s, d) for s, d in outs],
        in_specs=[sm] * len(scalars) + [vm] * len(arrays),
        out_specs=[vm] * len(outs),
        scratch_shapes=list(scratch),
        compiler_params=params(mib),
        cost_estimate=pl.CostEstimate(flops=int(us * 1e9), bytes_accessed=1000, transcendentals=0),
    )(*scalars, *arrays)


def rolled_down(ext_ref, copies, rows):
    for r in range(8):
        copies[r, 8:rows, :] = ext_ref[8 - r : rows - r, :]


def shift_kernel(taps_n, key_ref, halo_ref, taps_ref, age_ref, tail_ref, value_ref, ks_ref, st_ref, ext, copies):
    rows, channels = key_ref.shape
    ext[0:taps_n, :] = halo_ref[...].astype(f32)
    ext[taps_n : taps_n + rows, :] = key_ref[...].astype(f32)
    rolled_down(ext, copies, rows + taps_n)

    def block(b, carry):
        start = pl.multiple_of(b * 64, 64)
        age = age_ref[pl.ds(start, 64), :]
        acc = jnp.zeros((64, channels), f32)
        for m in range(taps_n // 8):
            for r in range(8):
                j = 8 * m + r
                moved = copies[r, pl.ds(start + taps_n - 8 * m, 64), :]
                acc = acc + jnp.where(age >= j, moved, 0.0) * taps_ref[j : j + 1, :]
        ks_ref[pl.ds(start, 64), :] = acc
        return carry

    lax.fori_loop(0, rows // 64, block, 0)
    kt = (ks_ref[...] * tail_ref[...]).astype(bf16)
    st_ref[...] = compact(tn(value_ref[...], kt))


def shift_forward(key, halo, taps, age, tail, value):
    rows, channels = key.shape
    taps_n = taps.shape[0]
    return kernel_call(
        functools.partial(shift_kernel, taps_n),
        [((rows, channels), f32), ((HEAD_DIM, channels), bf16)],
        (key, halo, taps, age, tail, value),
        scratch=        [pltpu.VMEM((rows + taps_n, channels), f32), pltpu.VMEM((8, rows + taps_n, channels), f32)],
        us=10.0,
    )


def decay_factors(rate_row, rows):
    pos = lax.broadcasted_iota(jnp.int32, (rows, rate_row.shape[1]), 0).astype(f32)
    mid = 0.5 * rows
    q_fac = jnp.exp(-rate_row * (pos - mid))
    k_fac = jnp.exp(rate_row * (pos - mid))
    rise = jnp.exp(-rate_row * (pos + 1.0))
    tail = jnp.exp(-rate_row * (rows - 1.0 - pos))
    whole = jnp.exp(-rate_row * rows)
    return pos, mid, q_fac, k_fac, rise, tail, whole


def h3_kernel(q_ref, ks_ref, v_ref, sin_ref, rate_ref, segc_ref, segr_ref, entry_ref, y_ref, save_ref):
    rows, channels = q_ref.shape
    blocks = rows // CHUNK
    _, _, q_fac, k_fac, rise, tail, whole = decay_factors(rate_ref[...], CHUNK)
    heads = head_masks(CHUNK, channels)
    block_diag = same_head(channels)
    causal = lax.broadcasted_iota(jnp.int32, (CHUNK, CHUNK), 0) >= lax.broadcasted_iota(
        jnp.int32, (CHUNK, CHUNK), 1
    )
    state = expand(sin_ref[...])
    for b in range(blocks):
        sl = slice(b * CHUNK, (b + 1) * CHUNK)
        seg_c = segc_ref[sl, :]
        seg_r = segr_ref[:, sl]
        before = entry_ref[...] if b == 0 else segc_ref[b * CHUNK - 1 : b * CHUNK, :]
        last = segc_ref[(b + 1) * CHUNK - 1 : (b + 1) * CHUNK, :]
        carried = (seg_c == before).astype(f32)
        final = (seg_c == last).astype(f32)
        keep = (last == before).astype(f32)
        q = q_ref[sl, :].astype(f32) * scale
        k = ks_ref[sl, :]
        v = v_ref[sl, :]
        qf = (q * q_fac).astype(bf16)
        kf = (k * k_fac).astype(bf16)
        qr = (q * (rise * carried)).astype(bf16)
        kt = (k * (tail * final)).astype(bf16)
        allowed = causal & (seg_c == seg_r)
        save_ref[b, :, :] = state
        y = nt(qr, state.astype(bf16))
        for hm in heads:
            scores = nt(jnp.where(hm, qf, jnp.zeros_like(qf)), kf)
            scores = jnp.where(allowed, scores, 0.0).astype(bf16)
            y = y + jnp.where(hm, nn(scores, v), 0.0)
        y_ref[sl, :] = y.astype(bf16)
        state = state * (whole * keep) + jnp.where(block_diag, tn(v, kt), 0.0)


def h3_forward_call(q, ks, v, state_in, rate_row, seg_col, seg_row, entry):
    rows, channels = q.shape
    return kernel_call(
        h3_kernel,
        [((rows, channels), bf16), ((rows // CHUNK, channels, channels), f32)],
        (q, ks, v, state_in, rate_row, seg_col, seg_row, entry),
        us=5.0,
    )


def h3_back_kernel(
    taps_n,
    q_ref,
    ks_ref,
    v_ref,
    dy_ref,
    save_ref,
    dst_ref,
    rate_ref,
    segc_ref,
    segr_ref,
    entry_ref,
    key_ref,
    halo_ref,
    taps_ref,
    age_ref,
    rem_ref,
    dq_ref,
    dk_ref,
    dhalo_ref,
    dv_ref,
    dtaps_ref,
    drate_ref,
    ext,
    copies,
    dext,
    dcopies,
    tap_acc,
):
    rows, channels = q_ref.shape
    blocks = rows // CHUNK
    pos, mid, q_fac, k_fac, rise, tail, whole = decay_factors(rate_ref[...], CHUNK)
    heads = head_masks(CHUNK, channels)
    block_diag = same_head(channels)
    row = lax.broadcasted_iota(jnp.int32, (CHUNK, CHUNK), 0)
    lane = lax.broadcasted_iota(jnp.int32, (CHUNK, CHUNK), 1)
    dstate = expand(dst_ref[...])
    drate = jnp.zeros((1, channels), f32)
    dext[0:taps_n, :] = jnp.zeros((taps_n, channels), f32)
    dext[rows + taps_n : rows + 2 * taps_n, :] = jnp.zeros((taps_n, channels), f32)
    for b in reversed(range(blocks)):
        sl = slice(b * CHUNK, (b + 1) * CHUNK)
        seg_c = segc_ref[sl, :]
        seg_r = segr_ref[:, sl]
        before = entry_ref[...] if b == 0 else segc_ref[b * CHUNK - 1 : b * CHUNK, :]
        last = segc_ref[(b + 1) * CHUNK - 1 : (b + 1) * CHUNK, :]
        carried = (seg_c == before).astype(f32)
        final = (seg_c == last).astype(f32)
        keep = (last == before).astype(f32)
        q = q_ref[sl, :].astype(f32) * scale
        k = ks_ref[sl, :]
        v = v_ref[sl, :]
        dy = dy_ref[sl, :]
        qf = (q * q_fac).astype(bf16)
        kf = (k * k_fac).astype(bf16)
        rise_c = rise * carried
        tail_c = tail * final
        qr = (q * rise_c).astype(bf16)
        kt = (k * tail_c).astype(bf16)
        same = seg_c == seg_r
        low_mask = (row >= lane) & same
        up_mask = (row <= lane) & same
        state = save_ref[b, :, :]
        dstate_b = dstate.astype(bf16)
        dqf = jnp.zeros((CHUNK, channels), f32)
        dkf = jnp.zeros((CHUNK, channels), f32)
        dv = nt(kt, dstate_b)
        zero = jnp.zeros_like(qf)
        for hm in heads:
            kh = jnp.where(hm, kf, zero)
            vh = jnp.where(hm, v, zero)
            scores_t = jnp.where(up_mask, nt(kh, qf), 0.0).astype(bf16)
            dv = dv + jnp.where(hm, nn(scores_t, dy), 0.0)
            dsc = jnp.where(low_mask, nt(dy, vh), 0.0).astype(bf16)
            dsc_t = jnp.where(up_mask, nt(vh, dy), 0.0).astype(bf16)
            dqf = dqf + nn(dsc, kh)
            dkf = dkf + jnp.where(hm, nn(dsc_t, qf), 0.0)
        dqr = nn(dy, state.astype(bf16))
        dkt = nn(v, dstate_b)
        dq_ref[sl, :] = ((dqf * q_fac + dqr * rise_c) * scale).astype(bf16)
        dv_ref[sl, :] = dv.astype(bf16)
        dext[taps_n + b * CHUNK : taps_n + (b + 1) * CHUNK, :] = dkf * k_fac + dkt * tail_c
        part = (pos - mid) * (qf.astype(f32) * dqf - kf.astype(f32) * dkf)
        part = part + (pos + 1.0) * (qr.astype(f32) * dqr)
        part = part + (CHUNK - 1.0 - pos) * (kt.astype(f32) * dkt)
        drate = drate + jnp.sum(part, axis=0, keepdims=True)
        held = dstate * (whole * keep)
        drate = drate + CHUNK * jnp.sum(state * held, axis=0, keepdims=True)
        dstate = held + jnp.where(block_diag, tn(dy, qr), 0.0)
    drate_ref[...] = -drate

    total = rows + taps_n
    ext[0:taps_n, :] = halo_ref[...].astype(f32)
    ext[taps_n:total, :] = key_ref[...].astype(f32)
    rolled_down(ext, copies, total)
    for r in range(8):
        dcopies[r, 0 : total + taps_n - 8, :] = dext[r : total + taps_n - 8 + r, :]
    tap_acc[...] = jnp.zeros(tap_acc.shape, f32)

    def gathered(start):
        rem = rem_ref[pl.ds(start, 64), :]
        acc = jnp.zeros((64, channels), f32)
        for m in range(taps_n // 8):
            for r in range(8):
                j = 8 * m + r
                moved = dcopies[r, pl.ds(start + 8 * m, 64), :]
                acc = acc + jnp.where(rem >= j, moved, 0.0) * taps_ref[j : j + 1, :]
        return acc

    def block(b, carry):
        start = pl.multiple_of(b * 64, 64)
        dk_ref[pl.ds(start, 64), :] = gathered(start + taps_n)
        return carry

    lax.fori_loop(0, rows // 64, block, 0)
    dhalo_ref[...] = gathered(0).astype(bf16)

    def tap_block(b, carry):
        start = pl.multiple_of(b * 64, 64)
        age = age_ref[pl.ds(start, 64), :]
        grad = dext[pl.ds(start + taps_n, 64), :]
        for m in range(taps_n // 8):
            for r in range(8):
                j = 8 * m + r
                moved = copies[r, pl.ds(start + taps_n - 8 * m, 64), :]
                term = jnp.where(age >= j, moved, 0.0) * grad
                tap_acc[j, :, :] += jnp.sum(term.reshape(8, 8, channels), axis=0)
        return carry

    lax.fori_loop(0, rows // 64, tap_block, 0)
    dtaps_ref[...] = jnp.sum(tap_acc[...], axis=1)


def h3_back_call(q, ks, v, dy, save, dstate, rate_row, seg_col, seg_row, entry, key, halo, taps, age, rem):
    rows, channels = q.shape
    taps_n = taps.shape[0]
    total = rows + taps_n
    return kernel_call(
        functools.partial(h3_back_kernel, taps_n),
        [
            ((rows, channels), bf16),
            ((rows, channels), f32),
            ((taps_n, channels), bf16),
            ((rows, channels), bf16),
            ((taps_n, channels), f32),
            ((1, channels), f32),
        ],
        (q, ks, v, dy, save, dstate, rate_row, seg_col, seg_row, entry, key, halo, taps, age, rem),
        scratch=[
            pltpu.VMEM((total, channels), f32),
            pltpu.VMEM((8, total, channels), f32),
            pltpu.VMEM((total + taps_n, channels), f32),
            pltpu.VMEM((8, total + taps_n, channels), f32),
            pltpu.VMEM((taps_n, 8, channels), f32),
        ],
        mib=48,
        us=26.0,
    )


def attend_kernel(resume, finish, lim_ref, q_ref, k_ref, v_ref, segc_ref, segr_ref, *refs):
    if resume:
        acc_in, col_in = refs[:2]
        refs = refs[2:]
    rows, channels = q_ref.shape
    n_heads = channels // HEAD_DIM
    heads = head_masks(CHUNK, channels)
    row = lax.broadcasted_iota(jnp.int32, (CHUNK, CHUNK), 0)
    lane = lax.broadcasted_iota(jnp.int32, (CHUNK, CHUNK), 1)
    stat_lane = lax.broadcasted_iota(jnp.int32, (CHUNK, 128), 1)
    for b in range(rows // CHUNK):
        sl = slice(b * CHUNK, (b + 1) * CHUNK)
        low, high, diagonal = lim_ref[0, b], lim_ref[1, b], lim_ref[2, b]
        q = q_ref[sl, :]
        seg_c = segc_ref[sl, :]
        qh = [jnp.where(hm, q, jnp.zeros_like(q)) for hm in heads]

        def step(t, carry):
            at = pl.multiple_of(t * CHUNK, CHUNK)
            keys = k_ref[pl.ds(at, CHUNK), :]
            values = v_ref[pl.ds(at, CHUNK), :]
            seg_r = segr_ref[t]
            allowed = (row >= lane + (t - diagonal) * CHUNK) & (seg_c == seg_r)
            new = []
            for h in range(n_heads):
                top, total, acc = carry[h]
                z = jnp.where(allowed, nt(qh[h], keys) * scale, masked_low)
                new_top = jnp.maximum(top, jnp.max(z, axis=1, keepdims=True))
                shrink = jnp.exp(top - new_top)
                e = jnp.where(allowed, jnp.exp(z - new_top), 0.0)
                total = total * shrink + jnp.sum(e, axis=1, keepdims=True)
                acc = acc * shrink + nn(e.astype(bf16), values)
                new.append((new_top, total, acc))
            return tuple(new)

        if resume:
            col = col_in[sl, :]
            held = acc_in[sl, :]
            start = tuple((col[:, h : h + 1], col[:, 8 + h : 9 + h], held) for h in range(n_heads))
        else:
            start = tuple(
                (
                    jnp.full((CHUNK, 1), masked_low, f32),
                    jnp.zeros((CHUNK, 1), f32),
                    jnp.zeros((CHUNK, channels), f32),
                )
                for _ in range(n_heads)
            )
        state = lax.fori_loop(low, high + 1, step, start)
        out = jnp.zeros((CHUNK, channels), f32)
        stats = jnp.zeros((CHUNK, 128), f32)
        for h in range(n_heads):
            top, total, acc = state[h]
            out = jnp.where(heads[h], acc / total if finish else acc, out)
            stats = jnp.where(stat_lane == h, top, stats)
            stats = jnp.where(stat_lane == 8 + h, total, stats)
        refs[0][sl, :] = out
        if finish:
            refs[1][b, :, :] = stats.T[0:16, :]
            refs[2][sl, :] = out.astype(bf16)
        else:
            refs[1][sl, :] = stats


def attend(lim, q, k, v, seg_col, seg_tiles, held=(), finish=True):
    rows, channels = q.shape
    if finish:
        outs = [((rows, channels), f32), ((rows // CHUNK, 16, CHUNK), f32), ((rows, channels), bf16)]
    else:
        outs = [((rows, channels), f32), ((rows, 128), f32)]
    return kernel_call(
        functools.partial(attend_kernel, bool(held), finish),
        outs,
        (q, k, v, seg_col, seg_tiles, *held),
        scalars=(lim,),
        mib=48,
        us=5.0,
    )


def attend_back_kernel(
    lim_ref, q_ref, k_ref, v_ref, do_ref, o_ref, stat_ref, qseg_ref, kseg_ref, dqin_ref, dq_ref, dkv_ref, acc
):
    rows, channels = q_ref.shape
    n_heads = channels // HEAD_DIM
    heads = head_masks(CHUNK, channels)
    row = lax.broadcasted_iota(jnp.int32, (CHUNK, CHUNK), 0)
    lane = lax.broadcasted_iota(jnp.int32, (CHUNK, CHUNK), 1)
    stat_lane = lax.broadcasted_iota(jnp.int32, (CHUNK, 128), 1)
    acc[...] = jnp.zeros(acc.shape, f32)
    for b in range(rows // CHUNK):
        sl = slice(b * CHUNK, (b + 1) * CHUNK)
        low, high, diagonal = lim_ref[0, b], lim_ref[1, b], lim_ref[2, b]
        q = q_ref[sl, :]
        do = do_ref[sl, :].astype(f32)
        o = o_ref[sl, :]
        seg_q = qseg_ref[b]
        zero = jnp.zeros_like(q)
        qh = [jnp.where(hm, q, zero) for hm in heads]
        cols = jnp.zeros((CHUNK, 128), f32)
        for h in range(n_heads):
            inner = jnp.sum(jnp.where(heads[h], do * o, 0.0), axis=1, keepdims=True)
            cols = jnp.where(stat_lane == h, inner, cols)
        inner_rows = cols.T
        totals = stat_ref[b, 8:16, :]
        inv_cols = jnp.concatenate([1.0 / jnp.maximum(totals, 1e-30), jnp.zeros((120, CHUNK), f32)]).T
        wh = []
        for h in range(n_heads):
            inv = inv_cols[:, h : h + 1]
            wh.append(jnp.where(heads[h], do * inv, 0.0).astype(bf16))

        def step(t, dq):
            at = pl.multiple_of(t * CHUNK, CHUNK)
            keys = k_ref[pl.ds(at, CHUNK), :]
            values = v_ref[pl.ds(at, CHUNK), :]
            seg_k = kseg_ref[pl.ds(at, CHUNK), :]
            allowed = (lane >= row + (t - diagonal) * CHUNK) & (seg_k == seg_q)
            dk = jnp.zeros((CHUNK, channels), f32)
            dv = jnp.zeros((CHUNK, channels), f32)
            for h in range(n_heads):
                top = stat_ref[b, h : h + 1, :]
                total = stat_ref[b, 8 + h : 9 + h, :]
                z = jnp.where(allowed, nt(keys, qh[h]) * scale, masked_low)
                e = jnp.where(allowed, jnp.exp(z - top), 0.0)
                dp = nt(values, wh[h])
                dz = (e * (dp - inner_rows[h : h + 1, :] / total)).astype(bf16)
                dk = dk + nn(dz, qh[h])
                dv = dv + nn(e.astype(bf16), wh[h])
                dq = dq + jnp.where(heads[h], tn(dz, keys), 0.0)
            acc[0, pl.ds(at, CHUNK), :] += dk
            acc[1, pl.ds(at, CHUNK), :] += dv
            return dq

        dq = lax.fori_loop(low, high + 1, step, jnp.zeros((CHUNK, channels), f32))
        dq_ref[sl, :] = (dq * scale + dqin_ref[sl, :].astype(f32)).astype(dq_ref.dtype)
    dkv_ref[:, 0:channels] = (acc[0] * scale).astype(dkv_ref.dtype)
    dkv_ref[:, channels : 2 * channels] = acc[1].astype(dkv_ref.dtype)


def attend_back(lim, q, k, v, do, o, stats, q_tiles, key_col, dq_in, dq_type, dkv_type):
    rows, channels = q.shape
    return kernel_call(
        attend_back_kernel,
        [((rows, channels), dq_type), ((k.shape[0], 2 * channels), dkv_type)],
        (q, k, v, do, o, stats, q_tiles, key_col, dq_in),
        scalars=(lim,),
        scratch=[pltpu.VMEM((2, k.shape[0], channels), f32)],
        mib=56,
        us=7.0,
    )


def by_rows(rows, step, body):
    def one(i, carry):
        body(pl.ds(pl.multiple_of(i * step, step), step))
        return carry

    lax.fori_loop(0, rows // step, one, 0)


def norm_kernel(n_add, x_ref, *refs):
    adds, gain_ref, outs = refs[:n_add], refs[n_add], refs[n_add + 1 :]

    def body(at):
        x = x_ref[at, :].astype(f32)
        for a in adds:
            x = x + a[at, :].astype(f32)
        center = jnp.mean(x, axis=1, keepdims=True)
        moved = x - center
        inv = lax.rsqrt(jnp.mean(moved * moved, axis=1, keepdims=True) + epsilon)
        outs[0][at, :] = x
        outs[1][at, :] = (moved * inv * gain_ref[...]).astype(bf16)

    by_rows(x_ref.shape[0], 32, body)


def norm(x, adds, gain):
    shape = x.shape
    return kernel_call(
        functools.partial(norm_kernel, len(adds)),
        [(shape, f32), (shape, bf16)],
        (x, *adds, gain.reshape(1, -1)),
        us=2.0,
    )


def norm_back_kernel(n_add, x_ref, grad_ref, *refs):
    adds, gain_ref, outs = refs[:n_add], refs[n_add], refs[n_add + 1 :]

    def body(at):
        x = x_ref[at, :]
        center = jnp.mean(x, axis=1, keepdims=True)
        moved = x - center
        inv = lax.rsqrt(jnp.mean(moved * moved, axis=1, keepdims=True) + epsilon)
        unit = moved * inv
        d = adds[0][at, :].astype(f32)
        for a in adds[1:]:
            d = d + a[at, :].astype(f32)
        d = d * gain_ref[...]
        mean_d = jnp.mean(d, axis=1, keepdims=True)
        mean_du = jnp.mean(d * unit, axis=1, keepdims=True)
        grad = grad_ref[at, :].astype(f32) + inv * (d - mean_d - unit * mean_du)
        outs[0][at, :] = grad
        outs[1][at, :] = grad.astype(bf16)

    by_rows(x_ref.shape[0], 32, body)


def norm_back(x, grad, adds, gain):
    shape = x.shape
    return kernel_call(
        functools.partial(norm_back_kernel, len(adds)),
        [(shape, f32), (shape, bf16)],
        (x, grad, *adds, gain.reshape(1, -1)),
        us=2.0,
    )


def gelu_both(u):
    inner = 0.7978845608028654 * (u + 0.044715 * (u * u * u))
    t = jnp.tanh(inner)
    half = 0.5 * (1.0 + t)
    slope = half + 0.5 * u * (1.0 - t * t) * (0.7978845608028654 * (1.0 + 0.134145 * (u * u)))
    return u * half, slope


def feed_forward_kernel(n, hid, *refs):
    ms, w_ref = refs[:n], refs[n]
    parts, r_ref, slope_ref, up = refs[n + 1 : 2 * n + 1], refs[2 * n + 1], refs[2 * n + 2], refs[2 * n + 3]
    size = ms[0].shape[0]
    for i in range(n):
        up[...] = nn(ms[i][...], w_ref[:, 0:hid])

        def body(at):
            r, slope = gelu_both(up[at, :])
            to = pl.ds(pl.multiple_of(at.start + i * size, 32), 32)
            r_ref[to, :] = r.astype(bf16)
            slope_ref[to, :] = slope.astype(bf16)

        by_rows(size, 32, body)
        parts[i][...] = nt(r_ref[i * size : (i + 1) * size, :], w_ref[:, hid : 2 * hid]).astype(bf16)


def feed_forward(ms, w, hid):
    n, size = len(ms), ms[0].shape[0]
    model = ms[0].shape[1]
    out = kernel_call(
        functools.partial(feed_forward_kernel, n, hid),
        [((size, model), bf16)] * n + [((n * size, hid), bf16)] * 2,
        (*ms, w),
        scratch=[pltpu.VMEM((size, hid), f32)],
        us=5.0,
    )
    return out[:n], out[n], out[n + 1]


def feed_mid_kernel(n, hid, *refs):
    ms, gs, w_ref, gain_ref = refs[:n], refs[n : 2 * n], refs[2 * n], refs[2 * n + 1]
    outs = refs[2 * n + 2 :]
    parts, r_ref, du_ref, gsum_ref, up, dr = outs[:n], outs[n], outs[n + 1], outs[n + 2], outs[n + 3], outs[n + 4]
    size = ms[0].shape[0]
    gsum_ref[...] = jnp.zeros(gsum_ref.shape, f32)
    for i in range(n):
        up[...] = nn(ms[i][...], w_ref[:, 0:hid])
        dr[...] = nn(gs[i][...], w_ref[:, hid : 2 * hid])

        def body(at):
            r, slope = gelu_both(up[at, :])
            to = pl.ds(pl.multiple_of(at.start + i * size, 32), 32)
            r_ref[to, :] = r.astype(bf16)
            du_ref[to, :] = (dr[at, :] * slope).astype(bf16)

        by_rows(size, 32, body)
        part = nt(du_ref[i * size : (i + 1) * size, :], w_ref[:, 0:hid])
        parts[i][...] = part.astype(bf16)
        gsum_ref[...] += jnp.sum(part * ms[i][...].astype(f32), axis=0, keepdims=True)
    gsum_ref[...] = gsum_ref[...] / gain_ref[...]


def feed_mid(ms, gs, w, hid, gain):
    n, size = len(ms), ms[0].shape[0]
    model = ms[0].shape[1]
    out = kernel_call(
        functools.partial(feed_mid_kernel, n, hid),
        [((size, model), bf16)] * n + [((n * size, hid), bf16)] * 2 + [((1, model), f32)],
        (*ms, *gs, w, gain.reshape(1, -1)),
        scratch=[pltpu.VMEM((size, hid), f32)] * 2,
        us=6.0,
    )
    return out[:n], out[n], out[n + 1], out[n + 2]


def feed_back_kernel(n, hid, *refs):
    ms, gs, slope_ref, w_ref, gain_ref = refs[:n], refs[n : 2 * n], refs[2 * n], refs[2 * n + 1], refs[2 * n + 2]
    outs = refs[2 * n + 3 :]
    parts, du_ref, gsum_ref, dr = outs[:n], outs[n], outs[n + 1], outs[n + 2]
    size = ms[0].shape[0]
    gsum_ref[...] = jnp.zeros(gsum_ref.shape, f32)
    for i in range(n):
        dr[...] = nn(gs[i][...], w_ref[:, hid : 2 * hid])

        def body(at):
            to = pl.ds(pl.multiple_of(at.start + i * size, 32), 32)
            du_ref[to, :] = (dr[at, :] * slope_ref[to, :].astype(f32)).astype(bf16)

        by_rows(size, 32, body)
        part = nt(du_ref[i * size : (i + 1) * size, :], w_ref[:, 0:hid])
        parts[i][...] = part.astype(bf16)
        gsum_ref[...] += jnp.sum(part * ms[i][...].astype(f32), axis=0, keepdims=True)
    gsum_ref[...] = gsum_ref[...] / gain_ref[...]


def feed_back(ms, gs, slope, w, hid, gain):
    n, size = len(ms), ms[0].shape[0]
    model = ms[0].shape[1]
    out = kernel_call(
        functools.partial(feed_back_kernel, n, hid),
        [((size, model), bf16)] * n + [((n * size, hid), bf16), ((1, model), f32)],
        (*ms, *gs, slope, w, gain.reshape(1, -1)),
        scratch=[pltpu.VMEM((size, hid), f32)],
        us=4.0,
    )
    return out[:n], out[n], out[n + 1]


def places(core_ref, n, size):
    if n == 1:
        return [pl.ds(0, size)]
    core = core_ref[0]
    return [
        pl.ds(pl.multiple_of(core * size, size), size),
        pl.ds(pl.multiple_of((1 - core) * size, size), size),
    ]


def project_kernel(n, at_lane, channels, core_ref, *refs):
    ns, w_ref, outs = refs[:n], refs[n], refs[n + 1 :]
    size = ns[0].shape[0]
    for i, to in enumerate(places(core_ref, n, size)):
        x = ns[i][...]
        triple = nn(x, w_ref[:, at_lane : at_lane + 3 * channels])
        for j in range(3):
            outs[j][to, :] = triple[:, j * channels : (j + 1) * channels].astype(bf16)
        outs[3][to, :] = x


def project(core, ns, w, at_lane, channels):
    n, size, model = len(ns), ns[0].shape[0], ns[0].shape[1]
    return kernel_call(
        functools.partial(project_kernel, n, at_lane, channels),
        [((n * size, channels), bf16)] * 3 + [((n * size, model), bf16)],
        (*ns, w),
        scalars=(core,),
        us=3.0,
    )


def out_kernel(n, at_lane, core_ref, y_ref, w_ref, *parts):
    channels = y_ref.shape[1]
    size = parts[0].shape[0]
    for i, to in enumerate(places(core_ref, n, size)):
        parts[i][...] = nt(y_ref[to, :].astype(bf16), w_ref[:, at_lane : at_lane + channels]).astype(bf16)


def project_out(core, n, y, w, at_lane):
    size, model = y.shape[0] // n, w.shape[0]
    return kernel_call(
        functools.partial(out_kernel, n, at_lane),
        [((size, model), bf16)] * n,
        (y, w),
        scalars=(core,),
        us=2.0,
    )


def out_back_kernel(n, at_lane, channels, state, core_ref, *refs):
    gs, w_ref = refs[:n], refs[n]
    refs = refs[n + 1 :]
    if state:
        q_ref, rise_ref = refs[:2]
        refs = refs[2:]
    dy_ref, ordered_ref = refs[0], refs[1]
    size = gs[0].shape[0]
    for i, to in enumerate(places(core_ref, n, size)):
        g = gs[i][...]
        dy_ref[to, :] = nn(g, w_ref[:, at_lane : at_lane + channels]).astype(bf16)
        ordered_ref[to, :] = g
    if state:
        qr = (q_ref[...].astype(f32) * scale * rise_ref[...]).astype(bf16)
        refs[2][...] = compact(tn(dy_ref[...], qr))


def out_back(core, gs, w, at_lane, channels, state=()):
    n, size, model = len(gs), gs[0].shape[0], gs[0].shape[1]
    outs = [((n * size, channels), bf16), ((n * size, model), bf16)]
    if state:
        outs.append(((HEAD_DIM, channels), bf16))
    return kernel_call(
        functools.partial(out_back_kernel, n, at_lane, channels, bool(state)),
        outs,
        (*gs, w, *state),
        scalars=(core,),
        us=2.0,
    )


def project_back_kernel(n, at_lane, kind, count, core_ref, dq_ref, *refs):
    others = refs[:count]
    w_ref, n_ref, gain_ref = refs[count : count + 3]
    outs = refs[count + 3 :]
    parts, cat_ref, gsum_ref = outs[:n], outs[n], outs[n + 1]
    rows, channels = dq_ref.shape
    cat_ref[:, 0:channels] = dq_ref[...]
    if kind == "halo":
        dk_ref, dv_ref, extra_ref = others
        cut = rows - extra_ref.shape[0]
        cat_ref[0:cut, channels : 2 * channels] = dk_ref[0:cut, :].astype(bf16)
        cat_ref[cut:rows, channels : 2 * channels] = (
            dk_ref[cut:rows, :] + extra_ref[...].astype(f32)
        ).astype(bf16)
        cat_ref[:, 2 * channels : 3 * channels] = dv_ref[...].astype(bf16)
    else:
        total = others[0][...].astype(f32)
        for other in others[1:]:
            total = total + other[...].astype(f32)
        cat_ref[:, channels : 3 * channels] = total.astype(bf16)
    size = parts[0].shape[0]
    gsum_ref[...] = jnp.zeros(gsum_ref.shape, f32)
    for i, to in enumerate(places(core_ref, n, size)):
        part = nt(cat_ref[to, :], w_ref[:, at_lane : at_lane + 3 * channels])
        parts[i][...] = part.astype(bf16)
        gsum_ref[...] += jnp.sum(part * n_ref[to, :].astype(f32), axis=0, keepdims=True)
    gsum_ref[...] = gsum_ref[...] / gain_ref[...]


def project_back(core, n, kind, dq, others, w, at_lane, normed, gain):
    rows, channels = dq.shape
    size, model = rows // n, normed.shape[1]
    out = kernel_call(
        functools.partial(project_back_kernel, n, at_lane, kind, len(others)),
        [((size, model), bf16)] * n + [((rows, 3 * channels), bf16), ((1, model), f32)],
        (dq, *others, w, normed, gain.reshape(1, -1)),
        scalars=(core,),
        us=3.0,
    )
    return out[:n], out[n], out[n + 1]


def at_rows(value, start, count):
    return lax.dynamic_slice_in_dim(value, start, count, 0)


def tie(*values):
    return lax.optimization_barrier(values)


class Rows:
    halves = 1

    def __init__(self):
        self.blocks = lax.axis_size("ctx")
        self.place = lax.axis_index("ctx")
        self.core = self.place

    def enter(self, rows):
        return rows

    def leave(self, rows):
        return rows

    def leave_grad(self, rows):
        return rows

    def spread(self, rows):
        return [rows]

    def total(self, parts):
        return [lax.psum(parts[0], "tp")]

    def local(self, value):
        return value

    def weights(self, first, lower, upper):
        return [lax.all_gather(w, "fsdp", axis=0, tiled=True) for w in (first, lower, upper)]

    def ids(self, ids, taps_n):
        n = self.blocks
        halo = lax.ppermute(
            ids[ids.shape[0] - taps_n :].astype(bf16), "ctx", [(i, i + 1) for i in range(n - 1)]
        )
        return ids, halo.astype(jnp.int32), None

    def from_previous(self, value):
        n = self.blocks
        return lax.ppermute(value, "ctx", [(i, i + 1) for i in range(n - 1)])

    def to_previous(self, value):
        n = self.blocks
        return lax.ppermute(value, "ctx", [(i + 1, i) for i in range(n - 1)])

    def state_before(self, factor, state):
        factors = lax.all_gather(factor.astype(bf16), "ctx").astype(f32)
        states = lax.all_gather(state, "ctx")

        def one(hop, held):
            return states[hop].astype(f32) + factors[hop] * held

        held = lax.fori_loop(0, self.place, one, jnp.zeros(state.shape, f32))
        return held.astype(bf16)

    def grad_after(self, factor, dstate):
        factors = lax.all_gather(factor.astype(bf16), "ctx").astype(f32)
        states = lax.all_gather(dstate, "ctx")

        def one(hop, held):
            at = self.blocks - 1 - hop
            return states[at].astype(f32) + factors[at] * held

        held = lax.fori_loop(0, self.blocks - 1 - self.place, one, jnp.zeros(dstate.shape, f32))
        return held.astype(bf16)

    def attend(self, q, k, v, ids, prev_ids):
        rows = q.shape[0]
        keys = lax.all_gather(k, "ctx", axis=0, tiled=True)
        values = lax.all_gather(v, "ctx", axis=0, tiled=True)
        key_ids = lax.all_gather(ids.astype(bf16), "ctx", axis=0, tiled=True).astype(jnp.int32)
        low = first_tiles(ids, key_ids)
        high = self.place * (rows // CHUNK) + jnp.arange(rows // CHUNK, dtype=jnp.int32)
        limits = jnp.stack([low, high, high])
        mixed, stats, mixed_bf = attend(
            limits, q, keys, values, ids[:, None], key_ids.reshape(-1, 1, CHUNK)
        )
        return mixed, stats, mixed_bf, (limits, keys, values, key_ids)

    def attend_back(self, kept, q, k, v, grad, mixed, stats, ids, prev_ids):
        limits, keys, values, key_ids = kept
        tiles = ids.reshape(-1, 1, CHUNK)
        dq, dkv = attend_back(
            limits, q, keys, values, grad, mixed, stats, tiles, key_ids[:, None],
            jnp.zeros(q.shape, bf16), bf16, bf16,
        )
        return dq, [lax.psum_scatter(dkv, "ctx", scatter_dimension=0, tiled=True)]

    def reduce(self, value):
        value = lax.psum_scatter(value, "fsdp", scatter_dimension=0, tiled=True)
        return lax.psum(value, "ctx")

    def over_places(self, value):
        return lax.psum(value, "tp")


class Pairs(Rows):
    halves = 2

    def __init__(self):
        self.blocks = 2
        self.core = lax.axis_index("ctx")
        self.chip = lax.axis_index("tp")
        self.place = self.chip // 2
        self.home = self.core == self.place

    def send(self, value, pairs):
        number = [(4 * c + t, 4 * d + u) for (c, t), (d, u) in pairs]
        return lax.ppermute(value, ("ctx", "tp"), number)

    def swap(self, value):
        return lax.ppermute(value, "ctx", [(0, 1), (1, 0)])

    def neighbour(self, value):
        return lax.ppermute(value, "tp", [(0, 1), (1, 0), (2, 3), (3, 2)])

    def across(self, value):
        return lax.ppermute(value, "tp", [(0, 2), (2, 0), (1, 3), (3, 1)])

    def from_home_core(self, value):
        return self.send(value, [((t // 2, t), (1 - t // 2, t)) for t in range(4)])

    def enter(self, rows):
        half = rows.shape[0] // 2
        got = self.from_home_core(at_rows(rows, (1 - self.core) * half, half))
        return jnp.where(self.home, at_rows(rows, self.core * half, half), got)

    def ids(self, ids, taps_n):
        other = self.swap(ids)
        own = jnp.where(self.home, ids, other)
        first = jnp.where(self.core == 0, ids, other)
        before = jnp.where(self.place == 1, first, 0)
        return own, before[ids.shape[0] - taps_n :], before

    def in_order(self, own, other):
        first = self.core == 0
        return jnp.concatenate([jnp.where(first, own, other), jnp.where(first, other, own)])

    def leave(self, rows):
        there = self.across(rows)
        got = self.swap(jnp.where(self.home, there, rows))
        return self.in_order(jnp.where(self.home, rows, there), got)

    def leave_grad(self, rows):
        return self.leave(rows.astype(bf16)).astype(f32)

    def spread(self, rows):
        return [rows, self.swap(rows)]

    def total(self, parts):
        own, other = parts
        both = (own.astype(f32) + self.swap(other).astype(f32)).astype(bf16)
        return [both, self.neighbour(both)]

    def local(self, value):
        got = self.send(
            value, [((c, 2 * c + e), (c, 2 - 2 * c + e)) for c in range(2) for e in range(2)]
        )
        return jnp.where(self.home, value, got)

    def around(self, value):
        return [lax.ppermute(value, "fsdp", [(i, i ^ k) for i in range(4)]) for k in (1, 2, 3)]

    def weights(self, first, lower, upper):
        first = self.local(first)
        first, lower = tie(first, lower)
        lower = self.local(lower)
        lower, upper = tie(lower, upper)
        upper = self.local(upper)
        place, size = lax.axis_index("fsdp"), first.shape[0]
        whole = jnp.zeros((4 * size, first.shape[1]), bf16)
        for k, part in enumerate([first] + self.around(first)):
            whole = lax.dynamic_update_slice_in_dim(whole, part, (place ^ k) * size, 0)
        return [whole] + [lax.all_gather(w, "fsdp", axis=0, tiled=True) for w in (lower, upper)]

    def from_previous(self, value):
        return self.send(value, [((c, t), (c, t + 2)) for c in range(2) for t in range(2)])

    def to_previous(self, value):
        return self.send(value, [((c, t + 2), (c, t)) for c in range(2) for t in range(2)])

    def state_before(self, factor, state):
        return self.from_previous(state)

    def grad_after(self, factor, dstate):
        return self.to_previous(dstate)

    def attend(self, q, k, v, ids, prev_ids):
        before = self.from_previous(jnp.concatenate([k, v], axis=1))
        channels, count = q.shape[1], q.shape[0] // CHUNK
        place = jnp.arange(count, dtype=jnp.int32)
        low = first_tiles(ids, jnp.concatenate([prev_ids, ids]))
        own_limits = jnp.stack([jnp.maximum(low - count, 0), place, place])
        prev_limits = jnp.stack([low, jnp.full_like(low, count - 1), place + count])
        seg_col, tiles, prev_tiles = ids[:, None], ids.reshape(-1, 1, CHUNK), prev_ids.reshape(-1, 1, CHUNK)
        held = attend(own_limits, q, k, v, seg_col, tiles, finish=False)
        keys, values = before[:, :channels], before[:, channels:]
        mixed, stats, mixed_bf = attend(prev_limits, q, keys, values, seg_col, prev_tiles, held)
        return mixed, stats, mixed_bf, (own_limits, prev_limits, keys, values)

    def attend_back(self, kept, q, k, v, grad, mixed, stats, ids, prev_ids):
        own_limits, prev_limits, keys, values = kept
        tiles = ids.reshape(-1, 1, CHUNK)
        dq, dkv_prev = attend_back(
            prev_limits, q, keys, values, grad, mixed, stats, tiles, prev_ids[:, None],
            jnp.zeros(q.shape, bf16), f32, bf16,
        )
        got = self.to_previous(dkv_prev)
        dq, dkv = attend_back(
            own_limits, q, k, v, grad, mixed, stats, tiles, ids[:, None], dq, bf16, f32
        )
        return dq, [dkv, got]

    def reduce(self, value):
        place = lax.axis_index("fsdp")
        size = value.shape[0] // 4
        total = at_rows(value, place * size, size).astype(f32)
        for k in (1, 2, 3):
            part = at_rows(value, (place ^ k) * size, size)
            total = total + lax.ppermute(part, "fsdp", [(i, i ^ k) for i in range(4)]).astype(f32)
        total = total.astype(bf16)
        got = self.send(
            total, [((c, 2 - 2 * c + e), (c, 2 * c + e)) for c in range(2) for e in range(2)]
        )
        total = (total.astype(f32) + got.astype(f32)).astype(bf16)
        return jnp.where(self.home, total, self.from_home_core(total))

    def over_places(self, value):
        value = (value.astype(f32) + self.neighbour(value).astype(f32)).astype(bf16)
        return value.astype(f32) + self.across(value).astype(f32)


def first_tiles(ids, key_ids):
    firsts = ids[::CHUNK]
    return jnp.sum((key_ids[None, :] < firsts[:, None]).astype(jnp.int32), axis=1) // CHUNK


def dot_tn(a, b):
    return jnp.einsum("tf,td->fd", a, b, preferred_element_type=f32).astype(bf16)


def mixer_setup(ids, halo_ids, taps_n, rate_row):
    rows, channels = ids.shape[0], rate_row.shape[1]
    ext = jnp.concatenate([halo_ids, ids])
    at = jnp.arange(rows + taps_n, dtype=jnp.int32)
    same = ext[:, None] == ext[None, :]
    age = jnp.sum((same & (at[None, :] < at[:, None])).astype(jnp.int32), axis=1)[taps_n:]
    rem = jnp.sum((same & (at[None, :] > at[:, None])).astype(jnp.int32), axis=1)
    entry, last = halo_ids[taps_n - 1], ids[rows - 1]
    pos = jnp.arange(rows, dtype=f32)[:, None]
    tail = jnp.exp(-rate_row * (rows - 1.0 - pos)) * (ids == last).astype(f32)[:, None]
    rise = jnp.exp(-rate_row * (pos + 1.0)) * (ids == entry).astype(f32)[:, None]
    factor = jnp.exp(-rate_row * rows) * (entry == last).astype(f32)
    return (
        jnp.broadcast_to(age[:, None], (rows, channels)),
        jnp.broadcast_to(rem[:, None], (rows + taps_n, channels)),
        tail,
        rise,
        factor,
        entry.reshape(1, 1),
    )


def feed_shares(reduced):
    width = reduced.shape[1] // 2
    return reduced[:, :width].astype(f32), reduced[:, width:].T.astype(f32)


def mixer_shares(reduced, channels):
    parts = [reduced[:, j * channels : (j + 1) * channels].astype(f32) for j in range(3)]
    return jnp.stack(parts), reduced[:, 3 * channels : 4 * channels].T.astype(f32)


def run(plan, inputs, cotangent, segments, gains, last_gain, in_weight, h3_out, attn_out, up_weight, down_weight, shift_taps, decay_rate):
    n = plan.halves
    slots = lax.axis_size("fsdp")
    hid = up_weight.shape[2]
    channels = h3_out.shape[0]
    taps_n = shift_taps.shape[0]
    share = h3_out.shape[1]
    core = plan.core.astype(jnp.int32).reshape(1)
    gap = (-3 * channels) % 128
    pad = jnp.zeros((share, gap), bf16)
    in_at, out1_at = 2 * hid, 2 * hid + 3 * channels + gap

    x_in = plan.enter(inputs[0])
    g_in = plan.enter(cotangent[0])
    ids, halo_ids, prev_ids = plan.ids(segments[0] + 1, taps_n)
    rows = ids.shape[0]
    first = jnp.concatenate([in_weight[0, j] for j in range(3)], axis=1)
    lower = jnp.concatenate([up_weight[0], down_weight[0].T, h3_out.T], axis=1)
    upper = jnp.concatenate(
        [up_weight[1], down_weight[1].T] + [in_weight[1, j] for j in range(3)] + [pad, attn_out.T], axis=1
    )
    first, lower, upper = plan.weights(first, lower, upper)
    both = plan.local(jnp.concatenate([shift_taps, decay_rate.reshape(1, -1)]))
    taps, rate_row = both[:taps_n], both[taps_n:]
    age, rem, tail, rise, factor, entry = mixer_setup(ids, halo_ids, taps_n, rate_row)
    seg_col, seg_row = ids[:, None], ids[None, :]

    x0, n0 = norm(x_in, [], gains[0])
    q0, k0, v0, n0 = project(core, plan.spread(n0), first, 0, channels)
    halo = plan.from_previous(k0[rows - taps_n :])
    ks, state_end = shift_forward(k0, halo, taps, age, tail, v0)
    state_in = plan.state_before(factor, state_end)
    y0, saved = h3_forward_call(q0, ks, v0, state_in, rate_row, seg_col, seg_row, entry)
    y0, lower = tie(y0, lower)
    parts = project_out(core, n, y0, lower, 2 * hid)
    x1, m0 = norm(x0, plan.total(parts), gains[1])
    m0s = plan.spread(m0)
    parts, r0, slope0 = feed_forward(m0s, lower, hid)
    x2, n2 = norm(x1, plan.total(parts), gains[2])

    q2, k2, v2, n2 = project(core, plan.spread(n2), upper, in_at, channels)
    mixed, stats, mixed_bf, kept = plan.attend(q2, k2, v2, ids, prev_ids)
    parts = project_out(core, n, mixed_bf, upper, out1_at)
    x3, m1 = norm(x2, plan.total(parts), last_gain)
    m1s = plan.spread(m1)

    g_ins = plan.spread(g_in)
    parts, r1, du1, gain3 = feed_mid(m1s, g_ins, upper, hid, last_gain)
    grad, grad_bf = norm_back(x3, g_in, plan.total(parts), last_gain)
    dmixed, grad_bf1 = out_back(core, plan.spread(grad_bf), upper, out1_at, channels)
    dq, dkv = plan.attend_back(kept, q2, k2, v2, dmixed, mixed, stats, ids, prev_ids)
    parts, cat1, gain2 = project_back(core, n, "sum", dq, dkv, upper, in_at, n2, gains[2])
    grad, grad_bf = norm_back(x2, grad, plan.total(parts), gains[2])

    size = rows // n
    parts = [
        jnp.einsum("tf,df->td", r1[i * size : (i + 1) * size], upper[:, hid : 2 * hid], preferred_element_type=f32).astype(bf16)
        for i in range(n)
    ]
    x4 = x3
    for part in plan.total(parts):
        x4 = x4 + part.astype(f32)
    output = plan.leave(x4.astype(bf16))
    feed1 = plan.reduce(
        jnp.concatenate([dot_tn(jnp.concatenate(m1s), du1), dot_tn(jnp.concatenate(g_ins), r1)], axis=1)
    )
    mix1 = plan.reduce(jnp.concatenate([dot_tn(n2, cat1), dot_tn(grad_bf1, mixed_bf)], axis=1))

    grad_bfs = plan.spread(grad_bf)
    parts, du0, gain1 = feed_back(m0s, grad_bfs, slope0, lower, hid, gains[1])
    feed0 = plan.reduce(
        jnp.concatenate([dot_tn(jnp.concatenate(m0s), du0), dot_tn(jnp.concatenate(grad_bfs), r0)], axis=1)
    )
    grad, grad_bf = norm_back(x1, grad, plan.total(parts), gains[1])
    dy, grad_bf0, dstate = out_back(core, plan.spread(grad_bf), lower, 2 * hid, channels, (q0, rise))
    dstate_end = plan.grad_after(factor, dstate)
    dstate_end, output, feed1 = tie(dstate_end, output, feed1)
    dq, dk, dhalo, dv, dtaps, drate = h3_back_call(
        q0, ks, v0, dy, saved, dstate_end, rate_row, seg_col, seg_row, entry, k0, halo, taps, age, rem
    )
    dq, mix1 = tie(dq, mix1)
    parts, cat0, gain0 = project_back(
        core, n, "halo", dq, (dk, dv, plan.to_previous(dhalo)), first, 0, n0, gains[0]
    )
    grad, _ = norm_back(x0, grad, plan.total(parts), gains[0])
    input_grad = plan.leave_grad(grad)

    mix0 = jnp.concatenate([dot_tn(n0, cat0), dot_tn(grad_bf0, y0)], axis=1)
    mix0 = mix0.reshape(slots, share, 4 * channels)
    taps_each = taps_n // slots
    small = jnp.concatenate(
        [
            dtaps.reshape(slots, taps_each, channels),
            jnp.pad(
                drate.reshape(-1, slots, HEAD_DIM // slots).transpose(1, 0, 2).reshape(slots, 1, -1),
                ((0, 0), (0, 0), (0, channels - channels // slots)),
            ),
            jnp.concatenate([gain0, gain1, gain2, gain3]).reshape(4, slots, share).transpose(1, 0, 2),
        ],
        axis=1,
    ).astype(bf16)
    small = jnp.pad(small, ((0, 0), (0, (-small.shape[1]) % 32), (0, 3 * channels)))
    height = share + small.shape[1]
    mix0 = plan.reduce(jnp.concatenate([mix0, small], axis=1).reshape(slots * height, 4 * channels))
    small = mix0[share:, :channels]
    in0_grad, out0_grad = mixer_shares(mix0[:share], channels)
    dtaps = small[:taps_each].astype(f32)
    drate = small[taps_each, : channels // slots].astype(f32).reshape(-1, HEAD_DIM // slots)
    gain_rows = plan.over_places(small[taps_each + 1 : taps_each + 5]).astype(f32)
    up0_grad, down0_grad = feed_shares(feed0)
    up1_grad, down1_grad = feed_shares(feed1)
    in1_grad, out1_grad = mixer_shares(mix1, channels)
    return (
        output[None].astype(bf16),
        input_grad[None],
        gain_rows[:3],
        gain_rows[3],
        jnp.stack([in0_grad, in1_grad]),
        out0_grad,
        out1_grad,
        jnp.stack([up0_grad, up1_grad]),
        jnp.stack([down0_grad, down1_grad]),
        dtaps,
        drate,
    )


def shards(*arguments):
    paired = lax.axis_size("ctx") == 2 and lax.axis_size("tp") == 4 and lax.axis_size("fsdp") == 4
    return run(Pairs() if paired else Rows(), *arguments)


def solution(mesh):
    placed = (
        P("fsdp", "ctx", None),
        P("fsdp", "ctx", None),
        P("fsdp", "ctx"),
        P(),
        P(),
        P(None, None, "fsdp", "tp"),
        P("tp", "fsdp"),
        P("tp", "fsdp"),
        P(None, "fsdp", "tp"),
        P(None, "tp", "fsdp"),
        P(None, "tp"),
        P("tp", None),
    )
    return jax.shard_map(
        shards,
        mesh=mesh,
        in_specs=placed,
        out_specs=(
            P("fsdp", "ctx", None),
            P("fsdp", "ctx", None),
            P(None, "fsdp"),
            P("fsdp"),
            P(None, None, "fsdp", "tp"),
            P("tp", "fsdp"),
            P("tp", "fsdp"),
            P(None, "fsdp", "tp"),
            P(None, "tp", "fsdp"),
            P("fsdp", "tp"),
            P("tp", "fsdp"),
        ),
        check_vma=False,
    )
```

time: 910 us -> 591 us (0.65)
  waiting for transfers between devices: 554 us -> 256 us
  starting transfers between devices: 14.2 us -> 114 us
  matrix products: 75.4 us -> 11.3 us
  blocking collectives: 55.4 us -> 0 us
  Pallas kernels: 70.8 us -> 104 us
  other arithmetic: 59 us -> 38.4 us
  local copies, waits for them, and re-layouts: 55.9 us -> 44.4 us
    psum x8 -> x0, waiting for transfers between devices: 382 us -> none  [the longest x7 382 us: total(): return lax.psum(partial.astype(bf16), 'tp').astype(f32)]
    ppermute x8 -> x66, waiting for transfers between devices: 0.02 us -> 256 us  [the longest x20 85.7 us: send(): return lax.ppermute(value, ('ctx', 'tp'), number)]
    reduce_scatter x5 -> x0, waiting for transfers between devices: 151 us -> none  [reduce(): lax.psum_scatter(value.astype(bf16), 'fsdp', scatter_dimension=dim, tiled...]
    ppermute x8 -> x66, starting transfers between devices: 12.1 us -> 114 us  [the longest x20 40.3 us: send(): return lax.ppermute(value, ('ctx', 'tp'), number)]
    dot_general x37 -> x10, matrix products: 75.4 us -> 11.3 us  [the longest x8 7.24 us: dot_tn(): jnp.einsum('tf,td->fd', a, b, preferred_element_type=f32).astype(bf16)]
    all_gather x4 -> x0, blocking collectives: 43.5 us -> none  [the longest x2 26.8 us: weights(): lax.all_gather(proj_in, 'fsdp', axis=1, tiled=True)]
    pallas_call x5 -> x26, Pallas kernels: 70.8 us -> 104 us  [kernel_call(): pl.pallas_call(kernel, out_shape=[jax.ShapeDtypeStruct(s, d) for s, d in...]
    reduce_sum x15 -> x1, other arithmetic: 25.2 us -> 0.2 us  [first_tiles(): jnp.sum((key_ids[None, :] < firsts[:, None]).astype(jnp.int32), axis=1)]
  transfers between devices with their start and end apart: 30 -> 68, of which waited for: 14 -> 35; matrix products, arithmetic and copies ran while one was open for 12% -> 10% of each run, Pallas kernels for 0% -> 11%
where the time goes in v2:
time: 591 us; the launch traced here: 585 us
  waiting for transfers between devices  256 us (43%)
  starting transfers between devices  114 us (19%)
  Pallas kernels  104 us (18%)
  local copies, waits for them, and re-layouts  44.4 us (8%)
  other arithmetic  38.4 us (6%)
  between operations  16.4 us (3%)
  matrix products  11.3 us (2%)
    pallas_call x26, Pallas kernels, kernel_call(): pl.pallas_call(kernel, out_shape=[jax.ShapeDtypeStruct(s, d) for s, d in...  104 us
    ppermute x20, waiting for transfers between devices, send(): return lax.ppermute(value, ('ctx', 'tp'), number)  85.7 us
    ppermute x9, waiting for transfers between devices, neighbour(): return lax.ppermute(value, 'tp', [(0, 1), (1, 0), (2, 3), (3, 2)])  81.4 us
    ppermute x20, starting transfers between devices, send(): return lax.ppermute(value, ('ctx', 'tp'), number)  40.3 us
    ppermute x12, waiting for transfers between devices, reduce(): lax.ppermute(part, 'fsdp', [(i, i ^ k) for i in range(4)]).astype(f32)  33.8 us
    unnamed x196, local copies, waits for them, and re-layouts  29.6 us
    ppermute x3, waiting for transfers between devices, across(): return lax.ppermute(value, 'tp', [(0, 2), (2, 0), (1, 3), (3, 1)])  27.8 us
    ppermute x19, starting transfers between devices, swap(): return lax.ppermute(value, 'ctx', [(0, 1), (1, 0)])  27 us
  transfers between devices with their start and end apart: 68, of which 35 were waited for; matrix products, arithmetic and copies ran while one was open for 10% of the time, Pallas kernels for 11%

profile of v2, /device:TPU:1, one launch (start us, length us, event | category | flops | bytes accessed | tf_op | source)
XLA Modules:
  0.0 584.6 jit_solution(7282073693208341697)
XLA Ops:
  18.1 7.8 %collective-permute-done.2 = bf16[192,576]{1,0:T(8,128)(2,1)} collective-permute-done((bf16[192,576]{1,0:T(8,128)(2,1)}, bf16[192,576]{1,0:T(8,128)(2,1)}, u32[]{:S(2)}, u32[]{:S(2)}) %collective-permute-start.2) | collective-permute-done | bytes 221216 | tf_op jit(solution)/shard_map/ppermute | solution.py:894
  32.2 13.9 %collective-permute-done.10 = bf16[192,1728]{1,0:T(8,128)(2,1)S(1)} collective-permute-done((bf16[192,1728]{1,0:T(8,128)(2,1)S(1)}, bf16[192,1728]{1,0:T(8,128)(2,1)S(1)}, u32[]{:S(2)}, u32[]{:S(2)}) %collective-permute-start.10) | collective-permute-done | bytes 663584 | tf_op jit(solution)/shard_map/ppermute | solution.py:894
  56.3 17.6 %collective-permute-done.4 = bf16[192,576]{1,0:T(8,128)(2,1)S(1)} collective-permute-done((bf16[192,576]{1,0:T(8,128)(2,1)S(1)}, bf16[192,576]{1,0:T(8,128)(2,1)S(1)}, u32[]{:S(2)}, u32[]{:S(2)}) %collective-permute-start.4) | collective-permute-done | bytes 221216 | tf_op jit(solution)/shard_map/ppermute | solution.py:947
  80.4 8.4 %shard_map.205 = (f32[768,192]{1,0:T(8,128)S(1)}, bf16[64,192]{1,0:T(8,128)(2,1)S(1)}) custom-call(bf16[768,192]{1,0:T(8,128)(2,1)S(1)} %get-tuple-element.98.key_ref, bf16[64,192]{1,0:T(8,128)(2,1)S(1)} %collective-permute-done.6.halo_ref, f32[64,192]{1,0:T(8,128)S(1)} %slice.189.taps_ref, s32[768,192]{1,0:T(8,128)S(1)} %broadcast_in_dim.24.age_ref, ...), custom_call_target="tpu_custom_call" | custom-call | flops 10000000000 | bytes 1000 | tf_op jit(solution)/shard_map/pallas_call | solution.py:62
  89.8 5.3 collective-permute-start.9
  95.1 9.1 %collective-permute-done.17 = bf16[192,2368]{1,0:T(8,128)(2,1)S(1)} collective-permute-done((bf16[192,2368]{1,0:T(8,128)(2,1)S(1)}, bf16[192,2368]{1,0:T(8,128)(2,1)S(1)}, u32[]{:S(2)}, u32[]{:S(2)}) %collective-permute-start.17) | collective-permute-done | bytes 909344 | tf_op jit(solution)/shard_map/ppermute | solution.py:894
  114.3 5.1 collective-permute-start.12
  119.4 13.4 %collective-permute-done.12.refs_1_ = bf16[384,768]{1,0:T(8,128)(2,1)S(1)} collective-permute-done((bf16[384,768]{1,0:T(8,128)(2,1)S(1)}, bf16[384,768]{1,0:T(8,128)(2,1)S(1)}, u32[]{:S(2)}, u32[]{:S(2)}) %collective-permute-start.12) | collective-permute-done | bytes 589856 | tf_op jit(solution)/shard_map/ppermute | solution.py:900
  137.7 4.3 shard_map.209
  145.8 13.1 %collective-permute-done.15.refs_1_ = bf16[384,768]{1,0:T(8,128)(2,1)S(1)} collective-permute-done((bf16[384,768]{1,0:T(8,128)(2,1)S(1)}, bf16[384,768]{1,0:T(8,128)(2,1)S(1)}, u32[]{:S(2)}, u32[]{:S(2)}) %collective-permute-start.15) | collective-permute-done | bytes 589856 | tf_op jit(solution)/shard_map/ppermute | solution.py:900
  169.6 4.8 collective-permute-start.18
  175.6 6.8 %shard_map.212 = (f32[768,192]{1,0:T(8,128)S(1)}, f32[768,128]{1,0:T(8,128)S(1)}) custom-call(s32[3,3]{1,0:T(4,128)S(1)} %pad_add_fusion.3.lim_ref, bf16[768,192]{1,0:T(8,128)(2,1)S(1)} %copy-done.59, bf16[768,192]{1,0:T(8,128)(2,1)S(1)} %get-tuple-element.117.k_ref, bf16[768,192]{1,0:T(8,128)(2,1)S(1)} %get-tuple-element.118.v_ref, ...), custom_call_target="tpu_custom_call" | custom-call | flops 5000000000 | bytes 1000 | tf_op jit(solution)/shard_map/pallas_call | solution.py:62
  182.4 4.4 collective-permute-done.18
  191.6 4.9 collective-permute-start.21
  196.7 14.6 %collective-permute-start.20 = (bf16[384,768]{1,0:T(8,128)(2,1)S(1)}, bf16[384,768]{1,0:T(8,128)(2,1)S(1)}, u32[]{:S(2)}, u32[]{:S(2)}) collective-permute-start(bf16[384,768]{1,0:T(8,128)(2,1)S(1)} %add_convert_fusion.9.refs_0_), channel_id=1, source_target_pairs={{0,1},{1,0},{2,3},{3,2},{4,5},{5,4},{6,7},{7,6},{8,9},{9,8},{10,11... | collective-permute-start | bytes 1769480 | tf_op jit(solution)/shard_map/ppermute | solution.py:900
  212.3 12.3 %collective-permute-done.20.refs_1_ = bf16[384,768]{1,0:T(8,128)(2,1)S(1)} collective-permute-done((bf16[384,768]{1,0:T(8,128)(2,1)S(1)}, bf16[384,768]{1,0:T(8,128)(2,1)S(1)}, u32[]{:S(2)}, u32[]{:S(2)}) %collective-permute-start.20) | collective-permute-done | bytes 589856 | tf_op jit(solution)/shard_map/ppermute | solution.py:900
  229.6 5.3 shard_map.216
  241.8 10.0 %collective-permute-done.25.refs_1_ = bf16[384,768]{1,0:T(8,128)(2,1)S(1)} collective-permute-done((bf16[384,768]{1,0:T(8,128)(2,1)S(1)}, bf16[384,768]{1,0:T(8,128)(2,1)S(1)}, u32[]{:S(2)}, u32[]{:S(2)}) %collective-permute-start.25) | collective-permute-done | bytes 589856 | tf_op jit(solution)/shard_map/ppermute | solution.py:900
  251.8 3.3 shard_map.217
  265.0 4.7 shard_map.219
  271.2 11.1 %shard_map.220 = (bf16[768,192]{1,0:T(8,128)(2,1)}, f32[768,384]{1,0:T(8,128)}) custom-call(s32[3,3]{1,0:T(4,128)} %copy-done.18, bf16[768,192]{1,0:T(8,128)(2,1)} %copy-done.58, bf16[768,192]{1,0:T(8,128)(2,1)} %copy-done.10, bf16[768,192]{1,0:T(8,128)(2,1)} %copy-done.11, bf16[768,192]{1,0:T(8,128)(2,1)} %copy-done.52, f32[768,192]{1,0:T(8,128)} %copy-done.67, ...), custom_call_target="tpu_custom_call" | custom-call | flops 7000000000 | bytes 1000 | tf_op jit(solution)/shard_map/pallas_call | solution.py:62
  282.2 27.2 %collective-permute-done.27.refs_1_ = bf16[768,384]{1,0:T(8,128)(2,1)S(1)} collective-permute-done((bf16[768,384]{1,0:T(8,128)(2,1)}, bf16[768,384]{1,0:T(8,128)(2,1)S(1)}, u32[]{:S(2)}, u32[]{:S(2)}) %collective-permute-start.27) | collective-permute-done | bytes 589856 | tf_op jit(solution)/shard_map/ppermute | solution.py:894
  316.7 2.6 fusion.4
  327.1 13.0 %collective-permute-done.36 = bf16[384,768]{1,0:T(8,128)(2,1)} collective-permute-done((bf16[384,768]{1,0:T(8,128)(2,1)}, bf16[384,768]{1,0:T(8,128)(2,1)}, u32[]{:S(2)}, u32[]{:S(2)}) %collective-permute-start.36) | collective-permute-done | bytes 589856 | tf_op jit(solution)/shard_map/ppermute | solution.py:900
  341.8 2.8 collective-permute-done.42
  345.9 11.8 %collective-permute-done.29.refs_1_ = bf16[384,768]{1,0:T(8,128)(2,1)S(1)} collective-permute-done((bf16[384,768]{1,0:T(8,128)(2,1)S(1)}, bf16[384,768]{1,0:T(8,128)(2,1)S(1)}, u32[]{:S(2)}, u32[]{:S(2)}) %collective-permute-start.29) | collective-permute-done | bytes 589856 | tf_op jit(solution)/shard_map/ppermute | solution.py:900
  357.7 3.3 shard_map.222
  361.1 3.0 collective-permute-start.30
  369.5 3.0 shard_map.223
  379.3 6.2 %collective-permute-done.46 = bf16[192,768]{0,1:T(8,128)(2,1)S(1)} collective-permute-done((bf16[192,768]{0,1:T(8,128)(2,1)S(1)}, bf16[192,768]{0,1:T(8,128)(2,1)S(1)}, u32[]{:S(2)}, u32[]{:S(2)}) %collective-permute-start.46) | collective-permute-done | bytes 294944 | tf_op jit(solution)/shard_map/ppermute | solution.py:1005
  387.3 4.2 collective-permute-start.38
  391.7 6.2 %collective-permute-done.61 = bf16[192,1536]{1,0:T(8,128)(2,1)S(1)} collective-permute-done((bf16[192,1536]{1,0:T(8,128)(2,1)S(1)}, bf16[192,1536]{1,0:T(8,128)(2,1)S(1)}, u32[]{:S(2)}, u32[]{:S(2)}) %collective-permute-start.61) | collective-permute-done | bytes 589856 | tf_op jit(solution)/shard_map/ppermute | solution.py:1005
  401.8 9.1 %collective-permute-done.63 = bf16[192,1536]{1,0:T(8,128)(2,1)S(1)} collective-permute-done((bf16[192,1536]{1,0:T(8,128)(2,1)S(1)}, bf16[192,1536]{1,0:T(8,128)(2,1)S(1)}, u32[]{:S(2)}, u32[]{:S(2)}) %collective-permute-start.63) | collective-permute-done | bytes 589856 | tf_op jit(solution)/shard_map/ppermute | solution.py:1005
  417.7 3.3 shard_map.224
  421.0 3.9 collective-permute-start.33
  431.5 3.3 collective-permute-done.65
  436.2 3.3 collective-permute-done.34.dst_ref
  440.6 24.0 %shard_map.226 = (bf16[768,192]{1,0:T(8,128)(2,1)S(1)}, f32[768,192]{1,0:T(8,128)S(1)}, bf16[64,192]{1,0:T(8,128)(2,1)S(1)}, bf16[768,192]{1,0:T(8,128)(2,1)S(1)...) custom-call(bf16[768,192]{1,0:T(8,128)(2,1)S(1)} %copy-done.50, f32[768,192]{1,0:T(8,128)S(1)} %copy-done.70, ...), custom_call_target="tpu_custom_call" | custom-call | flops 25999998976 | bytes 1000 | tf_op jit(solution)/shard_map/pallas_call | solution.py:62
  467.6 4.0 collective-permute-done.49.refs_2_
  483.0 9.3 %collective-permute-start.56 = (bf16[224,768]{0,1:T(8,128)(2,1)}, bf16[224,768]{0,1:T(8,128)(2,1)}, u32[]{:S(2)}, u32[]{:S(2)}) collective-permute-start(bf16[224,768]{0,1:T(8,128)(2,1)} %copy.165), channel_id=1, source_target_pairs={{0,24},{8,16},{16,8},{24,0},{1,25},{9,17},{17,9},{25,1},{2,26},{10... | collective-permute-start | bytes 1032200 | tf_op jit(solution)/shard_map/ppermute | solution.py:1005
  493.7 4.0 collective-permute-start.50
  498.8 7.8 %collective-permute-done.54 = bf16[224,768]{0,1:T(8,128)(2,1)} collective-permute-done((bf16[224,768]{0,1:T(8,128)(2,1)}, bf16[224,768]{0,1:T(8,128)(2,1)}, u32[]{:S(2)}, u32[]{:S(2)}) %collective-permute-start.54) | collective-permute-done | bytes 344096 | tf_op jit(solution)/shard_map/ppermute | solution.py:1005
  506.6 3.6 collective-permute-done.55
  516.0 3.8 collective-permute-done.57
  523.5 6.2 %collective-permute-done.58 = bf16[224,768]{0,1:T(8,128)(2,1)S(1)} collective-permute-done((bf16[224,768]{0,1:T(8,128)(2,1)S(1)}, bf16[224,768]{0,1:T(8,128)(2,1)S(1)}, u32[]{:S(2)}, u32[]{:S(2)}) %collective-permute-start.58) | collective-permute-done | bytes 344096 | tf_op jit(solution)/shard_map/ppermute | solution.py:894
  529.8 5.4 collective-permute-done.51.refs_1_
  535.1 4.1 shard_map.228
  540.6 26.6 %collective-permute-done.52 = bf16[384,768]{1,0:T(8,128)(2,1)S(1)} collective-permute-done((bf16[384,768]{1,0:T(8,128)(2,1)S(1)}, bf16[384,768]{1,0:T(8,128)(2,1)S(1)}, u32[]{:S(2)}, u32[]{:S(2)}) %collective-permute-start.52) | collective-permute-done | bytes 589856 | tf_op jit(solution)/shard_map/ppermute | solution.py:903
  (443 shorter events, 183.2 us)
Async XLA Ops:
  7.2 102.5 %all-gather.3.cloned.1.call-start = ((), (), s32[]{:S(2)}) async-start(), calls=%async_computation | async-start | bytes 3440640 | tf_op jit(solution)/shard_map/all_gather | solution.py:959
  8.0 22.2 %collective-permute-start.8 = (s32[768]{0:T(1024)S(1)}, s32[768]{0:T(1024)S(1)}, u32[]{:S(2)}, u32[]{:S(2)}) collective-permute-start(s32[768]{0:T(1024)S(1)} %add_reduce_fusion), channel_id=1, source_target_pairs={{0,4},{4,0},{1,5},{5,1},{2,6},{6,2},{3,7},{7,3},{8,12},{12,8},{9,1... | collective-permute-start | bytes 9224 | tf_op jit(solution)/shard_map/ppermute | solution.py:897
  9.8 38.9 %collective-permute-start.7 = (f32[65,192]{1,0:T(8,128)S(1)}, f32[65,192]{1,0:T(8,128)}, u32[]{:S(2)}, u32[]{:S(2)}) collective-permute-start(f32[65,192]{1,0:T(8,128)S(1)} %dynamic-update-slice.1), channel_id=1, source_target_pairs={{0,2},{1,3},{6,4},{7,5},{8,10},{9,11},{14,12},{15,13},{16,18},{17,... | collective-permute-start | bytes 149768 | tf_op jit(solution)/shard_map/ppermute | solution.py:894
  13.7 12.2 %collective-permute-start.2 = (bf16[192,576]{1,0:T(8,128)(2,1)}, bf16[192,576]{1,0:T(8,128)(2,1)}, u32[]{:S(2)}, u32[]{:S(2)}) collective-permute-start(bf16[192,576]{1,0:T(8,128)(2,1)} %pad_maximum_fusion.4), channel_id=1, source_target_pairs={{0,2},{1,3},{6,4},{7,5},{8,10},{9,11},{14,12},{15,13},{16,18},{17,... | collective-permute-start | bytes 663560 | tf_op jit(solution)/shard_map/ppermute | solution.py:894
  15.9 35.0 %collective-permute-start = (bf16[384,768]{1,0:T(8,128)(2,1)}, bf16[384,768]{1,0:T(8,128)(2,1)}, u32[]{:S(2)}, u32[]{:S(2)}) collective-permute-start(bf16[384,768]{1,0:T(8,128)(2,1)} %dynamic-slice_bitcast_fusion.1), channel_id=1, source_target_pairs={{0,4},{1,5},{6,2},{7,3},{8,12},{9,13},{14,10},{15,11},{16,20},{17,... | collective-permute-start | bytes 1769480 | tf_op jit(solution)/shard_map/ppermute | solution.py:894
  27.0 19.1 %collective-permute-start.10 = (bf16[192,1728]{1,0:T(8,128)(2,1)S(1)}, bf16[192,1728]{1,0:T(8,128)(2,1)S(1)}, u32[]{:S(2)}, u32[]{:S(2)}) collective-permute-start(bf16[192,1728]{1,0:T(8,128)(2,1)S(1)} %pad_maximum_fusion.2), channel_id=1, source_target_pairs={{0,2},{1,3},{6,4},{7,5},{8,10},{9,11},{14,12},{15,13},{16,18},{17,... | collective-permute-start | bytes 1990664 | tf_op jit(solution)/shard_map/ppermute | solution.py:894
  47.0 116.9 %all-gather.5.cloned.1.call-start = ((), (), s32[]{:S(2)}) async-start(), calls=%async_computation.1 | async-start | bytes 4669440 | tf_op jit(solution)/shard_map/all_gather | solution.py:959
  54.6 19.5 %collective-permute-start.1 = (bf16[384,768]{1,0:T(8,128)(2,1)S(1)}, bf16[384,768]{1,0:T(8,128)(2,1)S(1)}, u32[]{:S(2)}, u32[]{:S(2)}) collective-permute-start(bf16[384,768]{1,0:T(8,128)(2,1)S(1)} %get-tuple-element.95.refs_0_), channel_id=1, source_target_pairs={{0,4},{4,0},{1,5},{5,1},{2,6},{6,2},{3,7},{7,3},{8,12},{12,8},{9,1... | collective-permute-start | bytes 1769480 | tf_op jit(solution)/shard_map/ppermute | solution.py:897
  54.7 19.3 %collective-permute-start.5 = (bf16[192,576]{1,0:T(8,128)(2,1)S(1)}, bf16[192,576]{1,0:T(8,128)(2,1)S(1)}, u32[]{:S(2)}, u32[]{:S(2)}) collective-permute-start(bf16[192,576]{1,0:T(8,128)(2,1)S(1)} %broadcast_select_fusion.12), channel_id=1, source_target_pairs={{0,24},{8,16},{16,8},{24,0},{1,25},{9,17},{17,9},{25,1},{2,26},{10... | collective-permute-start | bytes 663560 | tf_op jit(solution)/shard_map/ppermute | solution.py:947
  55.9 18.0 %collective-permute-start.4 = (bf16[192,576]{1,0:T(8,128)(2,1)S(1)}, bf16[192,576]{1,0:T(8,128)(2,1)S(1)}, u32[]{:S(2)}, u32[]{:S(2)}) collective-permute-start(bf16[192,576]{1,0:T(8,128)(2,1)S(1)} %broadcast_select_fusion.12), channel_id=1, source_target_pairs={{0,16},{8,24},{16,0},{24,8},{1,17},{9,25},{17,1},{25,9},{2,18},{10... | collective-permute-start | bytes 663560 | tf_op jit(solution)/shard_map/ppermute | solution.py:947
  78.9 25.2 %collective-permute-start.17 = (bf16[192,2368]{1,0:T(8,128)(2,1)S(1)}, bf16[192,2368]{1,0:T(8,128)(2,1)S(1)}, u32[]{:S(2)}, u32[]{:S(2)}) collective-permute-start(bf16[192,2368]{1,0:T(8,128)(2,1)S(1)} %concatenate.77), channel_id=1, source_target_pairs={{0,2},{1,3},{6,4},{7,5},{8,10},{9,11},{14,12},{15,13},{16,18},{17,... | collective-permute-start | bytes 2727944 | tf_op jit(solution)/shard_map/ppermute | solution.py:894
  89.8 15.4 %collective-permute-start.9 = (bf16[64,192]{1,0:T(8,128)(2,1)S(1)}, bf16[64,192]{1,0:T(8,128)(2,1)S(1)}, u32[]{:S(2)}, u32[]{:S(2)}) collective-permute-start(bf16[64,192]{1,0:T(8,128)(2,1)S(1)} %get-tuple-element.101), channel_id=1, source_target_pairs={{0,2},{1,3},{4,6},{5,7},{8,10},{9,11},{12,14},{13,15},{16,18},{17,... | collective-permute-start | bytes 73736 | tf_op jit(solution)/shard_map/ppermute | solution.py:894
  114.3 18.5 %collective-permute-start.12 = (bf16[384,768]{1,0:T(8,128)(2,1)S(1)}, bf16[384,768]{1,0:T(8,128)(2,1)S(1)}, u32[]{:S(2)}, u32[]{:S(2)}) collective-permute-start(bf16[384,768]{1,0:T(8,128)(2,1)S(1)} %add_convert_fusion.11.refs_0_), channel_id=1, source_target_pairs={{0,1},{1,0},{2,3},{3,2},{4,5},{5,4},{6,7},{7,6},{8,9},{9,8},{10,11... | collective-permute-start | bytes 1769480 | tf_op jit(solution)/shard_map/ppermute | solution.py:900
  144.3 14.6 %collective-permute-start.15 = (bf16[384,768]{1,0:T(8,128)(2,1)S(1)}, bf16[384,768]{1,0:T(8,128)(2,1)S(1)}, u32[]{:S(2)}, u32[]{:S(2)}) collective-permute-start(bf16[384,768]{1,0:T(8,128)(2,1)S(1)} %add_convert_fusion.10.refs_0_), channel_id=1, source_target_pairs={{0,1},{1,0},{2,3},{3,2},{4,5},{5,4},{6,7},{7,6},{8,9},{9,8},{10,11... | collective-permute-start | bytes 1769480 | tf_op jit(solution)/shard_map/ppermute | solution.py:900
  169.6 17.1 %collective-permute-start.18 = (bf16[768,384]{1,0:T(8,128)(2,1)S(1)}, bf16[768,384]{1,0:T(8,128)(2,1)S(1)}, u32[]{:S(2)}, u32[]{:S(2)}) collective-permute-start(bf16[768,384]{1,0:T(8,128)(2,1)S(1)} %pad_maximum_fusion.3), channel_id=1, source_target_pairs={{0,2},{1,3},{4,6},{5,7},{8,10},{9,11},{12,14},{13,15},{16,18},{17,... | collective-permute-start | bytes 1769480 | tf_op jit(solution)/shard_map/ppermute | solution.py:894
  191.6 19.7 %collective-permute-start.21 = (bf16[384,768]{1,0:T(8,128)(2,1)S(1)}, bf16[384,768]{1,0:T(8,128)(2,1)S(1)}, u32[]{:S(2)}, u32[]{:S(2)}) collective-permute-start(bf16[384,768]{1,0:T(8,128)(2,1)S(1)} %dynamic-slice_bitcast_fusion), channel_id=1, source_target_pairs={{0,4},{1,5},{6,2},{7,3},{8,12},{9,13},{14,10},{15,11},{16,20},{17,... | collective-permute-start | bytes 1769480 | tf_op jit(solution)/shard_map/ppermute | solution.py:894
  196.7 27.8 %collective-permute-start.20 = (bf16[384,768]{1,0:T(8,128)(2,1)S(1)}, bf16[384,768]{1,0:T(8,128)(2,1)S(1)}, u32[]{:S(2)}, u32[]{:S(2)}) collective-permute-start(bf16[384,768]{1,0:T(8,128)(2,1)S(1)} %add_convert_fusion.9.refs_0_), channel_id=1, source_target_pairs={{0,1},{1,0},{2,3},{3,2},{4,5},{5,4},{6,7},{7,6},{8,9},{9,8},{10,11... | collective-permute-start | bytes 1769480 | tf_op jit(solution)/shard_map/ppermute | solution.py:900
  211.5 16.5 %collective-permute-start.23 = (bf16[384,768]{1,0:T(8,128)(2,1)S(1)}, bf16[384,768]{1,0:T(8,128)(2,1)S(1)}, u32[]{:S(2)}, u32[]{:S(2)}) collective-permute-start(bf16[384,768]{1,0:T(8,128)(2,1)S(1)} %bitcast_select_fusion.refs_2_.grad_ref), channel_id=1, source_target_pairs={{0,4},{4,0},{1,5},{5,1},{2,6},{6,2},{3,7},{7,3},{8,12},{12,8},{9,1... | collective-permute-start | bytes 1769480 | tf_op jit(solution)/shard_map/ppermute | solution.py:897
  237.2 14.6 %collective-permute-start.25 = (bf16[384,768]{1,0:T(8,128)(2,1)S(1)}, bf16[384,768]{1,0:T(8,128)(2,1)S(1)}, u32[]{:S(2)}, u32[]{:S(2)}) collective-permute-start(bf16[384,768]{1,0:T(8,128)(2,1)S(1)} %add_convert_fusion.8.refs_0_), channel_id=1, source_target_pairs={{0,1},{1,0},{2,3},{3,2},{4,5},{5,4},{6,7},{7,6},{8,9},{9,8},{10,11... | collective-permute-start | bytes 1769480 | tf_op jit(solution)/shard_map/ppermute | solution.py:900
  241.1 75.6 %collective-permute-start.35 = (bf16[384,768]{1,0:T(8,128)(2,1)}, bf16[384,768]{1,0:T(8,128)(2,1)}, u32[]{:S(2)}, u32[]{:S(2)}) collective-permute-start(bf16[384,768]{1,0:T(8,128)(2,1)} %convolution_convert_fusion.6), channel_id=1, source_target_pairs={{0,4},{4,0},{1,5},{5,1},{2,6},{6,2},{3,7},{7,3},{8,12},{12,8},{9,1... | collective-permute-start | bytes 1769480 | tf_op jit(solution)/shard_map/ppermute | solution.py:897
  260.3 59.0 %collective-permute-start.39 = (bf16[192,1536]{1,0:T(8,128)(2,1)}, bf16[192,1536]{1,0:T(8,128)(2,1)}, u32[]{:S(2)}, u32[]{:S(2)}) collective-permute-start(bf16[192,1536]{1,0:T(8,128)(2,1)} %get-tuple-element.239), channel_id=1, source_target_pairs={{0,8},{8,0},{16,24},{24,16},{1,9},{9,1},{17,25},{25,17},{2,10},{10... | collective-permute-start | bytes 1769480 | tf_op jit(solution)/shard_map/ppermute | solution.py:1005
  260.6 58.6 %collective-permute-start.40 = (bf16[192,1536]{1,0:T(8,128)(2,1)}, bf16[192,1536]{1,0:T(8,128)(2,1)}, u32[]{:S(2)}, u32[]{:S(2)}) collective-permute-start(bf16[192,1536]{1,0:T(8,128)(2,1)} %get-tuple-element.240), channel_id=1, source_target_pairs={{0,16},{8,24},{16,0},{24,8},{1,17},{9,25},{17,1},{25,9},{2,18},{10... | collective-permute-start | bytes 1769480 | tf_op jit(solution)/shard_map/ppermute | solution.py:1005
  261.8 57.4 %collective-permute-start.41 = (bf16[192,1536]{1,0:T(8,128)(2,1)}, bf16[192,1536]{1,0:T(8,128)(2,1)}, u32[]{:S(2)}, u32[]{:S(2)}) collective-permute-start(bf16[192,1536]{1,0:T(8,128)(2,1)} %get-tuple-element.241), channel_id=1, source_target_pairs={{0,24},{8,16},{16,8},{24,0},{1,25},{9,17},{17,9},{25,1},{2,26},{10... | collective-permute-start | bytes 1769480 | tf_op jit(solution)/shard_map/ppermute | solution.py:1005
  269.7 39.7 %collective-permute-start.27 = (bf16[768,384]{1,0:T(8,128)(2,1)}, bf16[768,384]{1,0:T(8,128)(2,1)S(1)}, u32[]{:S(2)}, u32[]{:S(2)}) collective-permute-start(bf16[768,384]{1,0:T(8,128)(2,1)} %get-tuple-element.136), channel_id=1, source_target_pairs={{2,0},{3,1},{6,4},{7,5},{10,8},{11,9},{14,12},{15,13},{18,16},{19,... | collective-permute-start | bytes 1769480 | tf_op jit(solution)/shard_map/ppermute | solution.py:894
  319.2 20.9 %collective-permute-start.36 = (bf16[384,768]{1,0:T(8,128)(2,1)}, bf16[384,768]{1,0:T(8,128)(2,1)}, u32[]{:S(2)}, u32[]{:S(2)}) collective-permute-start(bf16[384,768]{1,0:T(8,128)(2,1)} %fusion.4), channel_id=1, source_target_pairs={{0,1},{1,0},{2,3},{3,2},{4,5},{5,4},{6,7},{7,6},{8,9},{9,8},{10,11... | collective-permute-start | bytes 1769480 | tf_op jit(solution)/shard_map/ppermute | solution.py:900
  321.8 22.7 %collective-permute-start.42 = (bf16[192,1536]{1,0:T(8,128)(2,1)}, bf16[192,1536]{1,0:T(8,128)(2,1)}, u32[]{:S(2)}, u32[]{:S(2)}) collective-permute-start(bf16[192,1536]{1,0:T(8,128)(2,1)} %add_convert_fusion.4), channel_id=1, source_target_pairs={{2,0},{3,1},{4,6},{5,7},{10,8},{11,9},{12,14},{13,15},{18,16},{19,... | collective-permute-start | bytes 1769480 | tf_op jit(solution)/shard_map/ppermute | solution.py:894
  325.6 32.2 %collective-permute-start.29 = (bf16[384,768]{1,0:T(8,128)(2,1)S(1)}, bf16[384,768]{1,0:T(8,128)(2,1)S(1)}, u32[]{:S(2)}, u32[]{:S(2)}) collective-permute-start(bf16[384,768]{1,0:T(8,128)(2,1)S(1)} %add_convert_fusion.7.refs_0_), channel_id=1, source_target_pairs={{0,1},{1,0},{2,3},{3,2},{4,5},{5,4},{6,7},{7,6},{8,9},{9,8},{10,11... | collective-permute-start | bytes 1769480 | tf_op jit(solution)/shard_map/ppermute | solution.py:900
  341.7 34.9 %collective-permute-start.37 = (bf16[384,768]{1,0:T(8,128)(2,1)S(1)}, bf16[384,768]{1,0:T(8,128)(2,1)S(1)}, u32[]{:S(2)}, u32[]{:S(2)}) collective-permute-start(bf16[384,768]{1,0:T(8,128)(2,1)S(1)} %add_convert_fusion.5), channel_id=1, source_target_pairs={{0,2},{2,0},{1,3},{3,1},{4,6},{6,4},{5,7},{7,5},{8,10},{10,8},{9,1... | collective-permute-start | bytes 1769480 | tf_op jit(solution)/shard_map/ppermute | solution.py:903
  366.7 10.0 %collective-permute-start.44 = (bf16[192,768]{0,1:T(8,128)(2,1)S(1)}, bf16[192,768]{0,1:T(8,128)(2,1)S(1)}, u32[]{:S(2)}, u32[]{:S(2)}) collective-permute-start(bf16[192,768]{0,1:T(8,128)(2,1)S(1)} %get-tuple-element.250), channel_id=1, source_target_pairs={{0,8},{8,0},{16,24},{24,16},{1,9},{9,1},{17,25},{25,17},{2,10},{10... | collective-permute-start | bytes 884744 | tf_op jit(solution)/shard_map/ppermute | solution.py:1005
  366.8 10.6 %collective-permute-start.45 = (bf16[192,768]{0,1:T(8,128)(2,1)S(1)}, bf16[192,768]{0,1:T(8,128)(2,1)S(1)}, u32[]{:S(2)}, u32[]{:S(2)}) collective-permute-start(bf16[192,768]{0,1:T(8,128)(2,1)S(1)} %get-tuple-element.251), channel_id=1, source_target_pairs={{0,16},{8,24},{16,0},{24,8},{1,17},{9,25},{17,1},{25,9},{2,18},{10... | collective-permute-start | bytes 884744 | tf_op jit(solution)/shard_map/ppermute | solution.py:1005
  367.5 18.1 %collective-permute-start.46 = (bf16[192,768]{0,1:T(8,128)(2,1)S(1)}, bf16[192,768]{0,1:T(8,128)(2,1)S(1)}, u32[]{:S(2)}, u32[]{:S(2)}) collective-permute-start(bf16[192,768]{0,1:T(8,128)(2,1)S(1)} %get-tuple-element.252), channel_id=1, source_target_pairs={{0,24},{8,16},{16,8},{24,0},{1,25},{9,17},{17,9},{25,1},{2,26},{10... | collective-permute-start | bytes 884744 | tf_op jit(solution)/shard_map/ppermute | solution.py:1005
  372.5 14.8 %collective-permute-start.31 = (bf16[384,768]{1,0:T(8,128)(2,1)S(1)}, bf16[384,768]{1,0:T(8,128)(2,1)S(1)}, u32[]{:S(2)}, u32[]{:S(2)}) collective-permute-start(bf16[384,768]{1,0:T(8,128)(2,1)S(1)} %get-tuple-element.144), channel_id=1, source_target_pairs={{0,4},{4,0},{1,5},{5,1},{2,6},{6,2},{3,7},{7,3},{8,12},{12,8},{9,1... | collective-permute-start | bytes 1769480 | tf_op jit(solution)/shard_map/ppermute | solution.py:897
  376.6 21.3 %collective-permute-start.61 = (bf16[192,1536]{1,0:T(8,128)(2,1)S(1)}, bf16[192,1536]{1,0:T(8,128)(2,1)S(1)}, u32[]{:S(2)}, u32[]{:S(2)}) collective-permute-start(bf16[192,1536]{1,0:T(8,128)(2,1)S(1)} %get-tuple-element.236), channel_id=1, source_target_pairs={{0,8},{8,0},{16,24},{24,16},{1,9},{9,1},{17,25},{25,17},{2,10},{10... | collective-permute-start | bytes 1769480 | tf_op jit(solution)/shard_map/ppermute | solution.py:1005
  376.7 23.5 %collective-permute-start.62 = (bf16[192,1536]{1,0:T(8,128)(2,1)S(1)}, bf16[192,1536]{1,0:T(8,128)(2,1)S(1)}, u32[]{:S(2)}, u32[]{:S(2)}) collective-permute-start(bf16[192,1536]{1,0:T(8,128)(2,1)S(1)} %get-tuple-element.237), channel_id=1, source_target_pairs={{0,16},{8,24},{16,0},{24,8},{1,17},{9,25},{17,1},{25,9},{2,18},{10... | collective-permute-start | bytes 1769480 | tf_op jit(solution)/shard_map/ppermute | solution.py:1005
  377.4 33.5 %collective-permute-start.63 = (bf16[192,1536]{1,0:T(8,128)(2,1)S(1)}, bf16[192,1536]{1,0:T(8,128)(2,1)S(1)}, u32[]{:S(2)}, u32[]{:S(2)}) collective-permute-start(bf16[192,1536]{1,0:T(8,128)(2,1)S(1)} %get-tuple-element.238), channel_id=1, source_target_pairs={{0,24},{8,16},{16,8},{24,0},{1,25},{9,17},{17,9},{25,1},{2,26},{10... | collective-permute-start | bytes 1769480 | tf_op jit(solution)/shard_map/ppermute | solution.py:1005
  385.6 27.4 %collective-permute-start.43 = (bf16[192,1536]{1,0:T(8,128)(2,1)S(1)}, bf16[192,1536]{1,0:T(8,128)(2,1)S(1)}, u32[]{:S(2)}, u32[]{:S(2)}) collective-permute-start(bf16[192,1536]{1,0:T(8,128)(2,1)S(1)} %add_convert_fusion.3), channel_id=1, source_target_pairs={{0,4},{1,5},{6,2},{7,3},{8,12},{9,13},{14,10},{15,11},{16,20},{17,... | collective-permute-start | bytes 1769480 | tf_op jit(solution)/shard_map/ppermute | solution.py:894
  387.3 39.0 %collective-permute-start.38 = (bf16[384,768]{1,0:T(8,128)(2,1)S(1)}, bf16[384,768]{1,0:T(8,128)(2,1)S(1)}, u32[]{:S(2)}, u32[]{:S(2)}) collective-permute-start(bf16[384,768]{1,0:T(8,128)(2,1)S(1)} %broadcast_select_fusion.8), channel_id=1, source_target_pairs={{0,4},{4,0},{1,5},{5,1},{2,6},{6,2},{3,7},{7,3},{8,12},{12,8},{9,1... | collective-permute-start | bytes 1769480 | tf_op jit(solution)/shard_map/ppermute | solution.py:897
  397.9 16.0 %collective-permute-start.47 = (bf16[192,768]{0,1:T(8,128)(2,1)S(1)}, bf16[192,768]{0,1:T(8,128)(2,1)S(1)}, u32[]{:S(2)}, u32[]{:S(2)}) collective-permute-start(bf16[192,768]{0,1:T(8,128)(2,1)S(1)} %add_convert_fusion.15), channel_id=1, source_target_pairs={{2,0},{3,1},{4,6},{5,7},{10,8},{11,9},{12,14},{13,15},{18,16},{19,... | collective-permute-start | bytes 884744 | tf_op jit(solution)/shard_map/ppermute | solution.py:894
  400.3 17.5 %collective-permute-start.32 = (bf16[384,768]{1,0:T(8,128)(2,1)S(1)}, bf16[384,768]{1,0:T(8,128)(2,1)S(1)}, u32[]{:S(2)}, u32[]{:S(2)}) collective-permute-start(bf16[384,768]{1,0:T(8,128)(2,1)S(1)} %add_convert_fusion.6.refs_0_), channel_id=1, source_target_pairs={{0,1},{1,0},{2,3},{3,2},{4,5},{5,4},{6,7},{7,6},{8,9},{9,8},{10,11... | collective-permute-start | bytes 1769480 | tf_op jit(solution)/shard_map/ppermute | solution.py:900
  411.2 13.7 %collective-permute-start.64 = (bf16[192,1536]{1,0:T(8,128)(2,1)S(1)}, bf16[192,1536]{1,0:T(8,128)(2,1)S(1)}, u32[]{:S(2)}, u32[]{:S(2)}) collective-permute-start(bf16[192,1536]{1,0:T(8,128)(2,1)S(1)} %add_convert_fusion.1), channel_id=1, source_target_pairs={{2,0},{3,1},{4,6},{5,7},{10,8},{11,9},{12,14},{13,15},{18,16},{19,... | collective-permute-start | bytes 1769480 | tf_op jit(solution)/shard_map/ppermute | solution.py:894
  414.0 13.6 %collective-permute-start.48 = (bf16[192,768]{0,1:T(8,128)(2,1)S(1)}, bf16[192,768]{0,1:T(8,128)(2,1)S(1)}, u32[]{:S(2)}, u32[]{:S(2)}) collective-permute-start(bf16[192,768]{0,1:T(8,128)(2,1)S(1)} %add_convert_fusion.14), channel_id=1, source_target_pairs={{0,4},{1,5},{6,2},{7,3},{8,12},{9,13},{14,10},{15,11},{16,20},{17,... | collective-permute-start | bytes 884744 | tf_op jit(solution)/shard_map/ppermute | solution.py:894
  483.0 15.8 %collective-permute-start.56 = (bf16[224,768]{0,1:T(8,128)(2,1)}, bf16[224,768]{0,1:T(8,128)(2,1)}, u32[]{:S(2)}, u32[]{:S(2)}) collective-permute-start(bf16[224,768]{0,1:T(8,128)(2,1)} %copy.165), channel_id=1, source_target_pairs={{0,24},{8,16},{16,8},{24,0},{1,25},{9,17},{17,9},{25,1},{2,26},{10... | collective-permute-start | bytes 1032200 | tf_op jit(solution)/shard_map/ppermute | solution.py:1005
  492.3 14.2 %collective-permute-start.54 = (bf16[224,768]{0,1:T(8,128)(2,1)}, bf16[224,768]{0,1:T(8,128)(2,1)}, u32[]{:S(2)}, u32[]{:S(2)}) collective-permute-start(bf16[224,768]{0,1:T(8,128)(2,1)} %copy.163), channel_id=1, source_target_pairs={{0,8},{8,0},{16,24},{24,16},{1,9},{9,1},{17,25},{25,17},{2,10},{10... | collective-permute-start | bytes 1032200 | tf_op jit(solution)/shard_map/ppermute | solution.py:1005
  492.3 17.9 %collective-permute-start.55 = (bf16[224,768]{0,1:T(8,128)(2,1)}, bf16[224,768]{0,1:T(8,128)(2,1)}, u32[]{:S(2)}, u32[]{:S(2)}) collective-permute-start(bf16[224,768]{0,1:T(8,128)(2,1)} %copy.164), channel_id=1, source_target_pairs={{0,16},{8,24},{16,0},{24,8},{1,17},{9,25},{17,1},{25,9},{2,18},{10... | collective-permute-start | bytes 1032200 | tf_op jit(solution)/shard_map/ppermute | solution.py:1005
  493.7 21.0 %collective-permute-start.50 = (bf16[384,768]{1,0:T(8,128)(2,1)S(1)}, bf16[384,768]{1,0:T(8,128)(2,1)}, u32[]{:S(2)}, u32[]{:S(2)}) collective-permute-start(bf16[384,768]{1,0:T(8,128)(2,1)S(1)} %get-tuple-element.163), channel_id=1, source_target_pairs={{0,4},{4,0},{1,5},{5,1},{2,6},{6,2},{3,7},{7,3},{8,12},{12,8},{9,1... | collective-permute-start | bytes 1769480 | tf_op jit(solution)/shard_map/ppermute | solution.py:897
  515.9 19.2 %collective-permute-start.51 = (bf16[384,768]{1,0:T(8,128)(2,1)S(1)}, bf16[384,768]{1,0:T(8,128)(2,1)S(1)}, u32[]{:S(2)}, u32[]{:S(2)}) collective-permute-start(bf16[384,768]{1,0:T(8,128)(2,1)S(1)} %add_convert_fusion.2.refs_0_), channel_id=1, source_target_pairs={{0,1},{1,0},{2,3},{3,2},{4,5},{5,4},{6,7},{7,6},{8,9},{9,8},{10,11... | collective-permute-start | bytes 1769480 | tf_op jit(solution)/shard_map/ppermute | solution.py:900
  539.3 27.8 %collective-permute-start.52 = (bf16[384,768]{1,0:T(8,128)(2,1)S(1)}, bf16[384,768]{1,0:T(8,128)(2,1)S(1)}, u32[]{:S(2)}, u32[]{:S(2)}) collective-permute-start(bf16[384,768]{1,0:T(8,128)(2,1)S(1)} %convert_element_type.347), channel_id=1, source_target_pairs={{0,2},{2,0},{1,3},{3,1},{4,6},{6,4},{5,7},{7,5},{8,10},{10,8},{9,1... | collective-permute-start | bytes 1769480 | tf_op jit(solution)/shard_map/ppermute | solution.py:903
  540.2 28.4 %collective-permute-start.59 = (bf16[4,192]{0,1:T(8,128)(2,1)S(1)}, bf16[4,192]{0,1:T(8,128)(2,1)S(1)}, u32[]{:S(2)}, u32[]{:S(2)}) collective-permute-start(bf16[4,192]{0,1:T(8,128)(2,1)S(1)} %slice.194), channel_id=1, source_target_pairs={{0,1},{1,0},{2,3},{3,2},{4,5},{5,4},{6,7},{7,6},{8,9},{9,8},{10,11... | collective-permute-start | bytes 4616 | tf_op jit(solution)/shard_map/ppermute | solution.py:900
  (113 other events, 869.6 us)
Sparse Core Ops, SparseCore 0:
  47.1 52.9 all-gather.2
  105.3 49.9 all-gather.4
